TPU v7x, 32 devices: a whole 2x2x4 slice. The times are simulated.
32 devices in a mesh: rep: 2 (over x), ep: 8 (over z, y), sub: 2 (over core).
Axes of the slice: x: 2, y: 2, z: 4, core: 2. Of those that a mesh axis runs over, the one named last changes fastest.
Arguments:
- queries: bfloat16 [512, 36864], P(('rep', 'ep', 'sub')), parts along dimension 0, may hold values from -8 to 8
- page_pool: bfloat16 [1024, 36864], P(('rep', 'ep', 'sub')), parts along dimension 0, may hold values from -8 to 8
- page_table: int32 [128, 16], P('rep'), parts along dimension 0, may hold values from 0 to 511, as said below
- serving: int32 [128], P('rep'), parts along dimension 0, may hold values from 0 to 63, as said below
- context_len: int32 [128], P('rep'), parts along dimension 0, may hold values from 256 to 1024
- residual: bfloat16 [512, 3584], P(('rep', 'ep', 'sub')), parts along dimension 0, may hold values from -6 to 6
- routes: int32 [512, 2], P(('rep', 'ep', 'sub')), parts along dimension 0, may hold values from 0 to 3, all different within a row; in each aligned block of 16 rows (0 to 15, 16 to 31, ...) at most 10 rows name the same one
- route_scores: float32 [512, 2], P(('rep', 'ep', 'sub')), parts along dimension 0, may hold values from 0.1 to 1
- w_gate: bfloat16 [8, 3584, 512], P('ep', None, 'sub'), may hold values from -0.09375 to 0.09375
- w_up: bfloat16 [8, 3584, 512], P('ep', None, 'sub'), may hold values from -0.09375 to 0.09375
- w_down: bfloat16 [8, 512, 3584], P('ep', 'sub'), may hold values from -0.1875 to 0.1875
Outputs:
- latent_out: bfloat16 [512, 32768], P(('rep', 'ep', 'sub')), parts along dimension 0
- moe_out: bfloat16 [512, 3584], P(('rep', 'ep', 'sub')), parts along dimension 0
There are 2 independent parts, one for each index of `rep`. A program takes and returns all parts, laid end to end along the dimension named above; an argument that names none is the same for every part. Nothing has to cross between parts.
Inputs may be any that keep to these rules, and one draw needn't show every extreme that they name: Every request stands in exactly one serving slot. `page_table`: for each run of 4 serving slots starting at a multiple of 4, the pages listed for their requests come exactly 4 from each of the 16 blocks of 32 pages of page_pool. `routes`: within each aligned block of 16 rows no expert is named by more than 10 rows.
All inputs are finite; a program needn't handle non-finite values.
Results may differ from a plain program's by a relative error of at most 0.0054.
Values may be sent and summed in bfloat16 or wider, within the bound.
No kernel may reach another device: no remote copies, remote signals or barrier semaphores. Data moves between devices by JAX's collectives and lax.ppermute only.
A program may use at most 128 MiB of HBM per device.

v0:
```python
import jax
import jax.numpy as jnp
from jax import lax
from jax.sharding import PartitionSpec as P

HEADS = 64
LAT = 576
KV = 512
DRAFT = 4


score_scale = 192.0 ** (-0.5)
masked_score = -1e30


def expert_rows(rows, gate_slice, up_slice, down_slice):
    gate = jnp.dot(rows, gate_slice, preferred_element_type=jnp.float32)
    upward = jnp.dot(rows, up_slice, preferred_element_type=jnp.float32)
    hidden = (jax.nn.silu(gate) * upward).astype(jnp.bfloat16)
    return jnp.dot(hidden, down_slice, preferred_element_type=jnp.float32)


def local(
    queries,
    page_pool,
    page_table,
    serving,
    context_len,
    residual,
    routes,
    route_scores,
    w_gate,
    w_up,
    w_down,
):
    peers = lax.axis_size(("ep", "sub"))
    device = lax.axis_index(("ep", "sub"))
    rows_dev = residual.shape[0]
    requests_dev = rows_dev // DRAFT
    pages_each = page_table.shape[1]
    pool_pages = page_pool.shape[0]
    listed = requests_dev * pages_each
    fetched = listed // peers
    page_rows = page_pool.shape[1] // LAT
    listing = page_table[serving].reshape(peers, listed)
    owners = listing // pool_pages
    position = jnp.arange(listed, dtype=jnp.int32)
    ranking = jnp.where(owners == device, 0, listed) + position[None, :]
    wanted = jnp.argsort(ranking, axis=1)[:, :fetched]
    resident = jnp.take_along_axis(listing, wanted, axis=1) - device * pool_pages
    outgoing = page_pool[resident.reshape(-1)].reshape(peers, fetched, page_pool.shape[1])
    arrived = lax.all_to_all(outgoing, ("ep", "sub"), split_axis=0, concat_axis=0, tiled=True)
    n_ep = lax.axis_size("ep")
    n_sub = lax.axis_size("sub")
    experts = n_ep // 2
    top = routes.shape[1]
    capacity = rows_dev * top * 5 // (4 * experts)
    chosen = routes.reshape(-1)
    member = (chosen[:, None] == jnp.arange(experts, dtype=jnp.int32)[None, :]).astype(jnp.int32)
    before = jnp.cumsum(member, axis=0) - member
    rank = jnp.sum(before * member, axis=1)
    slot = (chosen * capacity + rank).reshape(rows_dev, top)
    hits = slot[:, :, None] == jnp.arange(experts * capacity, dtype=jnp.int32)[None, None, :]
    selector = jnp.any(hits, axis=1).astype(jnp.bfloat16)
    packed = jnp.einsum("rs,rd->sd", selector, residual, preferred_element_type=jnp.float32).astype(
        jnp.bfloat16
    )
    width = residual.shape[1]
    gate_slice = w_gate[0]
    up_slice = w_up[0]
    down_slice = w_down[0]
    sending = jnp.broadcast_to(
        packed.reshape(experts, 1, 1, capacity, width), (experts, 2, n_sub, capacity, width)
    )
    sending = sending.reshape(experts * 2 * n_sub, capacity, width)
    block = lax.all_to_all(sending, ("ep", "sub"), split_axis=0, concat_axis=0, tiled=True)
    partial_value = expert_rows(block.reshape(-1, width), gate_slice, up_slice, down_slice).reshape(
        block.shape
    )
    halves = lax.psum_scatter(
        partial_value.reshape(n_ep, n_sub, capacity, width), "sub", scatter_dimension=1, tiled=True
    )
    returned = lax.all_to_all(
        halves.reshape(n_ep, capacity, width).astype(jnp.bfloat16),
        "ep",
        split_axis=0,
        concat_axis=0,
        tiled=True,
    )
    own_list = lax.dynamic_index_in_dim(listing, device, 0, keepdims=False)
    arrival = jnp.argsort(own_list // pool_pages * listed + position)
    placing = jnp.argsort(arrival)
    context = arrived.reshape(listed, -1)[placing].reshape(
        requests_dev, pages_each * page_rows, LAT
    )
    served = lax.dynamic_slice_in_dim(serving, device * requests_dev, requests_dev)
    limits = context_len[served][:, None] - DRAFT + jnp.arange(DRAFT, dtype=jnp.int32)[None, :]
    grouped = queries.reshape(requests_dev, DRAFT, HEADS, LAT)
    scores = (
        jnp.einsum("rthc,rkc->rthk", grouped, context, preferred_element_type=jnp.float32)
        * score_scale
    )
    positions = jnp.arange(context.shape[1], dtype=jnp.int32)
    visible = positions[None, None, :] <= limits[:, :, None]
    scores = jnp.where(visible[:, :, None, :], scores, masked_score)
    highest = jnp.max(scores, axis=-1, keepdims=True)
    exponent = jnp.exp(scores - highest)
    shares = (exponent / jnp.sum(exponent, axis=-1, keepdims=True)).astype(jnp.bfloat16)
    latent = jnp.einsum(
        "rthk,rkc->rthc", shares, context[:, :, :KV], preferred_element_type=jnp.float32
    )
    latent_out = latent.astype(jnp.bfloat16).reshape(rows_dev, HEADS * KV)
    scaled = route_scores / jnp.sum(route_scores, axis=1, keepdims=True) * 2.5
    combiner = jnp.sum(jnp.where(hits, scaled[:, :, None], 0.0), axis=1)
    summed = returned.reshape(experts, 2, capacity, width).astype(jnp.float32).sum(axis=1)
    mixed = jnp.dot(
        combiner, summed.reshape(experts * capacity, width), precision=lax.Precision.HIGHEST
    )
    moe_out = (residual.astype(jnp.float32) + mixed).astype(jnp.bfloat16)
    return (latent_out, moe_out)


def solution(mesh):
    placed = (
        P(("rep", "ep", "sub"), None),
        P(("rep", "ep", "sub"), None),
        P("rep", None),
        P("rep"),
        P("rep"),
        P(("rep", "ep", "sub"), None),
        P(("rep", "ep", "sub"), None),
        P(("rep", "ep", "sub"), None),
        P("ep", None, "sub"),
        P("ep", None, "sub"),
        P("ep", "sub", None),
    )
    return jax.shard_map(
        local,
        mesh=mesh,
        in_specs=placed,
        out_specs=(P(("rep", "ep", "sub"), None), P(("rep", "ep", "sub"), None)),
        check_vma=False,
    )
```

profile of v0, /device:TPU:15, one launch (start us, length us, event | category | flops | bytes accessed | tf_op | source)
XLA Modules:
  0.0 267.8 jit_solution(2568971549813214769)
XLA Ops:
  7.2 0.9 copy.91
  8.1 0.1 eq.36
  8.4 0.2 select_reduce_fusion.1
  8.6 0.1 copy.92
  8.7 0.7 multiply_add_fusion
  9.5 1.2 convolution_convert_fusion
  10.7 0.1 broadcast_in_dim.72
  10.8 0.2 broadcast_in_dim.73
  10.9 48.1 %all_to_all.15 = bf16[16,10,3584]{2,1,0:T(8,128)(2,1)} all-to-all(bf16[16,10,3584]{2,1,0:T(8,128)(2,1)S(1)} %bitcast.72), channel_id=1, replica_groups=mesh['rep'=2,'ep'=8,'sub'=2] {'ep','sub'}, dimensions={0} | all-to-all | bytes 2293760 | tf_op jit(solution)/shard_map/all_to_all | solution.py:76
  59.1 1.7 reshape.131
  60.8 2.0 fusion.14
  62.7 2.6 fusion.20
  65.4 0.9 dot_general.28
  66.3 3.4 %fusion.10 = f32[8,2,10,3584]{3,0,2,1:T(8,128)} fusion(bf16[1,256,3584]{2,1,0:T(8,128)(2,1)} %param.21, bf16[8,2,10,256]{3,2,1,0:T(8,128)(2,1)S(1)} %dot_general.28), kind=kOutput, calls=%fused_computation.22 | convolution fusion | flops 293601280 | bytes 4210688 | tf_op jit(solution)/shard_map/dot_general | solution.py:20
  69.7 0.1 copy.82
  69.8 0.6 gather_fusion.1
  70.5 0.1 copy.83
  70.6 9.5 %reduce-scatter.2.cloned.1.call-done = f32[8,1,10,3584]{3,0,2,1:T(8,128)} async-done(((f32[8,2,10,3584]{3,0,2,1:T(8,128)}), f32[8,1,10,3584]{3,0,2,1:T(8,128)}) %reduce-scatter.2.cloned.1.call-update) | async-done | bytes 1146896 | tf_op jit(solution)/shard_map/reduce_scatter | solution.py:80
  80.1 1.3 convert_bitcast_fusion
  81.4 1.1 copy.94
  82.5 5.5 %all-to-all-start.2 = ((bf16[8,10,3584]{2,1,0:T(8,128)(2,1)}), bf16[8,10,3584]{2,1,0:T(8,128)(2,1)S(1)}, u32[]{:S(2)}, u32[]{:S(2)}) async-start(bf16[8,10,3584]{2,1,0:T(8,128)(2,1)} %copy.94), calls=%async_computation.3 | async-start | bytes 1835008 | tf_op jit(solution)/shard_map/all_to_all | solution.py:83
  88.0 1.0 sort.48
  89.1 0.1 copy.87
  89.2 0.1 reshape.166
  89.2 0.8 gather_fusion.4
  90.1 0.1 copy.88
  90.2 0.1 copy.89
  90.3 0.1 sub.47
  90.5 5.8 %gather_fusion.2 = bf16[64,36864]{1,0:T(8,128)(2,1)} fusion(bf16[32,36864]{1,0:T(8,128)(2,1)S(1)} %copy-done, s32[1024]{0:T(1024)S(1)} %pad_clamp_fusion.1), kind=kCustom, calls=%fused_computation.2 | custom fusion | bytes 9437440 | tf_op jit(solution)/shard_map/gather | solution.py:51
  96.2 7.6 %reshape.125 = bf16[16,4,36864]{2,1,0:T(4,128)(2,1)} reshape(bf16[64,36864]{1,0:T(8,128)(2,1)} %gather_fusion.2) | data formatting | bytes 9437184 | tf_op jit(solution)/shard_map/reshape | solution.py:51
  103.8 4.7 %all-to-all-done.2 = bf16[8,10,3584]{2,1,0:T(8,128)(2,1)S(1)} async-done(((bf16[8,10,3584]{2,1,0:T(8,128)(2,1)}), bf16[8,10,3584]{2,1,0:T(8,128)(2,1)S(1)}, u32[]{:S(2)}, u32[]{:S(2)}) %all-to-all-start.2) | async-done | bytes 573472 | tf_op jit(solution)/shard_map/all_to_all | solution.py:83
  108.4 7.7 %all-to-all-start = ((bf16[16,4,36864]{2,1,0:T(4,128)(2,1)}), bf16[16,4,36864]{2,1,0:T(4,128)(2,1)}, u32[]{:S(2)}, u32[]{:S(2)}) async-start(bf16[16,4,36864]{2,1,0:T(4,128)(2,1)} %reshape.125), calls=%async_computation | async-start | bytes 9437184 | tf_op jit(solution)/shard_map/all_to_all | solution.py:52
  116.2 3.5 %reshape.128 = bf16[4,4,64,576]{3,2,1,0:T(8,128)(2,1)} reshape(bf16[16,36864]{1,0:T(8,128)(2,1)} %param.11) | data formatting | bytes 2359296 | tf_op jit(solution)/shard_map/reshape | solution.py:98
  119.7 2.0 sort.49
  121.7 2.0 sort.50
  123.9 0.6 gather_fusion
  124.7 0.1 iota_compare_fusion
  124.8 1.1 convert_reduce_fusion
  125.9 1.3 reshape.132
  127.2 1.1 fusion.3
  128.2 91.6 %all-to-all-done = bf16[16,4,36864]{2,1,0:T(4,128)(2,1)} async-done(((bf16[16,4,36864]{2,1,0:T(4,128)(2,1)}), bf16[16,4,36864]{2,1,0:T(4,128)(2,1)}, u32[]{:S(2)}, u32[]{:S(2)}) %all-to-all-start) | async-done | bytes 4718624 | tf_op jit(solution)/shard_map/all_to_all | solution.py:52
  219.9 7.4 %reshape.126 = bf16[64,36864]{1,0:T(8,128)(2,1)} reshape(bf16[16,4,36864]{2,1,0:T(4,128)(2,1)} %all-to-all-done) | data formatting | bytes 9437184 | tf_op jit(solution)/shard_map/reshape | solution.py:93
  227.2 12.7 %gather_fusion.3 = bf16[64,36864]{1,0:T(8,128)(2,1)} fusion(bf16[64,36864]{1,0:T(8,128)(2,1)} %reshape.126, s32[1024]{0:T(1024)S(1)} %pad_clamp_fusion), kind=kCustom, calls=%fused_computation.3 | custom fusion | bytes 9437440 | tf_op jit(solution)/shard_map/gather | solution.py:93
  240.0 9.9 %reshape.127 = bf16[4,1024,576]{2,1,0:T(8,128)(2,1)} reshape(bf16[64,36864]{1,0:T(8,128)(2,1)} %gather_fusion.3) | data formatting | bytes 9437184 | tf_op jit(solution)/shard_map/reshape | solution.py:93
  249.9 4.7 %fusion.1 = f32[4,1024,4,64]{1,3,2,0:T(8,128)S(1)} fusion(bf16[4,4,64,576]{3,2,1,0:T(8,128)(2,1)} %reshape.128, bf16[4,1024,576]{2,1,0:T(8,128)(2,1)} %reshape.127), kind=kOutput, calls=%fused_computation.6 | convolution fusion | flops 1207959552 | bytes 10092544 | tf_op jit(solution)/shard_map/rthc,rkc->rthk/dot_general | solution.py:100
  254.6 3.5 %fusion.32 = (f32[4,4,64]{2,1,0:T(4,128)S(1)}, f32[4,4,64,1024]{3,2,1,0:T(8,128)S(1)}) fusion(f32[4,1024,4,64]{1,3,2,0:T(8,128)S(1)} %fusion.1, pred[4,4,1024]{2,1,0:T(4,128)(4,1)S(1)} %iota_compare_fusion), kind=kOutput, calls=%fused_computation.73 | output fusion | flops 6292479 | bytes 8409088 | tf_op jit(solution)/shard_map/sub | solution.py:107
  258.1 1.3 fusion.16
  259.4 1.5 copy.105
  (42 shorter events, 0.9 us)
Async XLA Ops:
  7.2 83.3 %copy-start = (bf16[32,36864]{1,0:T(8,128)(2,1)S(1)}, bf16[32,36864]{1,0:T(8,128)(2,1)}, u32[]{:S(2)}) copy-start(bf16[32,36864]{1,0:T(8,128)(2,1)} %param.12) | copy-start | bytes 7077892
  7.2 72.9 %reduce-scatter.2.cloned.1.call-start = ((), (), s32[]{:S(2)}) async-start(), calls=%async_computation.4 | async-start | bytes 3440640 | tf_op jit(solution)/shard_map/reduce_scatter | solution.py:80
  65.4 4.4 %copy-start.4 = (s32[64,16]{0,1:T(8,128)S(1)}, s32[64,16]{0,1:T(8,128)}, u32[]{:S(2)}) copy-start(s32[64,16]{0,1:T(8,128)} %param.13) | copy-start | bytes 12292
  65.4 4.4 %copy-start.6 = (s32[64]{0:T(128)S(1)}, s32[64]{0:T(128)}, u32[]{:S(2)}) copy-start(s32[64]{0:T(128)} %param.14) | copy-start | bytes 772
  82.5 25.9 %all-to-all-start.2 = ((bf16[8,10,3584]{2,1,0:T(8,128)(2,1)}), bf16[8,10,3584]{2,1,0:T(8,128)(2,1)S(1)}, u32[]{:S(2)}, u32[]{:S(2)}) async-start(bf16[8,10,3584]{2,1,0:T(8,128)(2,1)} %copy.94), calls=%async_computation.3 | async-start | bytes 1835008 | tf_op jit(solution)/shard_map/all_to_all | solution.py:83
  103.8 20.1 %copy-start.1 = (s32[64]{0:T(128)S(1)}, s32[64]{0:T(128)}, u32[]{:S(2)}) copy-start(s32[64]{0:T(128)} %param.15) | copy-start | bytes 772
  103.8 20.7 %copy-start.5 = (f32[16,2]{0,1:T(2,128)S(1)}, f32[16,2]{0,1:T(2,128)}, u32[]{:S(2)}) copy-start(f32[16,2]{0,1:T(2,128)} %param.18) | copy-start | bytes 388
  108.4 111.4 %all-to-all-start = ((bf16[16,4,36864]{2,1,0:T(4,128)(2,1)}), bf16[16,4,36864]{2,1,0:T(4,128)(2,1)}, u32[]{:S(2)}, u32[]{:S(2)}) async-start(bf16[16,4,36864]{2,1,0:T(4,128)(2,1)} %reshape.125), calls=%async_computation | async-start | bytes 9437184 | tf_op jit(solution)/shard_map/all_to_all | solution.py:52
  116.2 11.0 %copy-start.3 = (bf16[16,3584]{1,0:T(8,128)(2,1)S(1)}, bf16[16,3584]{1,0:T(8,128)(2,1)}, u32[]{:S(2)}) copy-start(bf16[16,3584]{1,0:T(8,128)(2,1)} %param.16) | copy-start | bytes 344068
  254.6 3.5 %copy-start.2 = (bf16[4,1024,576]{2,1,0:T(8,128)(2,1)S(1)}, bf16[4,1024,576]{2,1,0:T(8,128)(2,1)}, u32[]{:S(2)}) copy-start(bf16[4,1024,576]{2,1,0:T(8,128)(2,1)} %reshape.127) | copy-start | bytes 14155780
Sparse Core Ops, SparseCore 0:
  69.8 10.2 reduce-scatter.1
where the time goes:
time: 269 us; the launch traced here: 268 us
  waiting for transfers between devices  106 us (39%)
  local copies, waits for them, and re-layouts  57.6 us (21%)
  blocking collectives  48.1 us (18%)
  matrix products  16.1 us (6%)
  between operations  14.3 us (5%)
  starting transfers between devices  13.3 us (5%)
  other arithmetic  12.6 us (5%)
    all_to_all x1, waiting for transfers between devices, local(): lax.all_to_all(outgoing, ('ep', 'sub'), split_axis=0, concat_axis=0, tile...  91.6 us
    all_to_all x1, blocking collectives, local(): lax.all_to_all(sending, ('ep', 'sub'), split_axis=0, concat_axis=0, tiled...  48.1 us
    reshape x2, local copies, waits for them, and re-layouts, local(): arrived.reshape(listed, -1)[placing]  17.3 us
    gather x1, local copies, waits for them, and re-layouts, local(): arrived.reshape(listed, -1)[placing]  12.7 us
    reduce_scatter x1, waiting for transfers between devices, local(): lax.psum_scatter(partial_value.reshape(n_ep, n_sub, capacity, width), 'su...  9.49 us
    all_to_all x1, starting transfers between devices, local(): lax.all_to_all(outgoing, ('ep', 'sub'), split_axis=0, concat_axis=0, tile...  7.72 us
    reshape x1, local copies, waits for them, and re-layouts, local(): page_pool[resident.reshape(-1)].reshape(peers, fetched, page_pool.shape[1])  7.56 us
    gather x1, local copies, waits for them, and re-layouts, local(): page_pool[resident.reshape(-1)].reshape(peers, fetched, page_pool.shape[1])  5.76 us
  transfers between devices with their start and end apart: 3, of which 3 were waited for; matrix products, arithmetic and copies ran while one was open for 11% of the time, Pallas kernels for 0%

commit v1 on v0

v1 whole, which is shorter than its diff:
```python
import functools

import jax
import jax.numpy as jnp
from jax import lax
from jax.experimental import pallas as pl
from jax.experimental.pallas import tpu as pltpu
from jax.sharding import PartitionSpec as P

HEADS = 64
LAT = 576
KV = 512
DRAFT = 4
HALF = 640
SHIFT = HALF - LAT

score_scale = 192.0 ** (-0.5)
masked_score = -1e30


def stage_body(index_ref, pool_ref, out_ref, pages, sems):
    pages[...] = pool_ref[...].reshape(pages.shape)

    def copy(slot):
        return pltpu.make_async_copy(pages.at[index_ref[slot]], out_ref.at[slot], sems.at[slot])

    def begin(slot, carry):
        copy(slot).start()
        return carry

    def finish(slot, carry):
        copy(slot).wait()
        return carry

    lax.fori_loop(0, out_ref.shape[0], begin, 0)
    lax.fori_loop(0, out_ref.shape[0], finish, 0)


def stage_pages(index, pool):
    pairs = pool.shape[1] // (2 * LAT)
    slots = index.shape[0]
    return pl.pallas_call(
        stage_body,
        out_shape=jax.ShapeDtypeStruct((slots, pairs, 2 * LAT), pool.dtype),
        in_specs=[
            pl.BlockSpec(memory_space=pltpu.SMEM),
            pl.BlockSpec(memory_space=pltpu.VMEM),
        ],
        out_specs=pl.BlockSpec(memory_space=pl.ANY),
        scratch_shapes=[
            pltpu.VMEM((pool.shape[0], pairs, 2 * LAT), pool.dtype),
            pltpu.SemaphoreType.DMA((slots,)),
        ],
        compiler_params=pltpu.CompilerParams(vmem_limit_bytes=32 << 20),
        name="stage_pages",
    )(index, pool)


def attend_body(place_ref, limit_ref, low_ref, high_ref, pages_ref, out_ref, context, held, sems):
    requests, each, pairs, width = context.shape
    rows = low_ref.shape[1]

    def copy(r, i):
        return pltpu.make_async_copy(
            pages_ref.at[place_ref[r * each + i]], context.at[r, i], sems.at[r, i]
        )

    for r in range(requests):

        def begin(i, carry, r=r):
            copy(r, i).start()
            return carry

        lax.fori_loop(0, each, begin, 0)

    columns = each * pairs
    position = 2 * lax.broadcasted_iota(jnp.int32, (rows, columns), 1)
    draft = lax.broadcasted_iota(jnp.int32, (rows, columns), 0) % DRAFT
    early = position - draft
    contract = (((1,), (1,)), ((), ()))
    for r in range(requests):

        def finish(i, carry, r=r):
            copy(r, i).wait()
            return carry

        lax.fori_loop(0, each, finish, 0)
        block = context[r].reshape(columns, width)
        even = lax.dot_general(
            low_ref[r], block[:, :HALF], contract, preferred_element_type=jnp.float32
        )
        odd = lax.dot_general(
            high_ref[r], block[:, width - HALF :], contract, preferred_element_type=jnp.float32
        )
        limit = limit_ref[r]
        even = jnp.where(early <= limit, even * score_scale, masked_score)
        odd = jnp.where(early <= limit - 1, odd * score_scale, masked_score)
        highest = jnp.maximum(
            jnp.max(even, axis=-1, keepdims=True), jnp.max(odd, axis=-1, keepdims=True)
        )
        even = jnp.exp(even - highest)
        odd = jnp.exp(odd - highest)
        total = jnp.sum(even, axis=-1, keepdims=True) + jnp.sum(odd, axis=-1, keepdims=True)
        even = (even / total).astype(jnp.bfloat16)
        odd = (odd / total).astype(jnp.bfloat16)
        latent = jnp.dot(even, block[:, :KV], preferred_element_type=jnp.float32)
        other = jnp.dot(odd, block[:, width - HALF :], preferred_element_type=jnp.float32)
        latent = latent + other[:, SHIFT : SHIFT + KV]
        for h in range(rows // DRAFT):
            held[r * DRAFT : (r + 1) * DRAFT, h * KV : (h + 1) * KV] = latent[
                h * DRAFT : (h + 1) * DRAFT, :
            ]
    out_ref[...] = held[...].astype(out_ref.dtype)


def attend(place, limits, low, high, pages, each):
    requests, rows, _ = low.shape
    _, pairs, width = pages.shape
    out = (requests * DRAFT, (rows // DRAFT) * KV)
    return pl.pallas_call(
        attend_body,
        out_shape=jax.ShapeDtypeStruct(out, jnp.bfloat16),
        in_specs=[
            pl.BlockSpec(memory_space=pltpu.SMEM),
            pl.BlockSpec(memory_space=pltpu.SMEM),
            pl.BlockSpec(memory_space=pltpu.VMEM),
            pl.BlockSpec(memory_space=pltpu.VMEM),
            pl.BlockSpec(memory_space=pl.ANY),
        ],
        out_specs=pl.BlockSpec(memory_space=pltpu.VMEM),
        scratch_shapes=[
            pltpu.VMEM((requests, each, pairs, width), pages.dtype),
            pltpu.VMEM(out, jnp.float32),
            pltpu.SemaphoreType.DMA((requests, each)),
        ],
        compiler_params=pltpu.CompilerParams(vmem_limit_bytes=48 << 20),
        name="attend_pages",
    )(place, limits, low, high, pages)


def local(
    queries,
    page_pool,
    page_table,
    serving,
    context_len,
    residual,
    routes,
    route_scores,
    w_gate,
    w_up,
    w_down,
):
    group = ("ep", "sub")
    peers = lax.axis_size(group)
    device = lax.axis_index(group)
    rows_dev, width = residual.shape
    requests_dev = rows_dev // DRAFT
    pages_each = page_table.shape[1]
    pool_pages = page_pool.shape[0]
    listed = requests_dev * pages_each
    fetched = listed // peers
    n_requests = serving.shape[0]

    slots = jnp.arange(n_requests, dtype=jnp.int32)
    named = serving[:, None] == slots[None, :]
    listing = jnp.sum(jnp.where(named[:, :, None], page_table[None], 0), axis=1).reshape(
        peers, listed
    )
    owners = listing // pool_pages
    mine = owners == device
    position = jnp.arange(listed, dtype=jnp.int32)
    earlier = (position[:, None] < position[None, :]).astype(jnp.bfloat16)
    rank = jnp.dot(mine.astype(jnp.bfloat16), earlier, preferred_element_type=jnp.float32).astype(
        jnp.int32
    )
    nth = jnp.arange(fetched, dtype=jnp.int32)
    taken = mine[:, None, :] & (rank[:, None, :] == nth[None, :, None])
    resident = jnp.sum(jnp.where(taken, listing[:, None, :] - device * pool_pages, 0), axis=2)
    outgoing = stage_pages(resident.reshape(-1), page_pool)
    pairs = outgoing.shape[1]
    arrived = lax.all_to_all(
        outgoing.reshape(peers, fetched, pairs, 2 * LAT), group, split_axis=0, concat_axis=0, tiled=True
    )

    n_ep = lax.axis_size("ep")
    experts = n_ep // 2
    scaled = route_scores / jnp.sum(route_scores, axis=1, keepdims=True) * 2.5
    labels = jnp.arange(experts, dtype=jnp.int32)
    weights = jnp.sum(
        jnp.where(routes[:, :, None] == labels[None, None, :], scaled[:, :, None], 0.0), axis=1
    )
    coarse = lax.reduce_precision(weights, 8, 7)
    rest = weights - coarse
    middle = lax.reduce_precision(rest, 8, 7)
    fine = lax.reduce_precision(rest - middle, 8, 7)
    side = jnp.concatenate([coarse, middle, fine], axis=1).astype(jnp.bfloat16)
    side = jnp.pad(side, ((0, 0), (0, -side.shape[1] % 128)))
    everyone = lax.all_gather(
        jnp.concatenate([residual, side], axis=1), group, axis=0, tiled=True
    )
    rows = everyone[:, :width]
    parts = everyone[:, width : width + 3 * experts].astype(jnp.float32)
    expert = lax.axis_index("ep") // 2
    own = (jnp.arange(3 * experts, dtype=jnp.int32) % experts) == expert
    weight = jnp.sum(jnp.where(own[None, :], parts, 0.0), axis=1, keepdims=True)
    gate = jnp.dot(rows, w_gate[0], preferred_element_type=jnp.float32)
    upward = jnp.dot(rows, w_up[0], preferred_element_type=jnp.float32)
    hidden = (jax.nn.silu(gate) * upward).astype(jnp.bfloat16)
    partial_out = jnp.dot(hidden, w_down[0], preferred_element_type=jnp.float32) * weight
    mixed = lax.psum_scatter(partial_out, group, scatter_dimension=0, tiled=True)
    moe_out = (residual.astype(jnp.float32) + mixed).astype(jnp.bfloat16)

    own_list = lax.dynamic_index_in_dim(owners, device, 0, keepdims=False)
    same = (own_list[:, None] == own_list[None, :]) & (position[None, :] < position[:, None])
    place = own_list * fetched + jnp.sum(same.astype(jnp.int32), axis=1)
    served = lax.dynamic_slice_in_dim(serving, device * requests_dev, requests_dev)
    limits = jnp.sum(
        jnp.where(served[:, None] == slots[None, :], context_len[None, :], 0), axis=1
    ) - DRAFT
    heads = queries.reshape(requests_dev, DRAFT, HEADS, LAT).transpose(0, 2, 1, 3)
    heads = heads.reshape(requests_dev, HEADS * DRAFT, LAT)
    low = jnp.pad(heads, ((0, 0), (0, 0), (0, SHIFT)))
    high = jnp.pad(heads, ((0, 0), (0, 0), (SHIFT, 0)))
    latent_out = attend(
        place, limits, low, high, arrived.reshape(listed, pairs, 2 * LAT), pages_each
    )
    return (latent_out, moe_out)


def solution(mesh):
    placed = (
        P(("rep", "ep", "sub"), None),
        P(("rep", "ep", "sub"), None),
        P("rep", None),
        P("rep"),
        P("rep"),
        P(("rep", "ep", "sub"), None),
        P(("rep", "ep", "sub"), None),
        P(("rep", "ep", "sub"), None),
        P("ep", None, "sub"),
        P("ep", None, "sub"),
        P("ep", "sub", None),
    )
    return jax.shard_map(
        local,
        mesh=mesh,
        in_specs=placed,
        out_specs=(P(("rep", "ep", "sub"), None), P(("rep", "ep", "sub"), None)),
        check_vma=False,
    )
```

time: 269 us -> 185 us (0.69)
  the two profiles are of different devices: /device:TPU:15 before, /device:TPU:0 now
where the time goes in v1:
time: 185 us
  waiting for transfers between devices  112 us (61%)
  Pallas kernels  17.9 us (10%)
  local copies, waits for them, and re-layouts  14.6 us (8%)
  between operations  14.2 us (8%)
  other arithmetic  9.47 us (5%)
  matrix products  8.82 us (5%)
  starting transfers between devices  7.69 us (4%)
    all_gather x1, waiting for transfers between devices, local(): lax.all_gather(jnp.concatenate([residual, side], axis=1), group, axis=0,...  43.2 us
    all_to_all x1, waiting for transfers between devices, local(): lax.all_to_all(outgoing.reshape(peers, fetched, pairs, 2 * LAT), group, s...  36 us
    reduce_scatter x1, waiting for transfers between devices, local(): lax.psum_scatter(partial_out, group, scatter_dimension=0, tiled=True)  32.8 us
    pallas_call x1, Pallas kernels, attend(): pl.pallas_call(attend_body, out_shape=jax.ShapeDtypeStruct(out, jnp.bfloa...  9.04 us
    pallas_call x1, Pallas kernels, stage_pages(): pl.pallas_call(stage_body, out_shape=jax.ShapeDtypeStruct((slots, pairs,...  8.82 us
    all_to_all x1, starting transfers between devices, local(): lax.all_to_all(outgoing.reshape(peers, fetched, pairs, 2 * LAT), group, s...  7.43 us
    dot_general x1, matrix products, local(): jnp.dot(hidden, w_down[0], preferred_element_type=jnp.float32) * weight  5.99 us
    unnamed x15, local copies, waits for them, and re-layouts  5.88 us
  transfers between devices with their start and end apart: 3, of which 3 were waited for; matrix products, arithmetic and copies ran while one was open for 12% of the time, Pallas kernels for 10%

profile of v1, /device:TPU:0, one launch (start us, length us, event | category | flops | bytes accessed | tf_op | source)
XLA Modules:
  0.0 184.6 jit_solution(12813961634264416724)
XLA Ops:
  7.2 0.0 copy-start
  7.2 0.0 all-gather.2.cloned.1.call-start
  7.2 0.8 reduce_sum.67
  8.0 0.7 divide_multiply_fusion
  8.7 0.7 select_reduce_fusion.3
  9.4 0.1 copy.28
  9.5 1.6 fusion.28
  11.1 0.0 all-gather.2.cloned.1.call-update
  11.1 0.7 iota_compare_fusion.4
  11.9 1.9 %select_reduce_fusion = s32[64,16]{1,0:T(8,128)S(1)} fusion(s32[64,16]{0,1:T(8,128)} %param.13, pred[64,64]{1,0:T(8,128)(4,1)S(1)} %iota_compare_fusion.4), kind=kLoop, calls=%fused_computation.11 | loop fusion | flops 130048 | bytes 12288 | tf_op jit(solution)/shard_map/reduce_sum | solution.py:167
  13.7 0.1 reshape.99
  13.8 0.1 convolution_convert_fusion
  14.0 0.2 select_reduce_fusion.2
  14.1 0.1 copy.26
  14.2 0.1 reshape.102.index_ref
  14.3 0.0 copy-start.3
  14.3 1.7 copy-done.3
  16.0 8.8 %stage_pages.1 = bf16[64,32,1152]{2,1,0:T(8,128)(2,1)S(1)} custom-call(s32[64]{0:T(128)S(1)} %reshape.102.index_ref, bf16[32,36864]{1,0:T(8,128)(2,1)S(1)} %copy-done.3), custom_call_target="tpu_custom_call" | custom-call | tf_op jit(solution)/shard_map/stage_pages/pallas_call | solution.py:42
  24.8 0.0 copy-start.1
  24.8 2.2 %copy-done.1 = bf16[64,32,1152]{2,1,0:T(8,128)(2,1)} copy-done((bf16[64,32,1152]{2,1,0:T(8,128)(2,1)}, bf16[64,32,1152]{2,1,0:T(8,128)(2,1)S(1)}, u32[]{:S(2)}) %copy-start.1) | copy-done | bytes 4718616
  27.0 7.4 %all-to-all-start = ((bf16[16,4,32,1152]{3,2,1,0:T(8,128)(2,1)}), bf16[16,4,32,1152]{3,2,1,0:T(8,128)(2,1)}, u32[]{:S(2)}, u32[]{:S(2)}) async-start(bf16[16,4,32,1152]{3,2,1,0:T(8,128)(2,1)} %bitcast.25), calls=%async_computation | async-start | bytes 9437184 | tf_op jit(solution)/shard_map/all_to_all | solution.py:182
  34.4 0.2 reduce-scatter.2.cloned.1.call-start
  34.7 43.2 %all-gather.2.cloned.1.call-done = bf16[256,3712]{1,0:T(8,128)(2,1)} async-done(((bf16[16,3712]{1,0:T(8,128)(2,1)}), bf16[256,3712]{1,0:T(8,128)(2,1)}) %all-gather.2.cloned.1.call-update) | async-done | bytes 1900560 | tf_op jit(solution)/shard_map/all_gather | solution.py:199
  77.9 0.9 select_reduce_fusion.1
  78.9 2.7 %fusion.3 = f32[256,256]{1,0:T(8,128)S(1)} fusion(bf16[1,3584,256]{2,1,0:T(8,128)(2,1)} %param.19, bf16[256,3712]{1,0:T(8,128)(2,1)} %all-gather.2.cloned.1.call-done), kind=kOutput, calls=%fused_computation.4 | convolution fusion | flops 469762048 | bytes 3932160 | tf_op jit(solution)/shard_map/dot_general | solution.py:207
  81.6 0.0 copy-done
  81.6 6.0 %convolution_multiply_fusion = f32[256,3584]{1,0:T(8,128)} fusion(bf16[1,256,3584]{2,1,0:T(8,128)(2,1)S(1)} %copy-done, f32[256]{0:T(256)S(1)} %select_reduce_fusion.1, bf16[1,3584,256]{2,1,0:T(8,128)(2,1)} %param.20, bf16[256,3712]{1,0:T(8,128)(2,1)} %all-gather.2.cloned.1.call-done, f32[256,256]{1,0:T(8,128)S(1)} %fusion.3), kind=kOutput, calls=%fused_computation | convolution fusion | flops 940834816 | bytes 9438208 | tf_op jit(solution)/shard_map/dot_general | solution.py:210
  87.6 0.0 copy-start.5
  87.6 0.0 reduce-scatter.2.cloned.1.call-update
  87.6 0.6 copy-done.5
  88.2 0.1 dynamic_slice.8
  88.3 2.7 %reshape.100 = bf16[4,4,64,576]{3,2,1,0:T(8,128)(2,1)S(1)} reshape(bf16[16,36864]{1,0:T(8,128)(2,1)} %param.11) | data formatting | bytes 2359296 | tf_op jit(solution)/shard_map/reshape | solution.py:221
  90.9 1.0 copy.23
  92.0 0.0 copy-start.6
  92.0 1.2 copy.24
  93.2 0.2 convert_reduce_fusion
  93.4 0.0 copy-done.6
  93.4 0.2 select_reduce_fusion.4
  93.6 3.5 %fusion.37 = (bf16[4,256,640]{2,1,0:T(8,128)(2,1)S(1)}, bf16[4,256,640]{2,1,0:T(8,128)(2,1)}) fusion(bf16[4,256,576]{2,1,0:T(8,128)(2,1)} %copy.24), kind=kLoop, calls=%fused_computation.58 | loop fusion | bytes 3801088 | tf_op jit(solution)/shard_map/jit(_pad)/pad | solution.py:224
  97.1 36.0 %all-to-all-done = bf16[16,4,32,1152]{3,2,1,0:T(8,128)(2,1)} async-done(((bf16[16,4,32,1152]{3,2,1,0:T(8,128)(2,1)}), bf16[16,4,32,1152]{3,2,1,0:T(8,128)(2,1)}, u32[]{:S(2)}, u32[]{:S(2)}) %all-to-all-start) | async-done | bytes 4718624 | tf_op jit(solution)/shard_map/all_to_all | solution.py:182
  133.1 0.0 copy-start.2
  133.1 1.3 copy-done.2
  134.4 0.0 copy-start.4
  134.4 9.0 %attend_pages.1 = bf16[16,32768]{1,0:T(8,128)(2,1)} custom-call(s32[64]{0:T(128)S(1)} %multiply_add_fusion.place_ref, s32[4]{0:T(128)S(1)} %broadcast_add_fusion.limit_ref, bf16[4,256,640]{2,1,0:T(8,128)(2,1)S(1)} %copy-done.2, bf16[4,256,640]{2,1,0:T(8,128)(2,1)S(1)} %get-tuple-element.4.high_ref, bf16[64,32,1152]{2,1,0:T(8,128)(2,1)} %bitcast.5.pages_ref), custom_call_target="tpu_custom_call" | custom-call | tf_op jit(solution)/shard_map/attend_pages/pallas_call | solution.py:120
  143.4 32.8 %reduce-scatter.2.cloned.1.call-done = f32[16,3584]{1,0:T(8,128)} async-done(((f32[256,3584]{1,0:T(8,128)}), f32[16,3584]{1,0:T(8,128)}) %reduce-scatter.2.cloned.1.call-update) | async-done | bytes 229392 | tf_op jit(solution)/shard_map/reduce_scatter | solution.py:211
  176.2 0.0 copy-done.4
  176.2 1.6 add_convert_fusion
  (8 shorter events, 0.1 us)
Async XLA Ops:
  7.2 74.4 %copy-start = (bf16[1,256,3584]{2,1,0:T(8,128)(2,1)S(1)}, bf16[1,256,3584]{2,1,0:T(8,128)(2,1)}, u32[]{:S(2)}) copy-start(bf16[1,256,3584]{2,1,0:T(8,128)(2,1)} %param.21) | copy-start | bytes 5505028
  7.2 70.7 %all-gather.2.cloned.1.call-start = ((), (), s32[]{:S(2)}) async-start(), calls=%async_computation.2 | async-start | bytes 2019328 | tf_op jit(solution)/shard_map/all_gather | solution.py:199
  14.3 1.7 copy-start.3
  24.8 2.2 %copy-start.1 = (bf16[64,32,1152]{2,1,0:T(8,128)(2,1)}, bf16[64,32,1152]{2,1,0:T(8,128)(2,1)S(1)}, u32[]{:S(2)}) copy-start(bf16[64,32,1152]{2,1,0:T(8,128)(2,1)S(1)} %stage_pages.1) | copy-start | bytes 14155780
  27.0 106.1 %all-to-all-start = ((bf16[16,4,32,1152]{3,2,1,0:T(8,128)(2,1)}), bf16[16,4,32,1152]{3,2,1,0:T(8,128)(2,1)}, u32[]{:S(2)}, u32[]{:S(2)}) async-start(bf16[16,4,32,1152]{3,2,1,0:T(8,128)(2,1)} %bitcast.25), calls=%async_computation | async-start | bytes 9437184 | tf_op jit(solution)/shard_map/all_to_all | solution.py:182
  34.4 141.8 %reduce-scatter.2.cloned.1.call-start = ((), (), s32[]{:S(2)}) async-start(), calls=%async_computation.3 | async-start | bytes 3899392 | tf_op jit(solution)/shard_map/reduce_scatter | solution.py:211
  87.6 0.7 copy-start.5
  92.0 1.4 copy-start.6
  133.1 1.3 copy-start.2
  134.4 41.8 %copy-start.4 = (bf16[16,3584]{1,0:T(8,128)(2,1)S(1)}, bf16[16,3584]{1,0:T(8,128)(2,1)}, u32[]{:S(2)}) copy-start(bf16[16,3584]{1,0:T(8,128)(2,1)} %param.16) | copy-start | bytes 344068
Sparse Core Ops, SparseCore 0:
  11.2 66.6 all-gather.1
  87.7 88.4 reduce-scatter.1

commit v2 on v1

--- a/solution.py
+++ b/solution.py
@@ -18,42 +18,160 @@
 masked_score = -1e30
 
 
-def stage_body(index_ref, pool_ref, out_ref, pages, sems):
-    pages[...] = pool_ref[...].reshape(pages.shape)
-
-    def copy(slot):
-        return pltpu.make_async_copy(pages.at[index_ref[slot]], out_ref.at[slot], sems.at[slot])
-
-    def begin(slot, carry):
-        copy(slot).start()
+def ones_where(condition):
+    return jnp.where(condition, 1.0, 0.0).astype(jnp.bfloat16)
+
+
+def count(left, right):
+    return jnp.dot(left, right, preferred_element_type=jnp.float32)
+
+
+def stage_body(
+    peers, device_ref, table_ref, serving_ref, pool_ref, out_ref, pool, pages, order, index, *sems
+):
+    pool_sem, order_sem, page_sems = sems
+    fetch = pltpu.make_async_copy(pool_ref, pool, pool_sem)
+    fetch.start()
+    each, slots = table_ref.shape
+    span = slots // peers
+    fetched = out_ref.shape[0] // peers
+    held = jnp.full((each, slots), pool.shape[0], jnp.int32)
+    table = table_ref[...]
+    named = ones_where(lax.broadcasted_iota(jnp.int32, (slots, slots), 0) == serving_ref[...])
+    owner = count(lax.div(table, held).astype(jnp.float32).astype(jnp.bfloat16), named)
+    place = count(lax.rem(table, held).astype(jnp.float32).astype(jnp.bfloat16), named)
+    mine = owner == device_ref[0].astype(jnp.float32)
+    flags = ones_where(mine)
+    above = lax.broadcasted_iota(jnp.int32, (each, each), 1) < lax.broadcasted_iota(
+        jnp.int32, (each, each), 0
+    )
+    first = lax.broadcasted_iota(jnp.int32, (slots, slots), 0)
+    second = lax.broadcasted_iota(jnp.int32, (slots, slots), 1)
+    spans = jnp.full((slots, slots), span, jnp.int32)
+    before = (lax.div(first, spans) == lax.div(second, spans)) & (first < second)
+    whole = jnp.ones((each, each), jnp.bfloat16)
+    rank = count(ones_where(above), flags) + count(
+        count(whole, flags).astype(jnp.bfloat16), ones_where(before)
+    )
+    serves = ones_where(
+        lax.div(
+            lax.broadcasted_iota(jnp.int32, (slots, peers), 0),
+            jnp.full((slots, peers), span, jnp.int32),
+        )
+        == lax.broadcasted_iota(jnp.int32, (slots, peers), 1)
+    )
+    for k in range(fetched):
+        chosen = jnp.where(mine & (rank == k), place, 0.0).astype(jnp.bfloat16)
+        column = count(count(whole, chosen).astype(jnp.bfloat16), serves)
+        order[k : k + 1, :peers] = column[:1].astype(jnp.int32)
+    listing = pltpu.make_async_copy(order, index, order_sem)
+    listing.start()
+    fetch.wait()
+    pages[...] = pool[...].reshape(pages.shape)
+    listing.wait()
+
+    def copy(p, k):
+        slot = p * fetched + k
+        return pltpu.make_async_copy(pages.at[index[k, p]], out_ref.at[slot], page_sems.at[slot])
+
+    def begin(p, carry):
+        for k in range(fetched):
+            copy(p, k).start()
         return carry
 
-    def finish(slot, carry):
-        copy(slot).wait()
+    def finish(p, carry):
+        for k in range(fetched):
+            copy(p, k).wait()
         return carry
 
-    lax.fori_loop(0, out_ref.shape[0], begin, 0)
-    lax.fori_loop(0, out_ref.shape[0], finish, 0)
-
-
-def stage_pages(index, pool):
+    lax.fori_loop(0, peers, begin, 0)
+    lax.fori_loop(0, peers, finish, 0)
+
+
+def stage_pages(device, table, serving, pool, peers, slots):
     pairs = pool.shape[1] // (2 * LAT)
-    slots = index.shape[0]
+    fetched = slots // peers
+    listing = (fetched + -fetched % 8, peers + -peers % 128)
     return pl.pallas_call(
-        stage_body,
+        functools.partial(stage_body, peers),
         out_shape=jax.ShapeDtypeStruct((slots, pairs, 2 * LAT), pool.dtype),
         in_specs=[
             pl.BlockSpec(memory_space=pltpu.SMEM),
             pl.BlockSpec(memory_space=pltpu.VMEM),
+            pl.BlockSpec(memory_space=pltpu.VMEM),
+            pl.BlockSpec(memory_space=pltpu.HBM),
         ],
-        out_specs=pl.BlockSpec(memory_space=pl.ANY),
+        out_specs=pl.BlockSpec(memory_space=pltpu.HBM),
         scratch_shapes=[
+            pltpu.VMEM(pool.shape, pool.dtype),
             pltpu.VMEM((pool.shape[0], pairs, 2 * LAT), pool.dtype),
+            pltpu.VMEM(listing, jnp.int32),
+            pltpu.SMEM(listing, jnp.int32),
+            pltpu.SemaphoreType.DMA,
+            pltpu.SemaphoreType.DMA,
             pltpu.SemaphoreType.DMA((slots,)),
         ],
         compiler_params=pltpu.CompilerParams(vmem_limit_bytes=32 << 20),
         name="stage_pages",
-    )(index, pool)
+    )(device, table, serving, pool)
+
+
+def pack_body(experts, routes_ref, scores_ref, rows_ref, out_ref):
+    top, rows = routes_ref.shape
+    width = rows_ref.shape[1]
+    scores = scores_ref[...]
+    scaled = scores / jnp.sum(scores, axis=0, keepdims=True) * 2.5
+    labels = lax.broadcasted_iota(jnp.int32, (experts, rows), 0)
+    weights = jnp.zeros((experts, rows), jnp.float32)
+    for k in range(top):
+        weights += jnp.where(labels == routes_ref[k : k + 1, :], scaled[k : k + 1, :], 0.0)
+    out_ref[:, :width] = rows_ref[...]
+    side = jnp.zeros((rows, out_ref.shape[1] - width), jnp.float32)
+    line = lax.broadcasted_iota(jnp.int32, (experts, side.shape[1]), 1)
+    entry = lax.broadcasted_iota(jnp.int32, (experts, side.shape[1]), 0)
+    for part in range(3):
+        piece = weights.astype(jnp.bfloat16)
+        weights = weights - piece.astype(jnp.float32)
+        side += lax.dot_general(
+            piece,
+            ones_where(line == entry + part * experts),
+            (((0,), (0,)), ((), ())),
+            preferred_element_type=jnp.float32,
+        )
+    out_ref[:, width:] = side.astype(out_ref.dtype)
+
+
+def pack_rows(routes, scores, rows, experts):
+    side = 3 * experts
+    width = rows.shape[1] + side + -side % 128
+    return pl.pallas_call(
+        functools.partial(pack_body, experts),
+        out_shape=jax.ShapeDtypeStruct((rows.shape[0], width), rows.dtype),
+        name="pack_rows",
+    )(routes, scores, rows)
+
+
+def exchange(block, group, bit):
+    peers = lax.axis_size(group)
+    return lax.ppermute(block, group, [(d, d ^ bit) for d in range(peers)])
+
+
+def spread(block, group):
+    bit = lax.axis_size(group) // 2
+    while bit:
+        block = jnp.concatenate([block, exchange(block, group, bit)], axis=0)
+        bit //= 2
+    return block
+
+
+def collect(total, group):
+    bit = 1
+    while bit < lax.axis_size(group):
+        half = total.shape[0] // 2
+        sent = exchange(total[half:].astype(jnp.bfloat16), group, bit)
+        total = total[:half] + sent.astype(jnp.float32)
+        bit *= 2
+    return total
 
 
 def attend_body(place_ref, limit_ref, low_ref, high_ref, pages_ref, out_ref, context, held, sems):
@@ -125,7 +243,7 @@
             pl.BlockSpec(memory_space=pltpu.SMEM),
             pl.BlockSpec(memory_space=pltpu.VMEM),
             pl.BlockSpec(memory_space=pltpu.VMEM),
-            pl.BlockSpec(memory_space=pl.ANY),
+            pl.BlockSpec(memory_space=pltpu.HBM),
         ],
         out_specs=pl.BlockSpec(memory_space=pltpu.VMEM),
         scratch_shapes=[
@@ -162,43 +280,18 @@
     fetched = listed // peers
     n_requests = serving.shape[0]
 
-    slots = jnp.arange(n_requests, dtype=jnp.int32)
-    named = serving[:, None] == slots[None, :]
-    listing = jnp.sum(jnp.where(named[:, :, None], page_table[None], 0), axis=1).reshape(
-        peers, listed
-    )
-    owners = listing // pool_pages
-    mine = owners == device
-    position = jnp.arange(listed, dtype=jnp.int32)
-    earlier = (position[:, None] < position[None, :]).astype(jnp.bfloat16)
-    rank = jnp.dot(mine.astype(jnp.bfloat16), earlier, preferred_element_type=jnp.float32).astype(
-        jnp.int32
-    )
-    nth = jnp.arange(fetched, dtype=jnp.int32)
-    taken = mine[:, None, :] & (rank[:, None, :] == nth[None, :, None])
-    resident = jnp.sum(jnp.where(taken, listing[:, None, :] - device * pool_pages, 0), axis=2)
-    outgoing = stage_pages(resident.reshape(-1), page_pool)
+    n_ep = lax.axis_size("ep")
+    experts = n_ep // 2
+    everyone = spread(pack_rows(routes.T, route_scores.T, residual, experts), group)
+
+    outgoing = stage_pages(
+        device.reshape(1), page_table.T, serving.reshape(1, -1), page_pool, peers, listed
+    )
     pairs = outgoing.shape[1]
     arrived = lax.all_to_all(
         outgoing.reshape(peers, fetched, pairs, 2 * LAT), group, split_axis=0, concat_axis=0, tiled=True
     )
 
-    n_ep = lax.axis_size("ep")
-    experts = n_ep // 2
-    scaled = route_scores / jnp.sum(route_scores, axis=1, keepdims=True) * 2.5
-    labels = jnp.arange(experts, dtype=jnp.int32)
-    weights = jnp.sum(
-        jnp.where(routes[:, :, None] == labels[None, None, :], scaled[:, :, None], 0.0), axis=1
-    )
-    coarse = lax.reduce_precision(weights, 8, 7)
-    rest = weights - coarse
-    middle = lax.reduce_precision(rest, 8, 7)
-    fine = lax.reduce_precision(rest - middle, 8, 7)
-    side = jnp.concatenate([coarse, middle, fine], axis=1).astype(jnp.bfloat16)
-    side = jnp.pad(side, ((0, 0), (0, -side.shape[1] % 128)))
-    everyone = lax.all_gather(
-        jnp.concatenate([residual, side], axis=1), group, axis=0, tiled=True
-    )
     rows = everyone[:, :width]
     parts = everyone[:, width : width + 3 * experts].astype(jnp.float32)
     expert = lax.axis_index("ep") // 2
@@ -208,16 +301,18 @@
     upward = jnp.dot(rows, w_up[0], preferred_element_type=jnp.float32)
     hidden = (jax.nn.silu(gate) * upward).astype(jnp.bfloat16)
     partial_out = jnp.dot(hidden, w_down[0], preferred_element_type=jnp.float32) * weight
-    mixed = lax.psum_scatter(partial_out, group, scatter_dimension=0, tiled=True)
+    mixed = collect(partial_out, group)
     moe_out = (residual.astype(jnp.float32) + mixed).astype(jnp.bfloat16)
 
-    own_list = lax.dynamic_index_in_dim(owners, device, 0, keepdims=False)
+    served = lax.dynamic_slice_in_dim(serving, device * requests_dev, requests_dev)
+    slots = jnp.arange(n_requests, dtype=jnp.int32)
+    chosen = served[:, None] == slots[None, :]
+    own_list = jnp.sum(jnp.where(chosen[:, :, None], page_table[None], 0), axis=1)
+    own_list = own_list.reshape(-1) // pool_pages
+    position = jnp.arange(listed, dtype=jnp.int32)
     same = (own_list[:, None] == own_list[None, :]) & (position[None, :] < position[:, None])
     place = own_list * fetched + jnp.sum(same.astype(jnp.int32), axis=1)
-    served = lax.dynamic_slice_in_dim(serving, device * requests_dev, requests_dev)
-    limits = jnp.sum(
-        jnp.where(served[:, None] == slots[None, :], context_len[None, :], 0), axis=1
-    ) - DRAFT
+    limits = jnp.sum(jnp.where(chosen, context_len[None, :], 0), axis=1) - DRAFT
     heads = queries.reshape(requests_dev, DRAFT, HEADS, LAT).transpose(0, 2, 1, 3)
     heads = heads.reshape(requests_dev, HEADS * DRAFT, LAT)
     low = jnp.pad(heads, ((0, 0), (0, 0), (0, SHIFT)))

time: 185 us -> 156 us (0.84)
  the two profiles are of different devices: /device:TPU:0 before, /device:TPU:15 now
where the time goes in v2:
time: 156 us; the launch traced here: 153 us
  waiting for transfers between devices  74 us (47%)
  starting transfers between devices  28.5 us (18%)
  Pallas kernels  19.7 us (13%)
  local copies, waits for them, and re-layouts  16.7 us (11%)
  matrix products  6.73 us (4%)
  other arithmetic  6.62 us (4%)
    ppermute x8, waiting for transfers between devices, exchange(): return lax.ppermute(block, group, [(d, d ^ bit) for d in range(peers)])  74 us
    ppermute x8, starting transfers between devices, exchange(): return lax.ppermute(block, group, [(d, d ^ bit) for d in range(peers)])  20.7 us
    pallas_call x1, Pallas kernels, attend(): pl.pallas_call(attend_body, out_shape=jax.ShapeDtypeStruct(out, jnp.bfloa...  9.04 us
    unnamed x36, local copies, waits for them, and re-layouts  8.99 us
    pallas_call x1, Pallas kernels, stage_pages(): pl.pallas_call(functools.partial(stage_body, peers), out_shape=jax.ShapeD...  8.76 us
    all_to_all x1, starting transfers between devices, local(): lax.all_to_all(outgoing.reshape(peers, fetched, pairs, 2 * LAT), group, s...  7.73 us
    dot_general x1, matrix products, local(): jnp.dot(hidden, w_down[0], preferred_element_type=jnp.float32) * weight  6.07 us
    add x3, other arithmetic, collect(): total = total[:half] + sent.astype(jnp.float32)  4.17 us
  transfers between devices with their start and end apart: 9, of which 7 were waited for; matrix products, arithmetic and copies ran while one was open for 13% of the time, Pallas kernels for 6%

profile of v2, /device:TPU:15, one launch (start us, length us, event | category | flops | bytes accessed | tf_op | source)
XLA Modules:
  0.0 153.1 jit_solution(17801406032709304456)
XLA Ops:
  0.6 1.9 %pack_rows.1 = bf16[16,3712]{1,0:T(8,128)(2,1)} custom-call(s32[2,16]{1,0:T(2,128)} %bitcast.27, f32[2,16]{1,0:T(2,128)} %bitcast.28, bf16[16,3584]{1,0:T(8,128)(2,1)} %rows_ref.1), custom_call_target="tpu_custom_call" | custom-call | tf_op jit(solution)/shard_map/pack_rows/pallas_call | solution.py:147
  2.6 2.3 %collective-permute-start = (bf16[16,3712]{1,0:T(8,128)(2,1)}, bf16[16,3712]{1,0:T(8,128)(2,1)S(1)}, u32[]{:S(2)}, u32[]{:S(2)}) collective-permute-start(bf16[16,3712]{1,0:T(8,128)(2,1)} %pack_rows.1), channel_id=1, source_target_pairs={{0,8},{1,9},{2,10},{3,11},{4,12},{5,13},{6,14},{7,15},{8,0},{9,1},... | collective-permute-start | bytes 356360 | tf_op jit(solution)/shard_map/ppermute | solution.py:156
  4.9 5.7 %collective-permute-done = bf16[16,3712]{1,0:T(8,128)(2,1)S(1)} collective-permute-done((bf16[16,3712]{1,0:T(8,128)(2,1)}, bf16[16,3712]{1,0:T(8,128)(2,1)S(1)}, u32[]{:S(2)}, u32[]{:S(2)}) %collective-permute-start) | collective-permute-done | bytes 118816 | tf_op jit(solution)/shard_map/ppermute | solution.py:156
  10.6 0.9 pad_maximum_fusion.2
  11.5 0.1 collective-permute-start.1
  11.6 1.7 %copy-done.3 = bf16[32,36864]{1,0:T(8,128)(2,1)S(1)} copy-done((bf16[32,36864]{1,0:T(8,128)(2,1)S(1)}, bf16[32,36864]{1,0:T(8,128)(2,1)}, u32[]{:S(2)}) %copy-start.3) | copy-done | bytes 2359320
  13.2 0.7 copy-done.4
  13.9 0.7 copy-done.6
  14.6 8.8 %stage_pages.1 = bf16[64,32,1152]{2,1,0:T(8,128)(2,1)S(1)} custom-call(s32[1]{0:T(128)} %bitcast.3.device_ref, s32[16,64]{1,0:T(8,128)S(1)} %bitcast.24, s32[1,64]{1,0:T(1,128)S(1)} %bitcast.25, bf16[32,36864]{1,0:T(8,128)(2,1)S(1)} %copy-done.3), custom_call_target="tpu_custom_call" | custom-call | tf_op jit(solution)/shard_map/stage_pages/pallas_call | solution.py:95
  23.4 2.2 %copy-done.1 = bf16[64,32,1152]{2,1,0:T(8,128)(2,1)} copy-done((bf16[64,32,1152]{2,1,0:T(8,128)(2,1)}, bf16[64,32,1152]{2,1,0:T(8,128)(2,1)S(1)}, u32[]{:S(2)}) %copy-start.1) | copy-done | bytes 4718616
  25.6 7.7 %all-to-all-start = ((bf16[16,4,32,1152]{3,2,1,0:T(8,128)(2,1)}), bf16[16,4,32,1152]{3,2,1,0:T(8,128)(2,1)}, u32[]{:S(2)}, u32[]{:S(2)}) async-start(bf16[16,4,32,1152]{3,2,1,0:T(8,128)(2,1)} %bitcast.23), calls=%async_computation | async-start | bytes 9437184 | tf_op jit(solution)/shard_map/all_to_all | solution.py:291
  33.3 0.1 pad_maximum_fusion.1
  33.4 0.3 collective-permute-start.2
  33.7 36.3 %collective-permute-done.2 = bf16[64,3712]{1,0:T(8,128)(2,1)S(1)} collective-permute-done((bf16[64,3712]{1,0:T(8,128)(2,1)S(1)}, bf16[64,3712]{1,0:T(8,128)(2,1)S(1)}, u32[]{:S(2)}, u32[]{:S(2)}) %collective-permute-start.2) | collective-permute-done | bytes 475168 | tf_op jit(solution)/shard_map/ppermute | solution.py:156
  70.0 0.1 pad_maximum_fusion
  70.1 0.9 collective-permute-start.3
  71.1 2.1 %collective-permute-done.3 = bf16[128,3712]{1,0:T(8,128)(2,1)S(1)} collective-permute-done((bf16[128,3712]{1,0:T(8,128)(2,1)S(1)}, bf16[128,3712]{1,0:T(8,128)(2,1)S(1)}, u32[]{:S(2)}, u32[]{:S(2)}) %collective-permute-start.3) | collective-permute-done | bytes 950304 | tf_op jit(solution)/shard_map/ppermute | solution.py:156
  73.2 0.1 constant_dynamic-update-slice_fusion
  73.3 0.1 select_reduce_fusion
  73.4 1.1 copy-done.12
  74.5 0.7 fusion.1
  75.2 6.1 %convolution_multiply_fusion = f32[256,3584]{1,0:T(8,128)} fusion(bf16[1,256,3584]{2,1,0:T(8,128)(2,1)S(1)} %copy-done, f32[256]{0:T(256)S(1)} %select_reduce_fusion, f32[256,256]{1,0:T(8,128)S(1)} %fusion.1, bf16[1,3584,256]{2,1,0:T(8,128)(2,1)} %param.19, bf16[256,3712]{1,0:T(8,128)(2,1)} %copy-done.12), kind=kOutput, calls=%fused_computation | convolution fusion | flops 940834816 | bytes 9438208 | tf_op jit(solution)/shard_map/dot_general | solution.py:303
  81.3 1.6 %slice.75 = bf16[128,3584]{1,0:T(8,128)(2,1)S(1)} slice(f32[256,3584]{1,0:T(8,128)} %convolution_multiply_fusion), slice={[128:256], [0:3584]} | slice | bytes 1835008 | tf_op jit(solution)/shard_map/slice | solution.py:171
  82.9 0.4 collective-permute-start.4
  83.3 0.1 dynamic_slice.3
  83.4 0.2 select_reduce_fusion.2
  83.6 0.1 iota_compare_fusion.1
  83.7 1.9 %collective-permute-done.4 = bf16[128,3584]{1,0:T(8,128)(2,1)} collective-permute-done((bf16[128,3584]{1,0:T(8,128)(2,1)S(1)}, bf16[128,3584]{1,0:T(8,128)(2,1)}, u32[]{:S(2)}, u32[]{:S(2)}) %collective-permute-start.4) | collective-permute-done | bytes 917536 | tf_op jit(solution)/shard_map/ppermute | solution.py:156
  85.6 1.9 %slice_add_fusion = f32[128,3584]{1,0:T(8,128)S(1)} fusion(f32[256,3584]{1,0:T(8,128)} %convolution_multiply_fusion, bf16[128,3584]{1,0:T(8,128)(2,1)} %collective-permute-done.4), kind=kLoop, calls=%fused_computation.2 | loop fusion | flops 917504 | bytes 4587520 | tf_op jit(solution)/shard_map/add | solution.py:172
  87.5 1.2 copy-done.8
  88.8 0.1 collective-permute-start.5
  88.8 0.1 select_reduce_fusion.1
  89.0 0.1 reshape.115
  89.1 24.1 %collective-permute-done.5 = bf16[64,3584]{1,0:T(8,128)(2,1)S(1)} collective-permute-done((bf16[64,3584]{1,0:T(8,128)(2,1)S(1)}, bf16[64,3584]{1,0:T(8,128)(2,1)S(1)}, u32[]{:S(2)}, u32[]{:S(2)}) %collective-permute-start.5) | collective-permute-done | bytes 458784 | tf_op jit(solution)/shard_map/ppermute | solution.py:156
  113.2 1.3 slice_add_fusion.1
  114.5 7.6 %collective-permute-start.6 = (bf16[32,3584]{1,0:T(8,128)(2,1)S(1)}, bf16[32,3584]{1,0:T(8,128)(2,1)}, u32[]{:S(2)}, u32[]{:S(2)}) collective-permute-start(bf16[32,3584]{1,0:T(8,128)(2,1)S(1)} %slice.77), channel_id=1, source_target_pairs={{0,4},{1,5},{2,6},{3,7},{4,0},{5,1},{6,2},{7,3},{8,12},{9,13},{10,... | collective-permute-start | bytes 688136 | tf_op jit(solution)/shard_map/ppermute | solution.py:156
  122.1 0.2 convert_reduce_fusion
  122.3 2.7 %reshape.116 = bf16[4,4,64,576]{3,2,1,0:T(8,128)(2,1)S(1)} reshape(bf16[16,36864]{1,0:T(8,128)(2,1)} %param.11) | data formatting | bytes 2359296 | tf_op jit(solution)/shard_map/reshape | solution.py:316
  125.0 1.0 copy.19
  126.0 0.2 copy.20
  126.2 1.6 %collective-permute-done.6 = bf16[32,3584]{1,0:T(8,128)(2,1)} collective-permute-done((bf16[32,3584]{1,0:T(8,128)(2,1)S(1)}, bf16[32,3584]{1,0:T(8,128)(2,1)}, u32[]{:S(2)}, u32[]{:S(2)}) %collective-permute-start.6) | collective-permute-done | bytes 229408 | tf_op jit(solution)/shard_map/ppermute | solution.py:156
  127.8 1.0 slice_add_fusion.2
  128.9 9.0 %collective-permute-start.7 = (bf16[16,3584]{1,0:T(8,128)(2,1)S(1)}, bf16[16,3584]{1,0:T(8,128)(2,1)S(1)}, u32[]{:S(2)}, u32[]{:S(2)}) collective-permute-start(bf16[16,3584]{1,0:T(8,128)(2,1)S(1)} %slice.78), channel_id=1, source_target_pairs={{0,8},{1,9},{2,10},{3,11},{4,12},{5,13},{6,14},{7,15},{8,0},{9,1},... | collective-permute-start | bytes 344072 | tf_op jit(solution)/shard_map/ppermute | solution.py:156
  137.8 1.9 %fusion.21 = (bf16[4,256,640]{2,1,0:T(8,128)(2,1)S(1)}, bf16[4,256,640]{2,1,0:T(8,128)(2,1)}) fusion(bf16[4,256,576]{2,1,0:T(8,128)(2,1)S(1)} %copy.20), kind=kLoop, calls=%fused_computation.44 | loop fusion | bytes 3801088 | tf_op jit(solution)/shard_map/jit(_pad)/pad | solution.py:319
  139.7 2.3 %collective-permute-done.7 = bf16[16,3584]{1,0:T(8,128)(2,1)S(1)} collective-permute-done((bf16[16,3584]{1,0:T(8,128)(2,1)S(1)}, bf16[16,3584]{1,0:T(8,128)(2,1)S(1)}, u32[]{:S(2)}, u32[]{:S(2)}) %collective-permute-start.7) | collective-permute-done | bytes 114720 | tf_op jit(solution)/shard_map/ppermute | solution.py:156
  142.0 0.7 fusion.8
  142.7 1.3 copy-done.2
  144.0 9.0 %attend_pages.1 = bf16[16,32768]{1,0:T(8,128)(2,1)} custom-call(s32[64]{0:T(128)S(1)} %multiply_add_fusion.place_ref, s32[4]{0:T(128)S(1)} %broadcast_add_fusion.limit_ref, bf16[4,256,640]{2,1,0:T(8,128)(2,1)S(1)} %copy-done.2, bf16[4,256,640]{2,1,0:T(8,128)(2,1)S(1)} %get-tuple-element.2.high_ref, bf16[64,32,1152]{2,1,0:T(8,128)(2,1)} %bitcast.7.pages_ref), custom_call_target="tpu_custom_call" | custom-call | tf_op jit(solution)/shard_map/attend_pages/pallas_call | solution.py:238
  (38 shorter events, 0.3 us)
Async XLA Ops:
  0.6 74.6 %copy-start = (bf16[1,256,3584]{2,1,0:T(8,128)(2,1)S(1)}, bf16[1,256,3584]{2,1,0:T(8,128)(2,1)}, u32[]{:S(2)}) copy-start(bf16[1,256,3584]{2,1,0:T(8,128)(2,1)} %param.21) | copy-start | bytes 5505028
  2.6 8.0 %collective-permute-start = (bf16[16,3712]{1,0:T(8,128)(2,1)}, bf16[16,3712]{1,0:T(8,128)(2,1)S(1)}, u32[]{:S(2)}, u32[]{:S(2)}) collective-permute-start(bf16[16,3712]{1,0:T(8,128)(2,1)} %pack_rows.1), channel_id=1, source_target_pairs={{0,8},{1,9},{2,10},{3,11},{4,12},{5,13},{6,14},{7,15},{8,0},{9,1},... | collective-permute-start | bytes 356360 | tf_op jit(solution)/shard_map/ppermute | solution.py:156
  11.5 21.8 %collective-permute-start.1 = (bf16[32,3712]{1,0:T(8,128)(2,1)S(1)}, bf16[32,3712]{1,0:T(8,128)(2,1)S(1)}, u32[]{:S(2)}, u32[]{:S(2)}) collective-permute-start(bf16[32,3712]{1,0:T(8,128)(2,1)S(1)} %pad_maximum_fusion.2), channel_id=1, source_target_pairs={{0,4},{1,5},{2,6},{3,7},{4,0},{5,1},{6,2},{7,3},{8,12},{9,13},{10,... | collective-permute-start | bytes 712712 | tf_op jit(solution)/shard_map/ppermute | solution.py:156
  11.6 1.7 %copy-start.3 = (bf16[32,36864]{1,0:T(8,128)(2,1)S(1)}, bf16[32,36864]{1,0:T(8,128)(2,1)}, u32[]{:S(2)}) copy-start(bf16[32,36864]{1,0:T(8,128)(2,1)} %pool_ref.1) | copy-start | bytes 7077892
  13.2 0.7 copy-start.4
  13.9 0.7 copy-start.6
  23.4 2.2 %copy-start.1 = (bf16[64,32,1152]{2,1,0:T(8,128)(2,1)}, bf16[64,32,1152]{2,1,0:T(8,128)(2,1)S(1)}, u32[]{:S(2)}) copy-start(bf16[64,32,1152]{2,1,0:T(8,128)(2,1)S(1)} %stage_pages.1) | copy-start | bytes 14155780
  25.5 7.7 %copy-start.9 = (bf16[16,3712]{1,0:T(8,128)(2,1)S(1)}, bf16[16,3712]{1,0:T(8,128)(2,1)}, u32[]{:S(2)}) copy-start(bf16[16,3712]{1,0:T(8,128)(2,1)} %pack_rows.1) | copy-start | bytes 356356
  25.6 117.2 %all-to-all-start = ((bf16[16,4,32,1152]{3,2,1,0:T(8,128)(2,1)}), bf16[16,4,32,1152]{3,2,1,0:T(8,128)(2,1)}, u32[]{:S(2)}, u32[]{:S(2)}) async-start(bf16[16,4,32,1152]{3,2,1,0:T(8,128)(2,1)} %bitcast.23), calls=%async_computation | async-start | bytes 9437184 | tf_op jit(solution)/shard_map/all_to_all | solution.py:291
  33.4 36.6 %collective-permute-start.2 = (bf16[64,3712]{1,0:T(8,128)(2,1)S(1)}, bf16[64,3712]{1,0:T(8,128)(2,1)S(1)}, u32[]{:S(2)}, u32[]{:S(2)}) collective-permute-start(bf16[64,3712]{1,0:T(8,128)(2,1)S(1)} %pad_maximum_fusion.1), channel_id=1, source_target_pairs={{0,2},{1,3},{2,0},{3,1},{4,6},{5,7},{6,4},{7,5},{8,10},{9,11},{10,... | collective-permute-start | bytes 1425416 | tf_op jit(solution)/shard_map/ppermute | solution.py:156
  70.1 4.5 %copy-start.14 = (bf16[1,3584,256]{2,1,0:T(8,128)(2,1)S(1)}, bf16[1,3584,256]{2,1,0:T(8,128)(2,1)}, u32[]{:S(2)}) copy-start(bf16[1,3584,256]{2,1,0:T(8,128)(2,1)} %param.20) | copy-start | bytes 5505028
  70.1 3.1 %collective-permute-start.3 = (bf16[128,3712]{1,0:T(8,128)(2,1)S(1)}, bf16[128,3712]{1,0:T(8,128)(2,1)S(1)}, u32[]{:S(2)}, u32[]{:S(2)}) collective-permute-start(bf16[128,3712]{1,0:T(8,128)(2,1)S(1)} %pad_maximum_fusion), channel_id=1, source_target_pairs={{0,1},{1,0},{2,3},{3,2},{4,5},{5,4},{6,7},{7,6},{8,9},{9,8},{10,11... | collective-permute-start | bytes 2850824 | tf_op jit(solution)/shard_map/ppermute | solution.py:156
  73.3 1.2 copy-start.12
  75.2 8.1 %copy-start.7 = (s32[64]{0:T(128)S(1)}, s32[64]{0:T(128)}, u32[]{:S(2)}) copy-start(s32[64]{0:T(128)} %param.14) | copy-start | bytes 772
  75.2 8.2 %copy-start.15 = (s32[64]{0:T(128)S(1)}, s32[64]{0:T(128)}, u32[]{:S(2)}) copy-start(s32[64]{0:T(128)} %param.15) | copy-start | bytes 772
  82.9 2.7 %collective-permute-start.4 = (bf16[128,3584]{1,0:T(8,128)(2,1)S(1)}, bf16[128,3584]{1,0:T(8,128)(2,1)}, u32[]{:S(2)}, u32[]{:S(2)}) collective-permute-start(bf16[128,3584]{1,0:T(8,128)(2,1)S(1)} %slice.75), channel_id=1, source_target_pairs={{0,1},{1,0},{2,3},{3,2},{4,5},{5,4},{6,7},{7,6},{8,9},{9,8},{10,11... | collective-permute-start | bytes 2752520 | tf_op jit(solution)/shard_map/ppermute | solution.py:156
  83.7 5.2 %copy-start.5 = (s32[64,16]{0,1:T(8,128)S(1)}, s32[64,16]{0,1:T(8,128)}, u32[]{:S(2)}) copy-start(s32[64,16]{0,1:T(8,128)} %param.13) | copy-start | bytes 12292
  87.5 1.2 copy-start.8
  88.8 24.4 %collective-permute-start.5 = (bf16[64,3584]{1,0:T(8,128)(2,1)S(1)}, bf16[64,3584]{1,0:T(8,128)(2,1)S(1)}, u32[]{:S(2)}, u32[]{:S(2)}) collective-permute-start(bf16[64,3584]{1,0:T(8,128)(2,1)S(1)} %slice.76), channel_id=1, source_target_pairs={{0,2},{1,3},{2,0},{3,1},{4,6},{5,7},{6,4},{7,5},{8,10},{9,11},{10,... | collective-permute-start | bytes 1376264 | tf_op jit(solution)/shard_map/ppermute | solution.py:156
  114.5 7.7 %copy-start.10 = (f32[64,3584]{1,0:T(8,128)}, f32[64,3584]{1,0:T(8,128)S(1)}, u32[]{:S(2)}) copy-start(f32[64,3584]{1,0:T(8,128)S(1)} %slice_add_fusion.1) | copy-start | bytes 2752516
  114.5 13.3 %collective-permute-start.6 = (bf16[32,3584]{1,0:T(8,128)(2,1)S(1)}, bf16[32,3584]{1,0:T(8,128)(2,1)}, u32[]{:S(2)}, u32[]{:S(2)}) collective-permute-start(bf16[32,3584]{1,0:T(8,128)(2,1)S(1)} %slice.77), channel_id=1, source_target_pairs={{0,4},{1,5},{2,6},{3,7},{4,0},{5,1},{6,2},{7,3},{8,12},{9,13},{10,... | collective-permute-start | bytes 688136 | tf_op jit(solution)/shard_map/ppermute | solution.py:156
  126.0 1.8 %copy-start.11 = (f32[64,3584]{1,0:T(8,128)S(1)}, f32[64,3584]{1,0:T(8,128)}, u32[]{:S(2)}) copy-start(f32[64,3584]{1,0:T(8,128)} %copy-done.10) | copy-start | bytes 2752516
  128.9 13.2 %copy-start.13 = (bf16[16,3584]{1,0:T(8,128)(2,1)S(1)}, bf16[16,3584]{1,0:T(8,128)(2,1)}, u32[]{:S(2)}) copy-start(bf16[16,3584]{1,0:T(8,128)(2,1)} %rows_ref.1) | copy-start | bytes 344068
  128.9 13.2 %collective-permute-start.7 = (bf16[16,3584]{1,0:T(8,128)(2,1)S(1)}, bf16[16,3584]{1,0:T(8,128)(2,1)S(1)}, u32[]{:S(2)}, u32[]{:S(2)}) collective-permute-start(bf16[16,3584]{1,0:T(8,128)(2,1)S(1)} %slice.78), channel_id=1, source_target_pairs={{0,8},{1,9},{2,10},{3,11},{4,12},{5,13},{6,14},{7,15},{8,0},{9,1},... | collective-permute-start | bytes 344072 | tf_op jit(solution)/shard_map/ppermute | solution.py:156
  142.7 1.3 copy-start.2

commit v3 on v2

--- a/solution.py
+++ b/solution.py
@@ -111,7 +111,7 @@
             pltpu.SemaphoreType.DMA,
             pltpu.SemaphoreType.DMA((slots,)),
         ],
-        compiler_params=pltpu.CompilerParams(vmem_limit_bytes=32 << 20),
+        compiler_params=pltpu.CompilerParams(vmem_limit_bytes=56 << 20),
         name="stage_pages",
     )(device, table, serving, pool)
 
@@ -156,8 +156,7 @@
     return lax.ppermute(block, group, [(d, d ^ bit) for d in range(peers)])
 
 
-def spread(block, group):
-    bit = lax.axis_size(group) // 2
+def spread(block, group, bit):
     while bit:
         block = jnp.concatenate([block, exchange(block, group, bit)], axis=0)
         bit //= 2
@@ -166,24 +165,36 @@
 
 def collect(total, group):
     bit = 1
-    while bit < lax.axis_size(group):
+    while True:
         half = total.shape[0] // 2
         sent = exchange(total[half:].astype(jnp.bfloat16), group, bit)
+        bit *= 2
+        if bit == lax.axis_size(group):
+            return total[:half], sent
         total = total[:half] + sent.astype(jnp.float32)
-        bit *= 2
-    return total
-
-
-def attend_body(place_ref, limit_ref, low_ref, high_ref, pages_ref, out_ref, context, held, sems):
+
+
+def attend_body(
+    place_ref, limit_ref, low_hbm, high_hbm, pages_ref, out_ref, context, held, low_ref, high_ref, *sems
+):
     requests, each, pairs, width = context.shape
     rows = low_ref.shape[1]
+    page_sems, low_sems, high_sems = sems
 
     def copy(r, i):
         return pltpu.make_async_copy(
-            pages_ref.at[place_ref[r * each + i]], context.at[r, i], sems.at[r, i]
+            pages_ref.at[place_ref[r * each + i]], context.at[r, i], page_sems.at[r, i]
+        )
+
+    def copy_queries(r):
+        return (
+            pltpu.make_async_copy(low_hbm.at[r], low_ref.at[r], low_sems.at[r]),
+            pltpu.make_async_copy(high_hbm.at[r], high_ref.at[r], high_sems.at[r]),
         )
 
     for r in range(requests):
+        for query_copy in copy_queries(r):
+            query_copy.start()
 
         def begin(i, carry, r=r):
             copy(r, i).start()
@@ -202,6 +213,8 @@
             copy(r, i).wait()
             return carry
 
+        for query_copy in copy_queries(r):
+            query_copy.wait()
         lax.fori_loop(0, each, finish, 0)
         block = context[r].reshape(columns, width)
         even = lax.dot_general(
@@ -241,17 +254,21 @@
         in_specs=[
             pl.BlockSpec(memory_space=pltpu.SMEM),
             pl.BlockSpec(memory_space=pltpu.SMEM),
-            pl.BlockSpec(memory_space=pltpu.VMEM),
-            pl.BlockSpec(memory_space=pltpu.VMEM),
+            pl.BlockSpec(memory_space=pltpu.HBM),
+            pl.BlockSpec(memory_space=pltpu.HBM),
             pl.BlockSpec(memory_space=pltpu.HBM),
         ],
         out_specs=pl.BlockSpec(memory_space=pltpu.VMEM),
         scratch_shapes=[
             pltpu.VMEM((requests, each, pairs, width), pages.dtype),
             pltpu.VMEM(out, jnp.float32),
+            pltpu.VMEM(low.shape, low.dtype),
+            pltpu.VMEM(high.shape, high.dtype),
             pltpu.SemaphoreType.DMA((requests, each)),
+            pltpu.SemaphoreType.DMA((requests,)),
+            pltpu.SemaphoreType.DMA((requests,)),
         ],
-        compiler_params=pltpu.CompilerParams(vmem_limit_bytes=48 << 20),
+        compiler_params=pltpu.CompilerParams(vmem_limit_bytes=56 << 20),
         name="attend_pages",
     )(place, limits, low, high, pages)
 
@@ -282,16 +299,20 @@
 
     n_ep = lax.axis_size("ep")
     experts = n_ep // 2
-    everyone = spread(pack_rows(routes.T, route_scores.T, residual, experts), group)
+    packed = pack_rows(routes.T, route_scores.T, residual, experts)
+    far, near = peers // 2, peers // 4
+    across = [exchange(packed, group, bit) for bit in (far, near, far | near)]
 
     outgoing = stage_pages(
         device.reshape(1), page_table.T, serving.reshape(1, -1), page_pool, peers, listed
     )
+    packed, across, outgoing = lax.optimization_barrier((packed, across, outgoing))
     pairs = outgoing.shape[1]
     arrived = lax.all_to_all(
         outgoing.reshape(peers, fetched, pairs, 2 * LAT), group, split_axis=0, concat_axis=0, tiled=True
     )
 
+    everyone = spread(jnp.concatenate([packed, *across], axis=0), group, near // 2)
     rows = everyone[:, :width]
     parts = everyone[:, width : width + 3 * experts].astype(jnp.float32)
     expert = lax.axis_index("ep") // 2
@@ -301,8 +322,7 @@
     upward = jnp.dot(rows, w_up[0], preferred_element_type=jnp.float32)
     hidden = (jax.nn.silu(gate) * upward).astype(jnp.bfloat16)
     partial_out = jnp.dot(hidden, w_down[0], preferred_element_type=jnp.float32) * weight
-    mixed = collect(partial_out, group)
-    moe_out = (residual.astype(jnp.float32) + mixed).astype(jnp.bfloat16)
+    mixed, last = collect(partial_out, group)
 
     served = lax.dynamic_slice_in_dim(serving, device * requests_dev, requests_dev)
     slots = jnp.arange(n_requests, dtype=jnp.int32)
@@ -320,6 +340,8 @@
     latent_out = attend(
         place, limits, low, high, arrived.reshape(listed, pairs, 2 * LAT), pages_each
     )
+    latent_out, last = lax.optimization_barrier((latent_out, last))
+    moe_out = (residual.astype(jnp.float32) + mixed + last.astype(jnp.float32)).astype(jnp.bfloat16)
     return (latent_out, moe_out)
 
 

time: 156 us -> 141 us (0.904); the launches traced: 153 us -> 140 us
  starting transfers between devices: 28.5 us -> 13.8 us
  waiting for transfers between devices: 74 us -> 78.7 us
  local copies, waits for them, and re-layouts: 16.7 us -> 14 us
  Pallas kernels: 19.7 us -> 17.2 us
    all_to_all x1, waiting for transfers between devices: 0.01 us -> 20.1 us  [local(): lax.all_to_all(outgoing.reshape(peers, fetched, pairs, 2 * LAT), group, s...]
    ppermute x8 -> x9, waiting for transfers between devices: 74 us -> 58.6 us  [exchange(): return lax.ppermute(block, group, [(d, d ^ bit) for d in range(peers)])]
    ppermute x8 -> x9, starting transfers between devices: 20.7 us -> 7.27 us  [exchange(): return lax.ppermute(block, group, [(d, d ^ bit) for d in range(peers)])]
    unnamed x36 -> x24, local copies, waits for them, and re-layouts: 8.99 us -> 4.09 us
    pallas_call x1, Pallas kernels: 8.76 us -> 5.77 us  [stage_pages(): pl.pallas_call(functools.partial(stage_body, peers), out_shape=jax.ShapeD...]
    concatenate x1 -> x2, local copies, waits for them, and re-layouts: 0.11 us -> 2.02 us  [spread(): block = jnp.concatenate([block, exchange(block, group, bit)], axis=0)]
  transfers between devices with their start and end apart: 9 -> 10, of which waited for: 7 -> 8; matrix products, arithmetic and copies ran while one was open for 13% -> 19% of each run, Pallas kernels for 6% -> 11%
where the time goes in v3:
time: 141 us; the launch traced here: 140 us
  waiting for transfers between devices  78.7 us (56%)
  Pallas kernels  17.2 us (12%)
  local copies, waits for them, and re-layouts  14 us (10%)
  starting transfers between devices  13.8 us (10%)
  matrix products  8.2 us (6%)
  other arithmetic  7.53 us (5%)
    ppermute x9, waiting for transfers between devices, exchange(): return lax.ppermute(block, group, [(d, d ^ bit) for d in range(peers)])  58.6 us
    all_to_all x1, waiting for transfers between devices, local(): lax.all_to_all(outgoing.reshape(peers, fetched, pairs, 2 * LAT), group, s...  20.1 us
    pallas_call x1, Pallas kernels, attend(): pl.pallas_call(attend_body, out_shape=jax.ShapeDtypeStruct(out, jnp.bfloa...  9.55 us
    ppermute x9, starting transfers between devices, exchange(): return lax.ppermute(block, group, [(d, d ^ bit) for d in range(peers)])  7.27 us
    all_to_all x1, starting transfers between devices, local(): lax.all_to_all(outgoing.reshape(peers, fetched, pairs, 2 * LAT), group, s...  6.5 us
    dot_general x1, matrix products, local(): jnp.dot(hidden, w_down[0], preferred_element_type=jnp.float32) * weight  6.06 us
    pallas_call x1, Pallas kernels, stage_pages(): pl.pallas_call(functools.partial(stage_body, peers), out_shape=jax.ShapeD...  5.77 us
    add x3, other arithmetic, collect(): total = total[:half] + sent.astype(jnp.float32)  4.15 us
  transfers between devices with their start and end apart: 10, of which 8 were waited for; matrix products, arithmetic and copies ran while one was open for 19% of the time, Pallas kernels for 11%

profile of v3, /device:TPU:15, one launch (start us, length us, event | category | flops | bytes accessed | tf_op | source)
XLA Modules:
  0.0 140.3 jit_solution(6034205099871792075)
XLA Ops:
  0.6 1.9 %pack_rows.1 = bf16[16,3712]{1,0:T(8,128)(2,1)} custom-call(s32[2,16]{1,0:T(2,128)} %bitcast.26, f32[2,16]{1,0:T(2,128)} %bitcast.27, bf16[16,3584]{1,0:T(8,128)(2,1)} %rows_ref.1), custom_call_target="tpu_custom_call" | custom-call | tf_op jit(solution)/shard_map/pack_rows/pallas_call | solution.py:147
  2.6 2.3 %collective-permute-start = (bf16[16,3712]{1,0:T(8,128)(2,1)}, bf16[16,3712]{1,0:T(8,128)(2,1)S(1)}, u32[]{:S(2)}, u32[]{:S(2)}) collective-permute-start(bf16[16,3712]{1,0:T(8,128)(2,1)} %pack_rows.1), channel_id=1, source_target_pairs={{0,8},{1,9},{2,10},{3,11},{4,12},{5,13},{6,14},{7,15},{8,0},{9,1},... | collective-permute-start | bytes 356360 | tf_op jit(solution)/shard_map/ppermute | solution.py:156
  4.9 0.2 collective-permute-start.1
  5.0 0.2 collective-permute-start.2
  5.2 5.8 %stage_pages.1 = bf16[64,32,1152]{2,1,0:T(8,128)(2,1)} custom-call(s32[1]{0:T(128)} %bitcast.5.device_ref, s32[16,64]{1,0:T(8,128)} %bitcast.25, s32[1,64]{1,0:T(1,128)} %bitcast.28, bf16[32,36864]{1,0:T(8,128)(2,1)} %pool_ref.1), custom_call_target="tpu_custom_call" | custom-call | tf_op jit(solution)/shard_map/stage_pages/pallas_call | solution.py:95
  11.0 0.1 collective-permute-done
  11.1 4.5 %collective-permute-done.2 = bf16[16,3712]{1,0:T(8,128)(2,1)S(1)} collective-permute-done((bf16[16,3712]{1,0:T(8,128)(2,1)}, bf16[16,3712]{1,0:T(8,128)(2,1)S(1)}, u32[]{:S(2)}, u32[]{:S(2)}) %collective-permute-start.2) | collective-permute-done | bytes 118816 | tf_op jit(solution)/shard_map/ppermute | solution.py:156
  15.7 0.7 constant_dynamic-update-slice_fusion.4
  16.4 0.3 collective-permute-start.3
  16.7 6.5 %all-to-all-start = ((bf16[16,4,32,1152]{3,2,1,0:T(8,128)(2,1)}), bf16[16,4,32,1152]{3,2,1,0:T(8,128)(2,1)}, u32[]{:S(2)}, u32[]{:S(2)}) async-start(bf16[16,4,32,1152]{3,2,1,0:T(8,128)(2,1)} %bitcast.23), calls=%async_computation | async-start | bytes 9437184 | tf_op jit(solution)/shard_map/all_to_all | solution.py:311
  23.2 0.7 constant_dynamic-update-slice_fusion.3
  23.9 0.7 constant_dynamic-update-slice_fusion.2
  24.6 0.7 constant_dynamic-update-slice_fusion.1
  25.3 3.2 %collective-permute-done.3 = bf16[64,3712]{1,0:T(8,128)(2,1)S(1)} collective-permute-done((bf16[64,3712]{1,0:T(8,128)(2,1)S(1)}, bf16[64,3712]{1,0:T(8,128)(2,1)S(1)}, u32[]{:S(2)}, u32[]{:S(2)}) %collective-permute-start.3) | collective-permute-done | bytes 475168 | tf_op jit(solution)/shard_map/ppermute | solution.py:156
  28.5 1.0 constant_dynamic-update-slice_fusion
  29.5 2.2 %collective-permute-start.4 = (bf16[128,3712]{1,0:T(8,128)(2,1)}, bf16[128,3712]{1,0:T(8,128)(2,1)S(1)}, u32[]{:S(2)}, u32[]{:S(2)}) collective-permute-start(bf16[128,3712]{1,0:T(8,128)(2,1)} %get-tuple-element.18), channel_id=1, source_target_pairs={{0,1},{1,0},{2,3},{3,2},{4,5},{5,4},{6,7},{7,6},{8,9},{9,8},{10,11... | collective-permute-start | bytes 2850824 | tf_op jit(solution)/shard_map/ppermute | solution.py:156
  31.7 2.3 %collective-permute-done.4 = bf16[128,3712]{1,0:T(8,128)(2,1)S(1)} collective-permute-done((bf16[128,3712]{1,0:T(8,128)(2,1)}, bf16[128,3712]{1,0:T(8,128)(2,1)S(1)}, u32[]{:S(2)}, u32[]{:S(2)}) %collective-permute-start.4) | collective-permute-done | bytes 950304 | tf_op jit(solution)/shard_map/ppermute | solution.py:156
  34.1 1.0 constant_dynamic-update-slice_fusion.5
  35.1 0.9 select_reduce_fusion
  36.0 2.1 %fusion.1 = f32[256,256]{1,0:T(8,128)S(1)} fusion(bf16[1,3584,256]{2,1,0:T(8,128)(2,1)S(1)} %copy-done.8, bf16[256,3712]{1,0:T(8,128)(2,1)} %constant_dynamic-update-slice_fusion.5), kind=kOutput, calls=%fused_computation.4 | convolution fusion | flops 469762048 | bytes 3932160 | tf_op jit(solution)/shard_map/dot_general | solution.py:322
  38.2 6.1 %convolution_multiply_fusion = f32[256,3584]{1,0:T(8,128)} fusion(bf16[1,256,3584]{2,1,0:T(8,128)(2,1)S(1)} %copy-done, f32[256]{0:T(256)S(1)} %select_reduce_fusion, f32[256,256]{1,0:T(8,128)S(1)} %fusion.1, bf16[1,3584,256]{2,1,0:T(8,128)(2,1)} %param.19, bf16[256,3712]{1,0:T(8,128)(2,1)} %constant_dynamic-update-slice_fusion.5), kind=kOutput, calls=%fused_computation | convolution fusion | flops 940834816 | bytes 9438208 | tf_op jit(solution)/shard_map/dot_general | solution.py:324
  44.3 1.6 %slice.75 = bf16[128,3584]{1,0:T(8,128)(2,1)S(1)} slice(f32[256,3584]{1,0:T(8,128)} %convolution_multiply_fusion), slice={[128:256], [0:3584]} | slice | bytes 1835008 | tf_op jit(solution)/shard_map/slice | solution.py:170
  45.9 0.4 collective-permute-start.5
  46.3 0.1 dynamic_slice.3
  46.4 0.2 select_reduce_fusion.2
  46.6 0.1 iota_compare_fusion.1
  46.7 1.9 %collective-permute-done.5 = bf16[128,3584]{1,0:T(8,128)(2,1)} collective-permute-done((bf16[128,3584]{1,0:T(8,128)(2,1)S(1)}, bf16[128,3584]{1,0:T(8,128)(2,1)}, u32[]{:S(2)}, u32[]{:S(2)}) %collective-permute-start.5) | collective-permute-done | bytes 917536 | tf_op jit(solution)/shard_map/ppermute | solution.py:156
  48.6 1.9 %slice_add_fusion = f32[128,3584]{1,0:T(8,128)S(1)} fusion(f32[256,3584]{1,0:T(8,128)} %convolution_multiply_fusion, bf16[128,3584]{1,0:T(8,128)(2,1)} %collective-permute-done.5), kind=kLoop, calls=%fused_computation.2 | loop fusion | flops 917504 | bytes 4587520 | tf_op jit(solution)/shard_map/add | solution.py:174
  50.5 1.2 copy-done.1
  51.7 0.3 collective-permute-start.6
  52.0 0.1 select_reduce_fusion.1
  52.2 0.1 reshape.115
  52.3 0.6 broadcast_add_fusion.limit_ref
  52.9 16.1 %collective-permute-done.6 = bf16[64,3584]{1,0:T(8,128)(2,1)S(1)} collective-permute-done((bf16[64,3584]{1,0:T(8,128)(2,1)S(1)}, bf16[64,3584]{1,0:T(8,128)(2,1)S(1)}, u32[]{:S(2)}, u32[]{:S(2)}) %collective-permute-start.6) | collective-permute-done | bytes 458784 | tf_op jit(solution)/shard_map/ppermute | solution.py:156
  68.9 1.3 slice_add_fusion.1
  70.2 1.3 collective-permute-start.7
  71.6 0.2 convert_reduce_fusion
  71.7 2.7 %reshape.116 = bf16[4,4,64,576]{3,2,1,0:T(8,128)(2,1)S(1)} reshape(bf16[16,36864]{1,0:T(8,128)(2,1)} %param.11) | data formatting | bytes 2359296 | tf_op jit(solution)/shard_map/reshape | solution.py:336
  74.4 1.0 copy.19
  75.4 0.2 copy.20
  75.6 0.5 multiply_add_fusion.place_ref
  76.1 30.4 %collective-permute-done.7 = bf16[32,3584]{1,0:T(8,128)(2,1)} collective-permute-done((bf16[32,3584]{1,0:T(8,128)(2,1)S(1)}, bf16[32,3584]{1,0:T(8,128)(2,1)}, u32[]{:S(2)}, u32[]{:S(2)}) %collective-permute-start.7) | collective-permute-done | bytes 229408 | tf_op jit(solution)/shard_map/ppermute | solution.py:156
  106.6 1.0 slice_add_fusion.2
  107.6 0.1 collective-permute-start.8
  107.7 2.2 %fusion.21 = (bf16[4,256,640]{2,1,0:T(8,128)(2,1)}, bf16[4,256,640]{2,1,0:T(8,128)(2,1)}) fusion(bf16[4,256,576]{2,1,0:T(8,128)(2,1)S(1)} %copy.20), kind=kLoop, calls=%fused_computation.48 | loop fusion | bytes 3801088 | tf_op jit(solution)/shard_map/jit(_pad)/pad | solution.py:339
  109.9 20.1 %all-to-all-done = bf16[16,4,32,1152]{3,2,1,0:T(8,128)(2,1)} async-done(((bf16[16,4,32,1152]{3,2,1,0:T(8,128)(2,1)}), bf16[16,4,32,1152]{3,2,1,0:T(8,128)(2,1)}, u32[]{:S(2)}, u32[]{:S(2)}) %all-to-all-start) | async-done | bytes 4718624 | tf_op jit(solution)/shard_map/all_to_all | solution.py:311
  130.0 9.6 %attend_pages.1 = bf16[16,32768]{1,0:T(8,128)(2,1)} custom-call(s32[64]{0:T(128)} %multiply_add_fusion.place_ref, s32[4]{0:T(128)} %broadcast_add_fusion.limit_ref, bf16[4,256,640]{2,1,0:T(8,128)(2,1)} %get-tuple-element.17.low_hbm, bf16[4,256,640]{2,1,0:T(8,128)(2,1)} %get-tuple-element.16.high_hbm, bf16[64,32,1152]{2,1,0:T(8,128)(2,1)} %bitcast.9.pages_ref), custom_call_target="tpu_custom_call" | custom-call | tf_op jit(solution)/shard_map/attend_pages/pallas_call | solution.py:251
  139.6 0.7 fusion.8
  (27 shorter events, 0.2 us)
Async XLA Ops:
  0.6 37.6 %copy-start = (bf16[1,256,3584]{2,1,0:T(8,128)(2,1)S(1)}, bf16[1,256,3584]{2,1,0:T(8,128)(2,1)}, u32[]{:S(2)}) copy-start(bf16[1,256,3584]{2,1,0:T(8,128)(2,1)} %param.21) | copy-start | bytes 5505028
  2.6 8.6 %collective-permute-start = (bf16[16,3712]{1,0:T(8,128)(2,1)}, bf16[16,3712]{1,0:T(8,128)(2,1)S(1)}, u32[]{:S(2)}, u32[]{:S(2)}) collective-permute-start(bf16[16,3712]{1,0:T(8,128)(2,1)} %pack_rows.1), channel_id=1, source_target_pairs={{0,8},{1,9},{2,10},{3,11},{4,12},{5,13},{6,14},{7,15},{8,0},{9,1},... | collective-permute-start | bytes 356360 | tf_op jit(solution)/shard_map/ppermute | solution.py:156
  4.9 6.3 %collective-permute-start.1 = (bf16[16,3712]{1,0:T(8,128)(2,1)}, bf16[16,3712]{1,0:T(8,128)(2,1)S(1)}, u32[]{:S(2)}, u32[]{:S(2)}) collective-permute-start(bf16[16,3712]{1,0:T(8,128)(2,1)} %pack_rows.1), channel_id=1, source_target_pairs={{0,4},{1,5},{2,6},{3,7},{4,0},{5,1},{6,2},{7,3},{8,12},{9,13},{10,... | collective-permute-start | bytes 356360 | tf_op jit(solution)/shard_map/ppermute | solution.py:156
  5.0 10.6 %collective-permute-start.2 = (bf16[16,3712]{1,0:T(8,128)(2,1)}, bf16[16,3712]{1,0:T(8,128)(2,1)S(1)}, u32[]{:S(2)}, u32[]{:S(2)}) collective-permute-start(bf16[16,3712]{1,0:T(8,128)(2,1)} %pack_rows.1), channel_id=1, source_target_pairs={{0,12},{1,13},{2,14},{3,15},{4,8},{5,9},{6,10},{7,11},{8,4},{9,5},... | collective-permute-start | bytes 356360 | tf_op jit(solution)/shard_map/ppermute | solution.py:156
  5.2 10.5 %copy-start.4 = (bf16[16,3712]{1,0:T(8,128)(2,1)S(1)}, bf16[16,3712]{1,0:T(8,128)(2,1)}, u32[]{:S(2)}) copy-start(bf16[16,3712]{1,0:T(8,128)(2,1)} %pack_rows.1) | copy-start | bytes 356356
  16.4 12.1 %collective-permute-start.3 = (bf16[64,3712]{1,0:T(8,128)(2,1)S(1)}, bf16[64,3712]{1,0:T(8,128)(2,1)S(1)}, u32[]{:S(2)}, u32[]{:S(2)}) collective-permute-start(bf16[64,3712]{1,0:T(8,128)(2,1)S(1)} %pad_maximum_fusion), channel_id=1, source_target_pairs={{0,2},{1,3},{2,0},{3,1},{4,6},{5,7},{6,4},{7,5},{8,10},{9,11},{10,... | collective-permute-start | bytes 1425416 | tf_op jit(solution)/shard_map/ppermute | solution.py:156
  16.7 113.3 %all-to-all-start = ((bf16[16,4,32,1152]{3,2,1,0:T(8,128)(2,1)}), bf16[16,4,32,1152]{3,2,1,0:T(8,128)(2,1)}, u32[]{:S(2)}, u32[]{:S(2)}) async-start(bf16[16,4,32,1152]{3,2,1,0:T(8,128)(2,1)} %bitcast.23), calls=%async_computation | async-start | bytes 9437184 | tf_op jit(solution)/shard_map/all_to_all | solution.py:311
  29.5 4.5 %collective-permute-start.4 = (bf16[128,3712]{1,0:T(8,128)(2,1)}, bf16[128,3712]{1,0:T(8,128)(2,1)S(1)}, u32[]{:S(2)}, u32[]{:S(2)}) collective-permute-start(bf16[128,3712]{1,0:T(8,128)(2,1)} %get-tuple-element.18), channel_id=1, source_target_pairs={{0,1},{1,0},{2,3},{3,2},{4,5},{5,4},{6,7},{7,6},{8,9},{9,8},{10,11... | collective-permute-start | bytes 2850824 | tf_op jit(solution)/shard_map/ppermute | solution.py:156
  31.7 4.3 %copy-start.8 = (bf16[1,3584,256]{2,1,0:T(8,128)(2,1)S(1)}, bf16[1,3584,256]{2,1,0:T(8,128)(2,1)}, u32[]{:S(2)}) copy-start(bf16[1,3584,256]{2,1,0:T(8,128)(2,1)} %param.20) | copy-start | bytes 5505028
  38.2 8.1 %copy-start.7 = (s32[64]{0:T(128)S(1)}, s32[64]{0:T(128)}, u32[]{:S(2)}) copy-start(s32[64]{0:T(128)} %param.14) | copy-start | bytes 772
  38.2 8.2 %copy-start.9 = (s32[64]{0:T(128)S(1)}, s32[64]{0:T(128)}, u32[]{:S(2)}) copy-start(s32[64]{0:T(128)} %param.15) | copy-start | bytes 772
  45.9 2.7 %collective-permute-start.5 = (bf16[128,3584]{1,0:T(8,128)(2,1)S(1)}, bf16[128,3584]{1,0:T(8,128)(2,1)}, u32[]{:S(2)}, u32[]{:S(2)}) collective-permute-start(bf16[128,3584]{1,0:T(8,128)(2,1)S(1)} %slice.75), channel_id=1, source_target_pairs={{0,1},{1,0},{2,3},{3,2},{4,5},{5,4},{6,7},{7,6},{8,9},{9,8},{10,11... | collective-permute-start | bytes 2752520 | tf_op jit(solution)/shard_map/ppermute | solution.py:156
  46.7 5.4 %copy-start.6 = (s32[64,16]{0,1:T(8,128)S(1)}, s32[64,16]{0,1:T(8,128)}, u32[]{:S(2)}) copy-start(s32[64,16]{0,1:T(8,128)} %param.13) | copy-start | bytes 12292
  50.5 1.2 copy-start.1
  51.7 17.2 %collective-permute-start.6 = (bf16[64,3584]{1,0:T(8,128)(2,1)S(1)}, bf16[64,3584]{1,0:T(8,128)(2,1)S(1)}, u32[]{:S(2)}, u32[]{:S(2)}) collective-permute-start(bf16[64,3584]{1,0:T(8,128)(2,1)S(1)} %slice.76), channel_id=1, source_target_pairs={{0,2},{1,3},{2,0},{3,1},{4,6},{5,7},{6,4},{7,5},{8,10},{9,11},{10,... | collective-permute-start | bytes 1376264 | tf_op jit(solution)/shard_map/ppermute | solution.py:156
  70.2 1.4 copy-start.2
  70.2 36.3 %collective-permute-start.7 = (bf16[32,3584]{1,0:T(8,128)(2,1)S(1)}, bf16[32,3584]{1,0:T(8,128)(2,1)}, u32[]{:S(2)}, u32[]{:S(2)}) collective-permute-start(bf16[32,3584]{1,0:T(8,128)(2,1)S(1)} %slice.77), channel_id=1, source_target_pairs={{0,4},{1,5},{2,6},{3,7},{4,0},{5,1},{6,2},{7,3},{8,12},{9,13},{10,... | collective-permute-start | bytes 688136 | tf_op jit(solution)/shard_map/ppermute | solution.py:156
  75.4 31.1 %copy-start.3 = (f32[64,3584]{1,0:T(8,128)S(1)}, f32[64,3584]{1,0:T(8,128)}, u32[]{:S(2)}) copy-start(f32[64,3584]{1,0:T(8,128)} %copy-done.2) | copy-start | bytes 2752516
  107.6 32.0 %collective-permute-start.8 = (bf16[16,3584]{1,0:T(8,128)(2,1)S(1)}, bf16[16,3584]{1,0:T(8,128)(2,1)S(1)}, u32[]{:S(2)}, u32[]{:S(2)}) collective-permute-start(bf16[16,3584]{1,0:T(8,128)(2,1)S(1)} %slice.78), channel_id=1, source_target_pairs={{0,8},{1,9},{2,10},{3,11},{4,12},{5,13},{6,14},{7,15},{8,0},{9,1},... | collective-permute-start | bytes 344072 | tf_op jit(solution)/shard_map/ppermute | solution.py:156
  130.0 9.6 %copy-start.5 = (bf16[16,3584]{1,0:T(8,128)(2,1)S(1)}, bf16[16,3584]{1,0:T(8,128)(2,1)}, u32[]{:S(2)}) copy-start(bf16[16,3584]{1,0:T(8,128)(2,1)} %rows_ref.1) | copy-start | bytes 344068

commit v4 on v2

--- a/solution.py
+++ b/solution.py
@@ -1,4 +1,5 @@
 import functools
+import math
 
 import jax
 import jax.numpy as jnp
@@ -14,7 +15,7 @@
 HALF = 640
 SHIFT = HALF - LAT
 
-score_scale = 192.0 ** (-0.5)
+exponent_scale = 192.0 ** (-0.5) * math.log2(math.e)
 masked_score = -1e30
 
 
@@ -111,7 +112,7 @@
             pltpu.SemaphoreType.DMA,
             pltpu.SemaphoreType.DMA((slots,)),
         ],
-        compiler_params=pltpu.CompilerParams(vmem_limit_bytes=32 << 20),
+        compiler_params=pltpu.CompilerParams(vmem_limit_bytes=56 << 20),
         name="stage_pages",
     )(device, table, serving, pool)
 
@@ -156,74 +157,125 @@
     return lax.ppermute(block, group, [(d, d ^ bit) for d in range(peers)])
 
 
-def spread(block, group):
-    bit = lax.axis_size(group) // 2
-    while bit:
-        block = jnp.concatenate([block, exchange(block, group, bit)], axis=0)
-        bit //= 2
-    return block
-
-
-def collect(total, group):
-    bit = 1
-    while bit < lax.axis_size(group):
-        half = total.shape[0] // 2
-        sent = exchange(total[half:].astype(jnp.bfloat16), group, bit)
-        total = total[:half] + sent.astype(jnp.float32)
-        bit *= 2
-    return total
-
-
-def attend_body(place_ref, limit_ref, low_ref, high_ref, pages_ref, out_ref, context, held, sems):
+def expert_body(experts, label_ref, kept_ref, other_ref, *refs):
+    gate_hbm, up_hbm, down_hbm, kept_out, other_out, gate_ref, up_ref, down_ref, sems = refs
+    copies = [
+        pltpu.make_async_copy(gate_hbm, gate_ref, sems.at[0]),
+        pltpu.make_async_copy(up_hbm, up_ref, sems.at[1]),
+        pltpu.make_async_copy(down_hbm, down_ref, sems.at[2]),
+    ]
+    for weight_copy in copies:
+        weight_copy.start()
+    width = gate_ref.shape[0]
+    parts = []
+    copies[0].wait()
+    for rows_ref in (other_ref, kept_ref):
+        parts.append(jnp.dot(rows_ref[:, :width], gate_ref[...], preferred_element_type=jnp.float32))
+    copies[1].wait()
+    hiddens = []
+    for rows_ref, gate in zip((other_ref, kept_ref), parts):
+        upward = jnp.dot(rows_ref[:, :width], up_ref[...], preferred_element_type=jnp.float32)
+        hiddens.append((gate / (1.0 + jnp.exp(-gate)) * upward).astype(jnp.bfloat16))
+    copies[2].wait()
+    for rows_ref, hidden, out_ref in zip((other_ref, kept_ref), hiddens, (other_out, kept_out)):
+        side = rows_ref[:, width:].astype(jnp.float32)
+        line = lax.broadcasted_iota(jnp.int32, side.shape, 1)
+        mine = (line == label_ref[0]) | (line == label_ref[0] + experts)
+        mine = mine | (line == label_ref[0] + 2 * experts)
+        weight = jnp.sum(jnp.where(mine, side, 0.0), axis=1, keepdims=True)
+        total = jnp.dot(hidden, down_ref[...], preferred_element_type=jnp.float32) * weight
+        out_ref[...] = total.astype(out_ref.dtype)
+
+
+def expert_rows(label, kept, other, gate, up, down, experts):
+    return pl.pallas_call(
+        functools.partial(expert_body, experts),
+        out_shape=(
+            jax.ShapeDtypeStruct((kept.shape[0], gate.shape[0]), jnp.float32),
+            jax.ShapeDtypeStruct((other.shape[0], gate.shape[0]), jnp.bfloat16),
+        ),
+        in_specs=[pl.BlockSpec(memory_space=pltpu.SMEM)]
+        + [pl.BlockSpec(memory_space=pltpu.VMEM)] * 2
+        + [pl.BlockSpec(memory_space=pltpu.HBM)] * 3,
+        scratch_shapes=[
+            pltpu.VMEM(gate.shape, gate.dtype),
+            pltpu.VMEM(up.shape, up.dtype),
+            pltpu.VMEM(down.shape, down.dtype),
+            pltpu.SemaphoreType.DMA((3,)),
+        ],
+        compiler_params=pltpu.CompilerParams(vmem_limit_bytes=56 << 20),
+        cost_estimate=pl.CostEstimate(flops=0, bytes_accessed=0, transcendentals=0),
+        name="expert_rows",
+    )(label, kept, other, gate, up, down)
+
+
+def attend_body(plan_ref, query_ref, pages_ref, out_ref, context, held, sems):
     requests, each, pairs, width = context.shape
-    rows = low_ref.shape[1]
+    rows = query_ref.shape[1]
+    contract = (((1,), (1,)), ((), ()))
 
     def copy(r, i):
         return pltpu.make_async_copy(
-            pages_ref.at[place_ref[r * each + i]], context.at[r, i], sems.at[r, i]
-        )
-
+            pages_ref.at[plan_ref[2 * requests + r * each + i]], context.at[r, i], sems.at[r * each + i]
+        )
+
+    blank = jnp.zeros((pairs, width), context.dtype)
     for r in range(requests):
 
         def begin(i, carry, r=r):
             copy(r, i).start()
             return carry
 
-        lax.fori_loop(0, each, begin, 0)
+        lax.fori_loop(0, plan_ref[r], begin, 0)
+    for r in range(requests):
+
+        def clear(i, carry, r=r):
+            context[r, i] = blank
+            return carry
+
+        lax.fori_loop(plan_ref[r], each, clear, 0)
 
     columns = each * pairs
-    position = 2 * lax.broadcasted_iota(jnp.int32, (rows, columns), 1)
     draft = lax.broadcasted_iota(jnp.int32, (rows, columns), 0) % DRAFT
-    early = position - draft
-    contract = (((1,), (1,)), ((), ()))
-    for r in range(requests):
-
-        def finish(i, carry, r=r):
+    early = 2 * lax.broadcasted_iota(jnp.int32, (rows, columns), 1) - draft
+
+    def score(r):
+        def finish(i, carry):
             copy(r, i).wait()
             return carry
 
-        lax.fori_loop(0, each, finish, 0)
+        lax.fori_loop(0, plan_ref[r], finish, 0)
         block = context[r].reshape(columns, width)
+        low = query_ref[r]
+        high = pltpu.roll(low.astype(jnp.float32), SHIFT, 1).astype(low.dtype)
         even = lax.dot_general(
-            low_ref[r], block[:, :HALF], contract, preferred_element_type=jnp.float32
+            low, block[:, :HALF], contract, preferred_element_type=jnp.float32
         )
         odd = lax.dot_general(
-            high_ref[r], block[:, width - HALF :], contract, preferred_element_type=jnp.float32
-        )
-        limit = limit_ref[r]
-        even = jnp.where(early <= limit, even * score_scale, masked_score)
-        odd = jnp.where(early <= limit - 1, odd * score_scale, masked_score)
-        highest = jnp.maximum(
-            jnp.max(even, axis=-1, keepdims=True), jnp.max(odd, axis=-1, keepdims=True)
-        )
-        even = jnp.exp(even - highest)
-        odd = jnp.exp(odd - highest)
-        total = jnp.sum(even, axis=-1, keepdims=True) + jnp.sum(odd, axis=-1, keepdims=True)
-        even = (even / total).astype(jnp.bfloat16)
-        odd = (odd / total).astype(jnp.bfloat16)
-        latent = jnp.dot(even, block[:, :KV], preferred_element_type=jnp.float32)
-        other = jnp.dot(odd, block[:, width - HALF :], preferred_element_type=jnp.float32)
-        latent = latent + other[:, SHIFT : SHIFT + KV]
+            high, block[:, width - HALF :], contract, preferred_element_type=jnp.float32
+        )
+        return even, odd
+
+    scored = score(0)
+    for r in range(requests):
+        even, odd = scored
+        if r + 1 < requests:
+            scored = score(r + 1)
+        limit = plan_ref[requests + r]
+        even = jnp.where(early <= limit, even, masked_score)
+        odd = jnp.where(early < limit, odd, masked_score)
+        highest = jnp.max(jnp.maximum(even, odd), axis=-1, keepdims=True)
+        even = jnp.exp2((even - highest) * exponent_scale)
+        odd = jnp.exp2((odd - highest) * exponent_scale)
+        total = jnp.sum(even + odd, axis=-1, keepdims=True)
+        block = context[r].reshape(columns, width)
+        latent = jnp.dot(
+            even.astype(jnp.bfloat16), block[:, :KV], preferred_element_type=jnp.float32
+        )
+        other = jnp.dot(
+            odd.astype(jnp.bfloat16), block[:, width - HALF :], preferred_element_type=jnp.float32
+        )
+        latent = (latent + other[:, SHIFT : SHIFT + KV]) * (1.0 / total)
         for h in range(rows // DRAFT):
             held[r * DRAFT : (r + 1) * DRAFT, h * KV : (h + 1) * KV] = latent[
                 h * DRAFT : (h + 1) * DRAFT, :
@@ -231,8 +283,8 @@
     out_ref[...] = held[...].astype(out_ref.dtype)
 
 
-def attend(place, limits, low, high, pages, each):
-    requests, rows, _ = low.shape
+def attend(plan, query, pages, each):
+    requests, rows, _ = query.shape
     _, pairs, width = pages.shape
     out = (requests * DRAFT, (rows // DRAFT) * KV)
     return pl.pallas_call(
@@ -240,8 +292,6 @@
         out_shape=jax.ShapeDtypeStruct(out, jnp.bfloat16),
         in_specs=[
             pl.BlockSpec(memory_space=pltpu.SMEM),
-            pl.BlockSpec(memory_space=pltpu.SMEM),
-            pl.BlockSpec(memory_space=pltpu.VMEM),
             pl.BlockSpec(memory_space=pltpu.VMEM),
             pl.BlockSpec(memory_space=pltpu.HBM),
         ],
@@ -249,11 +299,11 @@
         scratch_shapes=[
             pltpu.VMEM((requests, each, pairs, width), pages.dtype),
             pltpu.VMEM(out, jnp.float32),
-            pltpu.SemaphoreType.DMA((requests, each)),
+            pltpu.SemaphoreType.DMA((requests * each,)),
         ],
-        compiler_params=pltpu.CompilerParams(vmem_limit_bytes=48 << 20),
+        compiler_params=pltpu.CompilerParams(vmem_limit_bytes=50 << 20),
         name="attend_pages",
-    )(place, limits, low, high, pages)
+    )(plan, query, pages)
 
 
 def local(
@@ -282,27 +332,37 @@
 
     n_ep = lax.axis_size("ep")
     experts = n_ep // 2
-    everyone = spread(pack_rows(routes.T, route_scores.T, residual, experts), group)
+    packed = pack_rows(routes.T, route_scores.T, residual, experts)
+    far, near = peers // 2, peers // 4
+    across = [exchange(packed, group, bit) for bit in (far, near, far | near)]
 
     outgoing = stage_pages(
         device.reshape(1), page_table.T, serving.reshape(1, -1), page_pool, peers, listed
     )
+    packed, across, outgoing = lax.optimization_barrier((packed, across, outgoing))
     pairs = outgoing.shape[1]
     arrived = lax.all_to_all(
         outgoing.reshape(peers, fetched, pairs, 2 * LAT), group, split_axis=0, concat_axis=0, tiled=True
     )
 
-    rows = everyone[:, :width]
-    parts = everyone[:, width : width + 3 * experts].astype(jnp.float32)
-    expert = lax.axis_index("ep") // 2
-    own = (jnp.arange(3 * experts, dtype=jnp.int32) % experts) == expert
-    weight = jnp.sum(jnp.where(own[None, :], parts, 0.0), axis=1, keepdims=True)
-    gate = jnp.dot(rows, w_gate[0], preferred_element_type=jnp.float32)
-    upward = jnp.dot(rows, w_up[0], preferred_element_type=jnp.float32)
-    hidden = (jax.nn.silu(gate) * upward).astype(jnp.bfloat16)
-    partial_out = jnp.dot(hidden, w_down[0], preferred_element_type=jnp.float32) * weight
-    mixed = collect(partial_out, group)
-    moe_out = (residual.astype(jnp.float32) + mixed).astype(jnp.bfloat16)
+    kept = jnp.concatenate([packed, *across], axis=0)
+    bit = near // 2
+    while bit > 1:
+        kept = jnp.concatenate([kept, exchange(kept, group, bit)], axis=0)
+        bit //= 2
+    other = exchange(kept, group, 1)
+    label = (lax.axis_index("ep") // 2).reshape(1)
+    mixed, leaving = expert_rows(label, kept, other, w_gate[0], w_up[0], w_down[0], experts)
+    bit = 1
+    while True:
+        last = exchange(leaving, group, bit)
+        bit *= 2
+        if bit == peers:
+            break
+        mixed = mixed + last.astype(jnp.float32)
+        half = mixed.shape[0] // 2
+        leaving = mixed[half:].astype(jnp.bfloat16)
+        mixed = mixed[:half]
 
     served = lax.dynamic_slice_in_dim(serving, device * requests_dev, requests_dev)
     slots = jnp.arange(n_requests, dtype=jnp.int32)
@@ -315,11 +375,12 @@
     limits = jnp.sum(jnp.where(chosen, context_len[None, :], 0), axis=1) - DRAFT
     heads = queries.reshape(requests_dev, DRAFT, HEADS, LAT).transpose(0, 2, 1, 3)
     heads = heads.reshape(requests_dev, HEADS * DRAFT, LAT)
-    low = jnp.pad(heads, ((0, 0), (0, 0), (0, SHIFT)))
-    high = jnp.pad(heads, ((0, 0), (0, 0), (SHIFT, 0)))
-    latent_out = attend(
-        place, limits, low, high, arrived.reshape(listed, pairs, 2 * LAT), pages_each
-    )
+    query = jnp.pad(heads, ((0, 0), (0, 0), (0, SHIFT)))
+    counts = jnp.minimum((limits + DRAFT - 1) // (2 * pairs) + 1, pages_each)
+    plan = jnp.concatenate([counts, limits, place])
+    latent_out = attend(plan, query, arrived.reshape(listed, pairs, 2 * LAT), pages_each)
+    latent_out, last = lax.optimization_barrier((latent_out, last))
+    moe_out = (residual.astype(jnp.float32) + mixed + last.astype(jnp.float32)).astype(jnp.bfloat16)
     return (latent_out, moe_out)
 
 

time: 156 us -> 138 us (0.88); the launches traced: 153 us -> 137 us
  local copies, waits for them, and re-layouts: 16.7 us -> 4.25 us
  waiting for transfers between devices: 74 us -> 81.2 us
  matrix products: 6.73 us -> 0 us
  starting transfers between devices: 28.5 us -> 25.1 us
  other arithmetic: 6.62 us -> 4.25 us
  Pallas kernels: 19.7 us -> 21.5 us
    unnamed x36 -> x20, local copies, waits for them, and re-layouts: 8.99 us -> 1.02 us
    dot_general x2 -> x0, matrix products: 6.73 us -> none  [the longest x1 6.07 us: local(): jnp.dot(hidden, w_down[0], preferred_element_type=jnp.float32) * weight]
    ppermute x8 -> x9, waiting for transfers between devices: 74 us -> 80.6 us  [exchange(): return lax.ppermute(block, group, [(d, d ^ bit) for d in range(peers)])]
    pallas_call x0 -> x1, Pallas kernels: none -> 6.25 us  [expert_rows(): pl.pallas_call(functools.partial(expert_body, experts), out_shape=(jax.Sh...]
    pallas_call x1, Pallas kernels: 8.76 us -> 5.78 us  [stage_pages(): pl.pallas_call(functools.partial(stage_body, peers), out_shape=jax.ShapeD...]
    ppermute x8 -> x9, starting transfers between devices: 20.7 us -> 18.9 us  [exchange(): return lax.ppermute(block, group, [(d, d ^ bit) for d in range(peers)])]
    pad x1, local copies, waits for them, and re-layouts: 1.89 us -> 0.12 us  [local(): query = jnp.pad(heads, ((0, 0), (0, 0), (0, SHIFT)))]
    slice x4 -> x3, local copies, waits for them, and re-layouts: 1.68 us -> 0.09 us  [local(): leaving = mixed[half:].astype(jnp.bfloat16)]
  transfers between devices with their start and end apart: 9 -> 10, of which waited for: 7 -> 8; matrix products, arithmetic and copies ran while one was open for 13% -> 5% of each run, Pallas kernels for 6% -> 14%
where the time goes in v4:
time: 138 us; the launch traced here: 137 us
  waiting for transfers between devices  81.2 us (59%)
  starting transfers between devices  25.1 us (18%)
  Pallas kernels  21.5 us (16%)
  local copies, waits for them, and re-layouts  4.25 us (3%)
  other arithmetic  4.25 us (3%)
    ppermute x9, waiting for transfers between devices, exchange(): return lax.ppermute(block, group, [(d, d ^ bit) for d in range(peers)])  80.6 us
    ppermute x9, starting transfers between devices, exchange(): return lax.ppermute(block, group, [(d, d ^ bit) for d in range(peers)])  18.9 us
    pallas_call x1, Pallas kernels, attend(): pl.pallas_call(attend_body, out_shape=jax.ShapeDtypeStruct(out, jnp.bfloa...  7.71 us
    all_to_all x1, starting transfers between devices, local(): lax.all_to_all(outgoing.reshape(peers, fetched, pairs, 2 * LAT), group, s...  6.29 us
    pallas_call x1, Pallas kernels, expert_rows(): pl.pallas_call(functools.partial(expert_body, experts), out_shape=(jax.Sh...  6.25 us
    pallas_call x1, Pallas kernels, stage_pages(): pl.pallas_call(functools.partial(stage_body, peers), out_shape=jax.ShapeD...  5.78 us
    add x3, other arithmetic, local(): mixed = mixed + last.astype(jnp.float32)  2.83 us
  transfers between devices with their start and end apart: 10, of which 8 were waited for; matrix products, arithmetic and copies ran while one was open for 5% of the time, Pallas kernels for 14%

profile of v4, /device:TPU:15, one launch (start us, length us, event | category | flops | bytes accessed | tf_op | source)
XLA Modules:
  0.0 137.1 jit_solution(3028200515493682727)
XLA Ops:
  0.6 1.8 %pack_rows.1 = bf16[16,3712]{1,0:T(8,128)(2,1)} custom-call(s32[2,16]{1,0:T(2,128)} %bitcast.20, f32[2,16]{1,0:T(2,128)} %bitcast.21, bf16[16,3584]{1,0:T(8,128)(2,1)} %rows_ref.1), custom_call_target="tpu_custom_call" | custom-call | tf_op jit(solution)/shard_map/pack_rows/pallas_call | solution.py:148
  2.4 2.3 %collective-permute-start = (bf16[16,3712]{1,0:T(8,128)(2,1)}, bf16[16,3712]{1,0:T(8,128)(2,1)S(1)}, u32[]{:S(2)}, u32[]{:S(2)}) collective-permute-start(bf16[16,3712]{1,0:T(8,128)(2,1)} %pack_rows.1), channel_id=1, source_target_pairs={{0,8},{1,9},{2,10},{3,11},{4,12},{5,13},{6,14},{7,15},{8,0},{9,1},... | collective-permute-start | bytes 356360 | tf_op jit(solution)/shard_map/ppermute | solution.py:157
  4.7 0.2 collective-permute-start.1
  4.9 0.2 collective-permute-start.2
  5.1 5.8 %stage_pages.1 = bf16[64,32,1152]{2,1,0:T(8,128)(2,1)} custom-call(s32[1]{0:T(128)} %bitcast.4.device_ref, s32[16,64]{1,0:T(8,128)} %bitcast.19, s32[1,64]{1,0:T(1,128)} %bitcast.22, bf16[32,36864]{1,0:T(8,128)(2,1)} %pool_ref.1), custom_call_target="tpu_custom_call" | custom-call | tf_op jit(solution)/shard_map/stage_pages/pallas_call | solution.py:96
  10.8 0.1 collective-permute-done
  11.0 0.0 collective-permute-done.1
  11.0 4.5 %collective-permute-done.2 = bf16[16,3712]{1,0:T(8,128)(2,1)S(1)} collective-permute-done((bf16[16,3712]{1,0:T(8,128)(2,1)}, bf16[16,3712]{1,0:T(8,128)(2,1)S(1)}, u32[]{:S(2)}, u32[]{:S(2)}) %collective-permute-start.2) | collective-permute-done | bytes 118816 | tf_op jit(solution)/shard_map/ppermute | solution.py:157
  15.5 6.3 %all-to-all-start = ((bf16[16,4,32,1152]{3,2,1,0:T(8,128)(2,1)}), bf16[16,4,32,1152]{3,2,1,0:T(8,128)(2,1)}, u32[]{:S(2)}, u32[]{:S(2)}) async-start(bf16[16,4,32,1152]{3,2,1,0:T(8,128)(2,1)} %bitcast.14), calls=%async_computation | async-start | bytes 9437184 | tf_op jit(solution)/shard_map/all_to_all | solution.py:344
  21.8 0.0 copy-done.2
  21.9 0.3 collective-permute-start.3
  22.3 36.2 %collective-permute-done.3 = bf16[64,3712]{1,0:T(8,128)(2,1)S(1)} collective-permute-done((bf16[64,3712]{1,0:T(8,128)(2,1)S(1)}, bf16[64,3712]{1,0:T(8,128)(2,1)S(1)}, u32[]{:S(2)}, u32[]{:S(2)}) %collective-permute-start.3) | collective-permute-done | bytes 475168 | tf_op jit(solution)/shard_map/ppermute | solution.py:157
  58.6 0.0 copy-start
  58.6 0.9 collective-permute-start.4
  59.5 2.1 %collective-permute-done.4.other_ref = bf16[128,3712]{1,0:T(8,128)(2,1)S(1)} collective-permute-done((bf16[128,3712]{1,0:T(8,128)(2,1)S(1)}, bf16[128,3712]{1,0:T(8,128)(2,1)S(1)}, u32[]{:S(2)}, u32[]{:S(2)}) %collective-permute-start.4) | collective-permute-done | bytes 950304 | tf_op jit(solution)/shard_map/ppermute | solution.py:157
  61.7 0.0 copy-done
  61.7 0.9 copy-done.3
  62.6 6.2 %expert_rows.1 = (f32[128,3584]{1,0:T(8,128)}, bf16[128,3584]{1,0:T(8,128)(2,1)}) custom-call(s32[1]{0:T(128)} %bitcast.9.label_ref, bf16[128,3712]{1,0:T(8,128)(2,1)} %copy-done, bf16[128,3712]{1,0:T(8,128)(2,1)} %copy-done.3, bf16[3584,256]{1,0:T(8,128)(2,1)} %bitcast.16, bf16[3584,256]{1,0:T(8,128)(2,1)} %bitcast.17, bf16[256,3584]{1,0:T(8,128)(2,1)} %bitcast.18), custom_call_target="tpu_custom_call" | custom-call | tf_op jit(solution)/shard_map/expert_rows/pallas_call | solution.py:191
  68.8 0.4 collective-permute-start.5
  69.3 0.0 copy-done.6
  69.3 0.1 dynamic_slice.3
  69.4 2.2 %collective-permute-done.5 = bf16[128,3584]{1,0:T(8,128)(2,1)S(1)} collective-permute-done((bf16[128,3584]{1,0:T(8,128)(2,1)}, bf16[128,3584]{1,0:T(8,128)(2,1)S(1)}, u32[]{:S(2)}, u32[]{:S(2)}) %collective-permute-start.5) | collective-permute-done | bytes 917536 | tf_op jit(solution)/shard_map/ppermute | solution.py:157
  71.6 1.7 %convert_add_fusion = f32[128,3584]{1,0:T(8,128)S(1)} fusion(f32[128,3584]{1,0:T(8,128)} %get-tuple-element.16, bf16[128,3584]{1,0:T(8,128)(2,1)S(1)} %collective-permute-done.5), kind=kLoop, calls=%fused_computation | loop fusion | flops 917504 | bytes 4587520 | tf_op jit(solution)/shard_map/add | solution.py:362
  73.3 0.0 copy-start.7
  73.4 0.1 collective-permute-start.6
  73.4 0.1 iota_compare_fusion.1
  73.5 0.0 copy-done.5
  73.5 0.1 select_reduce_fusion
  73.7 0.1 reshape.106
  73.8 0.2 convert_reduce_fusion
  73.9 0.0 copy-start.1
  74.0 17.6 %collective-permute-done.6 = bf16[64,3584]{1,0:T(8,128)(2,1)} collective-permute-done((bf16[64,3584]{1,0:T(8,128)(2,1)S(1)}, bf16[64,3584]{1,0:T(8,128)(2,1)}, u32[]{:S(2)}, u32[]{:S(2)}) %collective-permute-start.6) | collective-permute-done | bytes 458784 | tf_op jit(solution)/shard_map/ppermute | solution.py:157
  91.6 1.1 slice_add_fusion
  92.7 6.3 %collective-permute-start.7 = (bf16[32,3584]{1,0:T(8,128)(2,1)S(1)}, bf16[32,3584]{1,0:T(8,128)(2,1)S(1)}, u32[]{:S(2)}, u32[]{:S(2)}) collective-permute-start(bf16[32,3584]{1,0:T(8,128)(2,1)S(1)} %slice.44), channel_id=1, source_target_pairs={{0,4},{1,5},{2,6},{3,7},{4,0},{5,1},{6,2},{7,3},{8,12},{9,13},{10,... | collective-permute-start | bytes 688136 | tf_op jit(solution)/shard_map/ppermute | solution.py:157
  99.0 0.2 select_reduce_fusion.1
  99.2 17.7 %collective-permute-done.7 = bf16[32,3584]{1,0:T(8,128)(2,1)S(1)} collective-permute-done((bf16[32,3584]{1,0:T(8,128)(2,1)S(1)}, bf16[32,3584]{1,0:T(8,128)(2,1)S(1)}, u32[]{:S(2)}, u32[]{:S(2)}) %collective-permute-start.7) | collective-permute-done | bytes 229408 | tf_op jit(solution)/shard_map/ppermute | solution.py:157
  116.9 0.1 slice_add_fusion.1
  117.0 8.1 %collective-permute-start.8 = (bf16[16,3584]{1,0:T(8,128)(2,1)S(1)}, bf16[16,3584]{1,0:T(8,128)(2,1)S(1)}, u32[]{:S(2)}, u32[]{:S(2)}) collective-permute-start(bf16[16,3584]{1,0:T(8,128)(2,1)S(1)} %slice.45), channel_id=1, source_target_pairs={{0,8},{1,9},{2,10},{3,11},{4,12},{5,13},{6,14},{7,15},{8,0},{9,1},... | collective-permute-start | bytes 344072 | tf_op jit(solution)/shard_map/ppermute | solution.py:157
  125.1 1.6 %reshape.107 = bf16[4,4,64,576]{3,2,1,0:T(8,128)(2,1)S(1)} reshape(bf16[16,36864]{1,0:T(8,128)(2,1)S(1)} %copy-done.1) | data formatting | bytes 2359296 | tf_op jit(solution)/shard_map/reshape | solution.py:376
  126.8 1.0 copy.18
  127.8 0.2 copy.19
  128.0 0.1 pad.4.query_ref
  128.1 0.1 pad_add_fusion.plan_ref
  128.2 0.5 all-to-all-done
  128.7 7.7 %attend_pages.1 = bf16[16,32768]{1,0:T(8,128)(2,1)} custom-call(s32[72]{0:T(128)S(1)} %pad_add_fusion.plan_ref, bf16[4,256,640]{2,1,0:T(8,128)(2,1)S(1)} %pad.4.query_ref, bf16[64,32,1152]{2,1,0:T(8,128)(2,1)} %bitcast.8.pages_ref), custom_call_target="tpu_custom_call" | custom-call | tf_op jit(solution)/shard_map/attend_pages/pallas_call | solution.py:290
  136.4 0.0 collective-permute-done.8
  136.4 0.0 copy-done.4
  136.5 0.7 fusion.1
  (19 shorter events, 0.3 us)
Async XLA Ops:
  2.4 8.6 %collective-permute-start = (bf16[16,3712]{1,0:T(8,128)(2,1)}, bf16[16,3712]{1,0:T(8,128)(2,1)S(1)}, u32[]{:S(2)}, u32[]{:S(2)}) collective-permute-start(bf16[16,3712]{1,0:T(8,128)(2,1)} %pack_rows.1), channel_id=1, source_target_pairs={{0,8},{1,9},{2,10},{3,11},{4,12},{5,13},{6,14},{7,15},{8,0},{9,1},... | collective-permute-start | bytes 356360 | tf_op jit(solution)/shard_map/ppermute | solution.py:157
  4.7 6.3 %collective-permute-start.1 = (bf16[16,3712]{1,0:T(8,128)(2,1)}, bf16[16,3712]{1,0:T(8,128)(2,1)S(1)}, u32[]{:S(2)}, u32[]{:S(2)}) collective-permute-start(bf16[16,3712]{1,0:T(8,128)(2,1)} %pack_rows.1), channel_id=1, source_target_pairs={{0,4},{1,5},{2,6},{3,7},{4,0},{5,1},{6,2},{7,3},{8,12},{9,13},{10,... | collective-permute-start | bytes 356360 | tf_op jit(solution)/shard_map/ppermute | solution.py:157
  4.9 10.6 %collective-permute-start.2 = (bf16[16,3712]{1,0:T(8,128)(2,1)}, bf16[16,3712]{1,0:T(8,128)(2,1)S(1)}, u32[]{:S(2)}, u32[]{:S(2)}) collective-permute-start(bf16[16,3712]{1,0:T(8,128)(2,1)} %pack_rows.1), channel_id=1, source_target_pairs={{0,12},{1,13},{2,14},{3,15},{4,8},{5,9},{6,10},{7,11},{8,4},{9,5},... | collective-permute-start | bytes 356360 | tf_op jit(solution)/shard_map/ppermute | solution.py:157
  15.5 6.3 %copy-start.2 = (bf16[16,3712]{1,0:T(8,128)(2,1)S(1)}, bf16[16,3712]{1,0:T(8,128)(2,1)}, u32[]{:S(2)}) copy-start(bf16[16,3712]{1,0:T(8,128)(2,1)} %pack_rows.1) | copy-start | bytes 356356
  15.5 113.2 %all-to-all-start = ((bf16[16,4,32,1152]{3,2,1,0:T(8,128)(2,1)}), bf16[16,4,32,1152]{3,2,1,0:T(8,128)(2,1)}, u32[]{:S(2)}, u32[]{:S(2)}) async-start(bf16[16,4,32,1152]{3,2,1,0:T(8,128)(2,1)} %bitcast.14), calls=%async_computation | async-start | bytes 9437184 | tf_op jit(solution)/shard_map/all_to_all | solution.py:344
  21.9 36.7 %collective-permute-start.3 = (bf16[64,3712]{1,0:T(8,128)(2,1)S(1)}, bf16[64,3712]{1,0:T(8,128)(2,1)S(1)}, u32[]{:S(2)}, u32[]{:S(2)}) collective-permute-start(bf16[64,3712]{1,0:T(8,128)(2,1)S(1)} %pad_maximum_fusion), channel_id=1, source_target_pairs={{0,2},{1,3},{2,0},{3,1},{4,6},{5,7},{6,4},{7,5},{8,10},{9,11},{10,... | collective-permute-start | bytes 1425416 | tf_op jit(solution)/shard_map/ppermute | solution.py:157
  58.6 3.1 %copy-start = (bf16[128,3712]{1,0:T(8,128)(2,1)}, bf16[128,3712]{1,0:T(8,128)(2,1)S(1)}, u32[]{:S(2)}) copy-start(bf16[128,3712]{1,0:T(8,128)(2,1)S(1)} %constant_dynamic-update-slice_fusion.kept_ref) | copy-start | bytes 2850820
  58.6 3.1 %collective-permute-start.4 = (bf16[128,3712]{1,0:T(8,128)(2,1)S(1)}, bf16[128,3712]{1,0:T(8,128)(2,1)S(1)}, u32[]{:S(2)}, u32[]{:S(2)}) collective-permute-start(bf16[128,3712]{1,0:T(8,128)(2,1)S(1)} %constant_dynamic-update-slice_fusion.kept_ref), channel_id=1, source_target_pairs={{0,1},{1,0},{2,3},{3,2},{4,5},{5,4},{6,7},{7,6},{8,9},{9,8},{10,11... | collective-permute-start | bytes 2850824 | tf_op jit(solution)/shard_map/ppermute | solution.py:157
  61.7 0.9 copy-start.3
  62.6 6.7 %copy-start.6 = (s32[64]{0:T(128)S(1)}, s32[64]{0:T(128)}, u32[]{:S(2)}) copy-start(s32[64]{0:T(128)} %param.14) | copy-start | bytes 772
  68.8 2.8 %collective-permute-start.5 = (bf16[128,3584]{1,0:T(8,128)(2,1)}, bf16[128,3584]{1,0:T(8,128)(2,1)S(1)}, u32[]{:S(2)}, u32[]{:S(2)}) collective-permute-start(bf16[128,3584]{1,0:T(8,128)(2,1)} %get-tuple-element.17), channel_id=1, source_target_pairs={{0,1},{1,0},{2,3},{3,2},{4,5},{5,4},{6,7},{7,6},{8,9},{9,8},{10,11... | collective-permute-start | bytes 2752520 | tf_op jit(solution)/shard_map/ppermute | solution.py:157
  71.6 1.9 %copy-start.5 = (s32[64,16]{0,1:T(8,128)S(1)}, s32[64,16]{0,1:T(8,128)}, u32[]{:S(2)}) copy-start(s32[64,16]{0,1:T(8,128)} %param.13) | copy-start | bytes 12292
  73.3 25.7 %copy-start.7 = (s32[64]{0:T(128)S(1)}, s32[64]{0:T(128)}, u32[]{:S(2)}) copy-start(s32[64]{0:T(128)} %param.15) | copy-start | bytes 772
  73.4 18.2 %collective-permute-start.6 = (bf16[64,3584]{1,0:T(8,128)(2,1)S(1)}, bf16[64,3584]{1,0:T(8,128)(2,1)}, u32[]{:S(2)}, u32[]{:S(2)}) collective-permute-start(bf16[64,3584]{1,0:T(8,128)(2,1)S(1)} %slice.43), channel_id=1, source_target_pairs={{0,2},{1,3},{2,0},{3,1},{4,6},{5,7},{6,4},{7,5},{8,10},{9,11},{10,... | collective-permute-start | bytes 1376264 | tf_op jit(solution)/shard_map/ppermute | solution.py:157
  73.9 51.2 %copy-start.1 = (bf16[16,36864]{1,0:T(8,128)(2,1)S(1)}, bf16[16,36864]{1,0:T(8,128)(2,1)}, u32[]{:S(2)}) copy-start(bf16[16,36864]{1,0:T(8,128)(2,1)} %param.11) | copy-start | bytes 3538948
  92.7 24.2 %collective-permute-start.7 = (bf16[32,3584]{1,0:T(8,128)(2,1)S(1)}, bf16[32,3584]{1,0:T(8,128)(2,1)S(1)}, u32[]{:S(2)}, u32[]{:S(2)}) collective-permute-start(bf16[32,3584]{1,0:T(8,128)(2,1)S(1)} %slice.44), channel_id=1, source_target_pairs={{0,4},{1,5},{2,6},{3,7},{4,0},{5,1},{6,2},{7,3},{8,12},{9,13},{10,... | collective-permute-start | bytes 688136 | tf_op jit(solution)/shard_map/ppermute | solution.py:157
  117.0 19.4 %collective-permute-start.8 = (bf16[16,3584]{1,0:T(8,128)(2,1)S(1)}, bf16[16,3584]{1,0:T(8,128)(2,1)S(1)}, u32[]{:S(2)}, u32[]{:S(2)}) collective-permute-start(bf16[16,3584]{1,0:T(8,128)(2,1)S(1)} %slice.45), channel_id=1, source_target_pairs={{0,8},{1,9},{2,10},{3,11},{4,12},{5,13},{6,14},{7,15},{8,0},{9,1},... | collective-permute-start | bytes 344072 | tf_op jit(solution)/shard_map/ppermute | solution.py:157
  128.7 7.7 %copy-start.4 = (bf16[16,3584]{1,0:T(8,128)(2,1)S(1)}, bf16[16,3584]{1,0:T(8,128)(2,1)}, u32[]{:S(2)}) copy-start(bf16[16,3584]{1,0:T(8,128)(2,1)} %rows_ref.1) | copy-start | bytes 344068

commit v5 on v4

--- a/solution.py
+++ b/solution.py
@@ -17,6 +17,8 @@
 
 exponent_scale = 192.0 ** (-0.5) * math.log2(math.e)
 masked_score = -1e30
+JOIN_FLOPS = 300_000_000_000
+STAGE_FLOPS = 20_000_000_000
 
 
 def ones_where(condition):
@@ -113,6 +115,7 @@
             pltpu.SemaphoreType.DMA((slots,)),
         ],
         compiler_params=pltpu.CompilerParams(vmem_limit_bytes=56 << 20),
+        cost_estimate=pl.CostEstimate(flops=STAGE_FLOPS, bytes_accessed=0, transcendentals=0),
         name="stage_pages",
     )(device, table, serving, pool)
 
@@ -150,6 +153,24 @@
         out_shape=jax.ShapeDtypeStruct((rows.shape[0], width), rows.dtype),
         name="pack_rows",
     )(routes, scores, rows)
+
+
+def join_body(*refs):
+    blocks, out_ref = refs[:-1], refs[-1]
+    start = 0
+    for block_ref in blocks:
+        out_ref[start : start + block_ref.shape[0], :] = block_ref[...]
+        start += block_ref.shape[0]
+
+
+def join_rows(blocks):
+    rows = sum(block.shape[0] for block in blocks)
+    return pl.pallas_call(
+        join_body,
+        out_shape=jax.ShapeDtypeStruct((rows, blocks[0].shape[1]), blocks[0].dtype),
+        cost_estimate=pl.CostEstimate(flops=JOIN_FLOPS, bytes_accessed=0, transcendentals=0),
+        name="join_rows",
+    )(*blocks)
 
 
 def exchange(block, group, bit):
@@ -339,18 +360,21 @@
     outgoing = stage_pages(
         device.reshape(1), page_table.T, serving.reshape(1, -1), page_pool, peers, listed
     )
-    packed, across, outgoing = lax.optimization_barrier((packed, across, outgoing))
     pairs = outgoing.shape[1]
     arrived = lax.all_to_all(
         outgoing.reshape(peers, fetched, pairs, 2 * LAT), group, split_axis=0, concat_axis=0, tiled=True
     )
 
-    kept = jnp.concatenate([packed, *across], axis=0)
+    kept = join_rows([packed, *across])
     bit = near // 2
     while bit > 1:
         kept = jnp.concatenate([kept, exchange(kept, group, bit)], axis=0)
         bit //= 2
+    kept, queries = lax.optimization_barrier((kept, queries))
     other = exchange(kept, group, 1)
+    heads = queries.reshape(requests_dev, DRAFT, HEADS, LAT).transpose(0, 2, 1, 3)
+    heads = heads.reshape(requests_dev, HEADS * DRAFT, LAT)
+    query = jnp.pad(heads, ((0, 0), (0, 0), (0, SHIFT)))
     label = (lax.axis_index("ep") // 2).reshape(1)
     mixed, leaving = expert_rows(label, kept, other, w_gate[0], w_up[0], w_down[0], experts)
     bit = 1
@@ -360,6 +384,8 @@
         if bit == peers:
             break
         mixed = mixed + last.astype(jnp.float32)
+        if bit == 2:
+            mixed, query = lax.optimization_barrier((mixed, query))
         half = mixed.shape[0] // 2
         leaving = mixed[half:].astype(jnp.bfloat16)
         mixed = mixed[:half]
@@ -373,9 +399,6 @@
     same = (own_list[:, None] == own_list[None, :]) & (position[None, :] < position[:, None])
     place = own_list * fetched + jnp.sum(same.astype(jnp.int32), axis=1)
     limits = jnp.sum(jnp.where(chosen, context_len[None, :], 0), axis=1) - DRAFT
-    heads = queries.reshape(requests_dev, DRAFT, HEADS, LAT).transpose(0, 2, 1, 3)
-    heads = heads.reshape(requests_dev, HEADS * DRAFT, LAT)
-    query = jnp.pad(heads, ((0, 0), (0, 0), (0, SHIFT)))
     counts = jnp.minimum((limits + DRAFT - 1) // (2 * pairs) + 1, pages_each)
     plan = jnp.concatenate([counts, limits, place])
     latent_out = attend(plan, query, arrived.reshape(listed, pairs, 2 * LAT), pages_each)

time: 138 us -> 135 us (0.978)
  waiting for transfers between devices: 81.2 us -> 68.5 us
  starting transfers between devices: 25.1 us -> 29.1 us
  local copies, waits for them, and re-layouts: 4.25 us -> 7.55 us
  Pallas kernels: 21.5 us -> 23.6 us
    ppermute x9, waiting for transfers between devices: 80.6 us -> 65.4 us  [exchange(): return lax.ppermute(block, group, [(d, d ^ bit) for d in range(peers)])]
    ppermute x9, starting transfers between devices: 18.9 us -> 21.7 us  [exchange(): return lax.ppermute(block, group, [(d, d ^ bit) for d in range(peers)])]
    unnamed x20 -> x22, local copies, waits for them, and re-layouts: 1.02 us -> 3.61 us
    all_to_all x1, waiting for transfers between devices: 0.53 us -> 3.12 us  [local(): lax.all_to_all(outgoing.reshape(peers, fetched, pairs, 2 * LAT), group, s...]
    pallas_call x0 -> x1, Pallas kernels: none -> 1.87 us  [join_rows(): pl.pallas_call(join_body, out_shape=jax.ShapeDtypeStruct((rows, blocks[0]...]
  transfers between devices with their start and end apart: 10 -> 10, of which waited for: 8 -> 5; matrix products, arithmetic and copies ran while one was open for 5% -> 6% of each run, Pallas kernels for 14% -> 16%
where the time goes in v5:
time: 135 us
  waiting for transfers between devices  68.5 us (51%)
  starting transfers between devices  29.1 us (22%)
  Pallas kernels  23.6 us (17%)
  local copies, waits for them, and re-layouts  7.55 us (6%)
  other arithmetic  5.04 us (4%)
    ppermute x9, waiting for transfers between devices, exchange(): return lax.ppermute(block, group, [(d, d ^ bit) for d in range(peers)])  65.4 us
    ppermute x9, starting transfers between devices, exchange(): return lax.ppermute(block, group, [(d, d ^ bit) for d in range(peers)])  21.7 us
    pallas_call x1, Pallas kernels, attend(): pl.pallas_call(attend_body, out_shape=jax.ShapeDtypeStruct(out, jnp.bfloa...  7.86 us
    all_to_all x1, starting transfers between devices, local(): lax.all_to_all(outgoing.reshape(peers, fetched, pairs, 2 * LAT), group, s...  7.46 us
    pallas_call x1, Pallas kernels, expert_rows(): pl.pallas_call(functools.partial(expert_body, experts), out_shape=(jax.Sh...  6.33 us
    pallas_call x1, Pallas kernels, stage_pages(): pl.pallas_call(functools.partial(stage_body, peers), out_shape=jax.ShapeD...  5.79 us
    unnamed x22, local copies, waits for them, and re-layouts  3.61 us
    all_to_all x1, waiting for transfers between devices, local(): lax.all_to_all(outgoing.reshape(peers, fetched, pairs, 2 * LAT), group, s...  3.12 us
  transfers between devices with their start and end apart: 10, of which 5 were waited for; matrix products, arithmetic and copies ran while one was open for 6% of the time, Pallas kernels for 16%

profile of v5, /device:TPU:15, one launch (start us, length us, event | category | flops | bytes accessed | tf_op | source)
XLA Modules:
  0.0 134.6 jit_solution(11454000839275191220)
XLA Ops:
  0.6 1.8 %pack_rows.1.refs_0_ = bf16[16,3712]{1,0:T(8,128)(2,1)} custom-call(s32[2,16]{1,0:T(2,128)} %bitcast.20, f32[2,16]{1,0:T(2,128)} %bitcast.21, bf16[16,3584]{1,0:T(8,128)(2,1)} %rows_ref.1), custom_call_target="tpu_custom_call" | custom-call | tf_op jit(solution)/shard_map/pack_rows/pallas_call | solution.py:151
  2.4 1.3 collective-permute-start.2
  3.7 2.2 %collective-permute-start.1 = (bf16[16,3712]{1,0:T(8,128)(2,1)}, bf16[16,3712]{1,0:T(8,128)(2,1)S(1)}, u32[]{:S(2)}, u32[]{:S(2)}) collective-permute-start(bf16[16,3712]{1,0:T(8,128)(2,1)} %pack_rows.1.refs_0_), channel_id=1, source_target_pairs={{0,4},{1,5},{2,6},{3,7},{4,0},{5,1},{6,2},{7,3},{8,12},{9,13},{10,... | collective-permute-start | bytes 356360 | tf_op jit(solution)/shard_map/ppermute | solution.py:178
  5.9 0.0 collective-permute-start
  5.9 5.8 %stage_pages.1 = bf16[64,32,1152]{2,1,0:T(8,128)(2,1)} custom-call(s32[1]{0:T(128)} %bitcast.8.device_ref, s32[16,64]{1,0:T(8,128)} %bitcast.19, s32[1,64]{1,0:T(1,128)} %bitcast.22, bf16[32,36864]{1,0:T(8,128)(2,1)} %pool_ref.1), custom_call_target="tpu_custom_call" | custom-call | flops 20000000000 | tf_op jit(solution)/shard_map/stage_pages/pallas_call | solution.py:98
  11.7 7.5 %all-to-all-start = ((bf16[16,4,32,1152]{3,2,1,0:T(8,128)(2,1)}), bf16[16,4,32,1152]{3,2,1,0:T(8,128)(2,1)}, u32[]{:S(2)}, u32[]{:S(2)}) async-start(bf16[16,4,32,1152]{3,2,1,0:T(8,128)(2,1)} %bitcast.15), calls=%async_computation | async-start | bytes 9437184 | tf_op jit(solution)/shard_map/all_to_all | solution.py:364
  19.2 0.0 collective-permute-done.2.refs_3_
  19.2 0.0 collective-permute-done.1.refs_2_
  19.2 0.0 collective-permute-done.refs_1_
  19.2 0.6 copy-done.6
  19.8 0.1 copy-done.7
  19.9 0.6 copy-done.8
  20.5 1.9 %join_rows.1 = bf16[64,3712]{1,0:T(8,128)(2,1)} custom-call(bf16[16,3712]{1,0:T(8,128)(2,1)} %pack_rows.1.refs_0_, bf16[16,3712]{1,0:T(8,128)(2,1)} %copy-done.8, bf16[16,3712]{1,0:T(8,128)(2,1)} %copy-done.7, bf16[16,3712]{1,0:T(8,128)(2,1)} %copy-done.6), custom_call_target="tpu_custom_call" | custom-call | flops 299999985664 | tf_op jit(solution)/shard_map/join_rows/pallas_call | solution.py:168
  22.4 0.3 collective-permute-start.3
  22.7 33.2 %collective-permute-done.3 = bf16[64,3712]{1,0:T(8,128)(2,1)S(1)} collective-permute-done((bf16[64,3712]{1,0:T(8,128)(2,1)}, bf16[64,3712]{1,0:T(8,128)(2,1)S(1)}, u32[]{:S(2)}, u32[]{:S(2)}) %collective-permute-start.3) | collective-permute-done | bytes 475168 | tf_op jit(solution)/shard_map/ppermute | solution.py:178
  55.9 1.1 pad_maximum_fusion.kept_ref
  57.0 0.0 copy-start
  57.0 0.9 collective-permute-start.4
  57.9 2.1 %collective-permute-done.4.other_ref = bf16[128,3712]{1,0:T(8,128)(2,1)S(1)} collective-permute-done((bf16[128,3712]{1,0:T(8,128)(2,1)S(1)}, bf16[128,3712]{1,0:T(8,128)(2,1)S(1)}, u32[]{:S(2)}, u32[]{:S(2)}) %collective-permute-start.4) | collective-permute-done | bytes 950304 | tf_op jit(solution)/shard_map/ppermute | solution.py:178
  60.1 0.9 copy-done.3
  61.0 6.3 %expert_rows.1 = (f32[128,3584]{1,0:T(8,128)}, bf16[128,3584]{1,0:T(8,128)(2,1)}) custom-call(s32[1]{0:T(128)} %bitcast.label_ref, bf16[128,3712]{1,0:T(8,128)(2,1)} %copy-done, bf16[128,3712]{1,0:T(8,128)(2,1)} %copy-done.3, bf16[3584,256]{1,0:T(8,128)(2,1)} %bitcast.16, bf16[3584,256]{1,0:T(8,128)(2,1)} %bitcast.17, bf16[256,3584]{1,0:T(8,128)(2,1)} %bitcast.18), custom_call_target="tpu_custom_call" | custom-call | tf_op jit(solution)/shard_map/expert_rows/pallas_call | solution.py:212
  67.3 0.4 collective-permute-start.5
  67.8 0.1 dynamic_slice.3
  67.9 1.6 %reshape.108 = bf16[4,4,64,576]{3,2,1,0:T(8,128)(2,1)S(1)} reshape(bf16[16,36864]{1,0:T(8,128)(2,1)S(1)} %copy-done.2) | data formatting | bytes 2359296 | tf_op jit(solution)/shard_map/reshape | solution.py:375
  69.5 1.0 copy.18
  70.5 0.2 copy.19
  70.7 0.1 pad.4.query_ref
  70.8 0.0 collective-permute-done.5
  70.8 1.3 %copy-done.1 = f32[128,3584]{1,0:T(8,128)S(1)} copy-done((f32[128,3584]{1,0:T(8,128)S(1)}, f32[128,3584]{1,0:T(8,128)}, u32[]{:S(2)}) %copy-start.1) | copy-done | bytes 1835032
  72.2 1.4 %convert_add_fusion = f32[128,3584]{1,0:T(8,128)S(1)} fusion(f32[128,3584]{1,0:T(8,128)S(1)} %copy-done.1, bf16[128,3584]{1,0:T(8,128)(2,1)} %collective-permute-done.5), kind=kLoop, calls=%fused_computation | loop fusion | flops 917504 | bytes 4587520 | tf_op jit(solution)/shard_map/add | solution.py:386
  73.6 0.8 slice.42
  74.4 0.0 collective-permute-start.6
  74.4 0.1 iota_compare_fusion.1
  74.5 0.1 select_reduce_fusion
  74.7 0.1 reshape.106
  74.7 0.2 select_reduce_fusion.1
  74.9 24.4 %collective-permute-done.6 = bf16[64,3584]{1,0:T(8,128)(2,1)} collective-permute-done((bf16[64,3584]{1,0:T(8,128)(2,1)}, bf16[64,3584]{1,0:T(8,128)(2,1)}, u32[]{:S(2)}, u32[]{:S(2)}) %collective-permute-start.6) | collective-permute-done | bytes 458784 | tf_op jit(solution)/shard_map/ppermute | solution.py:178
  99.4 1.1 convert_add_fusion.1
  100.5 7.6 %collective-permute-start.7 = (bf16[32,3584]{1,0:T(8,128)(2,1)S(1)}, bf16[32,3584]{1,0:T(8,128)(2,1)S(1)}, u32[]{:S(2)}, u32[]{:S(2)}) collective-permute-start(bf16[32,3584]{1,0:T(8,128)(2,1)S(1)} %slice.43), channel_id=1, source_target_pairs={{0,4},{1,5},{2,6},{3,7},{4,0},{5,1},{6,2},{7,3},{8,12},{9,13},{10,... | collective-permute-start | bytes 688136 | tf_op jit(solution)/shard_map/ppermute | solution.py:178
  108.1 0.2 convert_reduce_fusion
  108.3 5.6 %collective-permute-done.7 = bf16[32,3584]{1,0:T(8,128)(2,1)S(1)} collective-permute-done((bf16[32,3584]{1,0:T(8,128)(2,1)S(1)}, bf16[32,3584]{1,0:T(8,128)(2,1)S(1)}, u32[]{:S(2)}, u32[]{:S(2)}) %collective-permute-start.7) | collective-permute-done | bytes 229408 | tf_op jit(solution)/shard_map/ppermute | solution.py:178
  113.9 0.1 slice_add_fusion
  113.9 8.9 %collective-permute-start.8 = (bf16[16,3584]{1,0:T(8,128)(2,1)S(1)}, bf16[16,3584]{1,0:T(8,128)(2,1)S(1)}, u32[]{:S(2)}, u32[]{:S(2)}) collective-permute-start(bf16[16,3584]{1,0:T(8,128)(2,1)S(1)} %slice.44), channel_id=1, source_target_pairs={{0,8},{1,9},{2,10},{3,11},{4,12},{5,13},{6,14},{7,15},{8,0},{9,1},... | collective-permute-start | bytes 344072 | tf_op jit(solution)/shard_map/ppermute | solution.py:178
  122.9 0.1 pad_add_fusion.plan_ref
  122.9 3.1 %all-to-all-done = bf16[16,4,32,1152]{3,2,1,0:T(8,128)(2,1)} async-done(((bf16[16,4,32,1152]{3,2,1,0:T(8,128)(2,1)}), bf16[16,4,32,1152]{3,2,1,0:T(8,128)(2,1)}, u32[]{:S(2)}, u32[]{:S(2)}) %all-to-all-start) | async-done | bytes 4718624 | tf_op jit(solution)/shard_map/all_to_all | solution.py:364
  126.1 7.9 %attend_pages.1 = bf16[16,32768]{1,0:T(8,128)(2,1)} custom-call(s32[72]{0:T(128)S(1)} %pad_add_fusion.plan_ref, bf16[4,256,640]{2,1,0:T(8,128)(2,1)S(1)} %pad.4.query_ref, bf16[64,32,1152]{2,1,0:T(8,128)(2,1)} %bitcast.12.pages_ref), custom_call_target="tpu_custom_call" | custom-call | tf_op jit(solution)/shard_map/attend_pages/pallas_call | solution.py:311
  133.9 0.0 collective-permute-done.8
  134.0 0.7 fusion.1
  (21 shorter events, 0.1 us)
Async XLA Ops:
  2.4 16.8 %collective-permute-start.2 = (bf16[16,3712]{1,0:T(8,128)(2,1)}, bf16[16,3712]{1,0:T(8,128)(2,1)S(1)}, u32[]{:S(2)}, u32[]{:S(2)}) collective-permute-start(bf16[16,3712]{1,0:T(8,128)(2,1)} %pack_rows.1.refs_0_), channel_id=1, source_target_pairs={{0,12},{1,13},{2,14},{3,15},{4,8},{5,9},{6,10},{7,11},{8,4},{9,5},... | collective-permute-start | bytes 356360 | tf_op jit(solution)/shard_map/ppermute | solution.py:178
  3.7 15.5 %collective-permute-start.1 = (bf16[16,3712]{1,0:T(8,128)(2,1)}, bf16[16,3712]{1,0:T(8,128)(2,1)S(1)}, u32[]{:S(2)}, u32[]{:S(2)}) collective-permute-start(bf16[16,3712]{1,0:T(8,128)(2,1)} %pack_rows.1.refs_0_), channel_id=1, source_target_pairs={{0,4},{1,5},{2,6},{3,7},{4,0},{5,1},{6,2},{7,3},{8,12},{9,13},{10,... | collective-permute-start | bytes 356360 | tf_op jit(solution)/shard_map/ppermute | solution.py:178
  5.9 13.3 %collective-permute-start = (bf16[16,3712]{1,0:T(8,128)(2,1)}, bf16[16,3712]{1,0:T(8,128)(2,1)S(1)}, u32[]{:S(2)}, u32[]{:S(2)}) collective-permute-start(bf16[16,3712]{1,0:T(8,128)(2,1)} %pack_rows.1.refs_0_), channel_id=1, source_target_pairs={{0,8},{1,9},{2,10},{3,11},{4,12},{5,13},{6,14},{7,15},{8,0},{9,1},... | collective-permute-start | bytes 356360 | tf_op jit(solution)/shard_map/ppermute | solution.py:178
  11.7 114.4 %all-to-all-start = ((bf16[16,4,32,1152]{3,2,1,0:T(8,128)(2,1)}), bf16[16,4,32,1152]{3,2,1,0:T(8,128)(2,1)}, u32[]{:S(2)}, u32[]{:S(2)}) async-start(bf16[16,4,32,1152]{3,2,1,0:T(8,128)(2,1)} %bitcast.15), calls=%async_computation | async-start | bytes 9437184 | tf_op jit(solution)/shard_map/all_to_all | solution.py:364
  19.2 0.6 copy-start.6
  19.2 0.7 copy-start.7
  19.9 0.7 copy-start.8
  22.4 33.5 %collective-permute-start.3 = (bf16[64,3712]{1,0:T(8,128)(2,1)}, bf16[64,3712]{1,0:T(8,128)(2,1)S(1)}, u32[]{:S(2)}, u32[]{:S(2)}) collective-permute-start(bf16[64,3712]{1,0:T(8,128)(2,1)} %join_rows.1), channel_id=1, source_target_pairs={{0,2},{1,3},{2,0},{3,1},{4,6},{5,7},{6,4},{7,5},{8,10},{9,11},{10,... | collective-permute-start | bytes 1425416 | tf_op jit(solution)/shard_map/ppermute | solution.py:178
  57.0 3.1 %copy-start = (bf16[128,3712]{1,0:T(8,128)(2,1)}, bf16[128,3712]{1,0:T(8,128)(2,1)S(1)}, u32[]{:S(2)}) copy-start(bf16[128,3712]{1,0:T(8,128)(2,1)S(1)} %pad_maximum_fusion.kept_ref) | copy-start | bytes 2850820
  57.0 3.1 %collective-permute-start.4 = (bf16[128,3712]{1,0:T(8,128)(2,1)S(1)}, bf16[128,3712]{1,0:T(8,128)(2,1)S(1)}, u32[]{:S(2)}, u32[]{:S(2)}) collective-permute-start(bf16[128,3712]{1,0:T(8,128)(2,1)S(1)} %pad_maximum_fusion.kept_ref), channel_id=1, source_target_pairs={{0,1},{1,0},{2,3},{3,2},{4,5},{5,4},{6,7},{7,6},{8,9},{9,8},{10,11... | collective-permute-start | bytes 2850824 | tf_op jit(solution)/shard_map/ppermute | solution.py:178
  60.1 0.9 copy-start.3
  61.0 6.8 %copy-start.9 = (s32[64]{0:T(128)S(1)}, s32[64]{0:T(128)}, u32[]{:S(2)}) copy-start(s32[64]{0:T(128)} %param.14) | copy-start | bytes 772
  61.0 6.9 %copy-start.2 = (bf16[16,36864]{1,0:T(8,128)(2,1)S(1)}, bf16[16,36864]{1,0:T(8,128)(2,1)}, u32[]{:S(2)}) copy-start(bf16[16,36864]{1,0:T(8,128)(2,1)} %param.11) | copy-start | bytes 3538948
  67.3 3.5 %collective-permute-start.5 = (bf16[128,3584]{1,0:T(8,128)(2,1)}, bf16[128,3584]{1,0:T(8,128)(2,1)}, u32[]{:S(2)}, u32[]{:S(2)}) collective-permute-start(bf16[128,3584]{1,0:T(8,128)(2,1)} %get-tuple-element.12), channel_id=1, source_target_pairs={{0,1},{1,0},{2,3},{3,2},{4,5},{5,4},{6,7},{7,6},{8,9},{9,8},{10,11... | collective-permute-start | bytes 2752520 | tf_op jit(solution)/shard_map/ppermute | solution.py:178
  70.7 1.5 %copy-start.1 = (f32[128,3584]{1,0:T(8,128)S(1)}, f32[128,3584]{1,0:T(8,128)}, u32[]{:S(2)}) copy-start(f32[128,3584]{1,0:T(8,128)} %get-tuple-element.11) | copy-start | bytes 5505028
  72.2 2.3 %copy-start.5 = (s32[64,16]{0,1:T(8,128)S(1)}, s32[64,16]{0,1:T(8,128)}, u32[]{:S(2)}) copy-start(s32[64,16]{0,1:T(8,128)} %param.13) | copy-start | bytes 12292
  72.2 2.6 %copy-start.10 = (s32[64]{0:T(128)S(1)}, s32[64]{0:T(128)}, u32[]{:S(2)}) copy-start(s32[64]{0:T(128)} %param.15) | copy-start | bytes 772
  74.4 24.9 %collective-permute-start.6 = (bf16[64,3584]{1,0:T(8,128)(2,1)}, bf16[64,3584]{1,0:T(8,128)(2,1)}, u32[]{:S(2)}, u32[]{:S(2)}) collective-permute-start(bf16[64,3584]{1,0:T(8,128)(2,1)} %slice.42), channel_id=1, source_target_pairs={{0,2},{1,3},{2,0},{3,1},{4,6},{5,7},{6,4},{7,5},{8,10},{9,11},{10,... | collective-permute-start | bytes 1376264 | tf_op jit(solution)/shard_map/ppermute | solution.py:178
  100.5 13.4 %collective-permute-start.7 = (bf16[32,3584]{1,0:T(8,128)(2,1)S(1)}, bf16[32,3584]{1,0:T(8,128)(2,1)S(1)}, u32[]{:S(2)}, u32[]{:S(2)}) collective-permute-start(bf16[32,3584]{1,0:T(8,128)(2,1)S(1)} %slice.43), channel_id=1, source_target_pairs={{0,4},{1,5},{2,6},{3,7},{4,0},{5,1},{6,2},{7,3},{8,12},{9,13},{10,... | collective-permute-start | bytes 688136 | tf_op jit(solution)/shard_map/ppermute | solution.py:178
  113.9 20.0 %collective-permute-start.8 = (bf16[16,3584]{1,0:T(8,128)(2,1)S(1)}, bf16[16,3584]{1,0:T(8,128)(2,1)S(1)}, u32[]{:S(2)}, u32[]{:S(2)}) collective-permute-start(bf16[16,3584]{1,0:T(8,128)(2,1)S(1)} %slice.44), channel_id=1, source_target_pairs={{0,8},{1,9},{2,10},{3,11},{4,12},{5,13},{6,14},{7,15},{8,0},{9,1},... | collective-permute-start | bytes 344072 | tf_op jit(solution)/shard_map/ppermute | solution.py:178
  126.1 7.9 %copy-start.4 = (bf16[16,3584]{1,0:T(8,128)(2,1)S(1)}, bf16[16,3584]{1,0:T(8,128)(2,1)}, u32[]{:S(2)}) copy-start(bf16[16,3584]{1,0:T(8,128)(2,1)} %rows_ref.1) | copy-start | bytes 344068

commit v6 on v5

--- a/solution.py
+++ b/solution.py
@@ -30,20 +30,27 @@
 
 
 def stage_body(
-    peers, device_ref, table_ref, serving_ref, pool_ref, out_ref, pool, pages, order, index, *sems
+    peers, group, table_ref, serving_ref, pool_ref, out_ref, pool, pages, order, index, *sems
 ):
-    pool_sem, order_sem, page_sems = sems
+    table, serving, pool_sem, order_sem, table_sems, page_sems = sems
     fetch = pltpu.make_async_copy(pool_ref, pool, pool_sem)
+    fetch_table = pltpu.make_async_copy(table_ref, table, table_sems.at[0])
+    fetch_serving = pltpu.make_async_copy(serving_ref, serving, table_sems.at[1])
+    fetch_table.start()
+    fetch_serving.start()
     fetch.start()
-    each, slots = table_ref.shape
+    each, slots = table.shape
     span = slots // peers
     fetched = out_ref.shape[0] // peers
+    fetch_table.wait()
+    fetch_serving.wait()
     held = jnp.full((each, slots), pool.shape[0], jnp.int32)
-    table = table_ref[...]
-    named = ones_where(lax.broadcasted_iota(jnp.int32, (slots, slots), 0) == serving_ref[...])
-    owner = count(lax.div(table, held).astype(jnp.float32).astype(jnp.bfloat16), named)
-    place = count(lax.rem(table, held).astype(jnp.float32).astype(jnp.bfloat16), named)
-    mine = owner == device_ref[0].astype(jnp.float32)
+    listed = table[...]
+    named = ones_where(lax.broadcasted_iota(jnp.int32, (slots, slots), 0) == serving[...])
+    owner = count(lax.div(listed, held).astype(jnp.float32).astype(jnp.bfloat16), named)
+    place = count(lax.rem(listed, held).astype(jnp.float32).astype(jnp.bfloat16), named)
+    device = lax.axis_index(group[0]) * lax.axis_size(group[1]) + lax.axis_index(group[1])
+    mine = owner == device.astype(jnp.float32)
     flags = ones_where(mine)
     above = lax.broadcasted_iota(jnp.int32, (each, each), 1) < lax.broadcasted_iota(
         jnp.int32, (each, each), 0
@@ -91,33 +98,31 @@
     lax.fori_loop(0, peers, finish, 0)
 
 
-def stage_pages(device, table, serving, pool, peers, slots):
+def stage_pages(group, table, serving, pool, peers, slots):
     pairs = pool.shape[1] // (2 * LAT)
     fetched = slots // peers
     listing = (fetched + -fetched % 8, peers + -peers % 128)
     return pl.pallas_call(
-        functools.partial(stage_body, peers),
+        functools.partial(stage_body, peers, group),
         out_shape=jax.ShapeDtypeStruct((slots, pairs, 2 * LAT), pool.dtype),
-        in_specs=[
-            pl.BlockSpec(memory_space=pltpu.SMEM),
-            pl.BlockSpec(memory_space=pltpu.VMEM),
-            pl.BlockSpec(memory_space=pltpu.VMEM),
-            pl.BlockSpec(memory_space=pltpu.HBM),
-        ],
+        in_specs=[pl.BlockSpec(memory_space=pltpu.HBM)] * 3,
         out_specs=pl.BlockSpec(memory_space=pltpu.HBM),
         scratch_shapes=[
             pltpu.VMEM(pool.shape, pool.dtype),
             pltpu.VMEM((pool.shape[0], pairs, 2 * LAT), pool.dtype),
             pltpu.VMEM(listing, jnp.int32),
             pltpu.SMEM(listing, jnp.int32),
+            pltpu.VMEM(table.shape, table.dtype),
+            pltpu.VMEM(serving.shape, serving.dtype),
             pltpu.SemaphoreType.DMA,
             pltpu.SemaphoreType.DMA,
+            pltpu.SemaphoreType.DMA((2,)),
             pltpu.SemaphoreType.DMA((slots,)),
         ],
         compiler_params=pltpu.CompilerParams(vmem_limit_bytes=56 << 20),
         cost_estimate=pl.CostEstimate(flops=STAGE_FLOPS, bytes_accessed=0, transcendentals=0),
         name="stage_pages",
-    )(device, table, serving, pool)
+    )(table, serving, pool)
 
 
 def pack_body(experts, routes_ref, scores_ref, rows_ref, out_ref):
@@ -355,17 +360,19 @@
     experts = n_ep // 2
     packed = pack_rows(routes.T, route_scores.T, residual, experts)
     far, near = peers // 2, peers // 4
-    across = [exchange(packed, group, bit) for bit in (far, near, far | near)]
+    across = {bit: exchange(packed, group, bit) for bit in (far,)}
 
     outgoing = stage_pages(
-        device.reshape(1), page_table.T, serving.reshape(1, -1), page_pool, peers, listed
-    )
+        group, page_table.T, serving.reshape(1, -1), page_pool, peers, listed
+    )
+    later, outgoing = lax.optimization_barrier((packed, outgoing))
+    across |= {bit: exchange(later, group, bit) for bit in (near, far | near,)}
     pairs = outgoing.shape[1]
     arrived = lax.all_to_all(
         outgoing.reshape(peers, fetched, pairs, 2 * LAT), group, split_axis=0, concat_axis=0, tiled=True
     )
 
-    kept = join_rows([packed, *across])
+    kept = join_rows([packed, across[far], across[near], across[far | near]])
     bit = near // 2
     while bit > 1:
         kept = jnp.concatenate([kept, exchange(kept, group, bit)], axis=0)

time: 135 us -> 134 us (level)
    unnamed x22 -> x24, local copies, waits for them, and re-layouts: 3.61 us -> 3.6 us
where the time goes in v6:
time: 134 us; the launch traced here: 133 us
  waiting for transfers between devices  68.5 us (51%)
  starting transfers between devices  28.3 us (21%)
  Pallas kernels  23 us (17%)
  local copies, waits for them, and re-layouts  7.54 us (6%)
  other arithmetic  5.04 us (4%)
    ppermute x9, waiting for transfers between devices, exchange(): return lax.ppermute(block, group, [(d, d ^ bit) for d in range(peers)])  65.4 us
    ppermute x9, starting transfers between devices, exchange(): return lax.ppermute(block, group, [(d, d ^ bit) for d in range(peers)])  21.8 us
    pallas_call x1, Pallas kernels, attend(): pl.pallas_call(attend_body, out_shape=jax.ShapeDtypeStruct(out, jnp.bfloa...  7.8 us
    all_to_all x1, starting transfers between devices, local(): lax.all_to_all(outgoing.reshape(peers, fetched, pairs, 2 * LAT), group, s...  6.5 us
    pallas_call x1, Pallas kernels, expert_rows(): pl.pallas_call(functools.partial(expert_body, experts), out_shape=(jax.Sh...  6.34 us
    pallas_call x1, Pallas kernels, stage_pages(): pl.pallas_call(functools.partial(stage_body, peers, group), out_shape=jax...  5.17 us
    unnamed x24, local copies, waits for them, and re-layouts  3.6 us
    all_to_all x1, waiting for transfers between devices, local(): lax.all_to_all(outgoing.reshape(peers, fetched, pairs, 2 * LAT), group, s...  3.13 us
  transfers between devices with their start and end apart: 10, of which 5 were waited for; matrix products, arithmetic and copies ran while one was open for 6% of the time, Pallas kernels for 16%

profile of v6, /device:TPU:15, one launch (start us, length us, event | category | flops | bytes accessed | tf_op | source)
XLA Modules:
  0.0 133.1 jit_solution(17695624695028244339)
XLA Ops:
  0.6 1.8 %pack_rows.1.refs_0_ = bf16[16,3712]{1,0:T(8,128)(2,1)} custom-call(s32[2,16]{1,0:T(2,128)} %bitcast.19, f32[2,16]{1,0:T(2,128)} %bitcast.20, bf16[16,3584]{1,0:T(8,128)(2,1)} %rows_ref.1), custom_call_target="tpu_custom_call" | custom-call | tf_op jit(solution)/shard_map/pack_rows/pallas_call | solution.py:156
  2.4 2.3 %collective-permute-start = (bf16[16,3712]{1,0:T(8,128)(2,1)}, bf16[16,3712]{1,0:T(8,128)(2,1)S(1)}, u32[]{:S(2)}, u32[]{:S(2)}) collective-permute-start(bf16[16,3712]{1,0:T(8,128)(2,1)} %pack_rows.1.refs_0_), channel_id=1, source_target_pairs={{0,8},{1,9},{2,10},{3,11},{4,12},{5,13},{6,14},{7,15},{8,0},{9,1},... | collective-permute-start | bytes 356360 | tf_op jit(solution)/shard_map/ppermute | solution.py:183
  4.7 5.2 %stage_pages.1 = bf16[64,32,1152]{2,1,0:T(8,128)(2,1)} custom-call(s32[16,64]{1,0:T(8,128)} %bitcast.18, s32[1,64]{1,0:T(1,128)} %bitcast.21, bf16[32,36864]{1,0:T(8,128)(2,1)} %pool_ref.1), custom_call_target="tpu_custom_call" | custom-call | flops 20000000000 | tf_op jit(solution)/shard_map/stage_pages/pallas_call | solution.py:105
  9.9 0.1 collective-permute-start.2
  10.0 1.2 collective-permute-start.1
  11.2 6.5 %all-to-all-start = ((bf16[16,4,32,1152]{3,2,1,0:T(8,128)(2,1)}), bf16[16,4,32,1152]{3,2,1,0:T(8,128)(2,1)}, u32[]{:S(2)}, u32[]{:S(2)}) async-start(bf16[16,4,32,1152]{3,2,1,0:T(8,128)(2,1)} %bitcast.14), calls=%async_computation | async-start | bytes 9437184 | tf_op jit(solution)/shard_map/all_to_all | solution.py:371
  17.7 0.0 collective-permute-done.refs_1_
  17.7 0.0 collective-permute-done.2.refs_3_
  17.7 0.0 collective-permute-done.1.refs_2_
  17.8 0.6 copy-done.7
  18.4 0.0 copy-done.8
  18.4 0.6 copy-done.9
  19.1 1.9 %join_rows.1 = bf16[64,3712]{1,0:T(8,128)(2,1)} custom-call(bf16[16,3712]{1,0:T(8,128)(2,1)} %pack_rows.1.refs_0_, bf16[16,3712]{1,0:T(8,128)(2,1)} %copy-done.7, bf16[16,3712]{1,0:T(8,128)(2,1)} %copy-done.9, bf16[16,3712]{1,0:T(8,128)(2,1)} %copy-done.8), custom_call_target="tpu_custom_call" | custom-call | flops 299999985664 | tf_op jit(solution)/shard_map/join_rows/pallas_call | solution.py:173
  20.9 0.3 collective-permute-start.3
  21.2 33.2 %collective-permute-done.3 = bf16[64,3712]{1,0:T(8,128)(2,1)S(1)} collective-permute-done((bf16[64,3712]{1,0:T(8,128)(2,1)}, bf16[64,3712]{1,0:T(8,128)(2,1)S(1)}, u32[]{:S(2)}, u32[]{:S(2)}) %collective-permute-start.3) | collective-permute-done | bytes 475168 | tf_op jit(solution)/shard_map/ppermute | solution.py:183
  54.4 1.1 pad_maximum_fusion.kept_ref
  55.5 0.0 copy-start
  55.5 0.9 collective-permute-start.4
  56.5 2.1 %collective-permute-done.4.other_ref = bf16[128,3712]{1,0:T(8,128)(2,1)S(1)} collective-permute-done((bf16[128,3712]{1,0:T(8,128)(2,1)S(1)}, bf16[128,3712]{1,0:T(8,128)(2,1)S(1)}, u32[]{:S(2)}, u32[]{:S(2)}) %collective-permute-start.4) | collective-permute-done | bytes 950304 | tf_op jit(solution)/shard_map/ppermute | solution.py:183
  58.6 0.9 copy-done.3
  59.5 6.3 %expert_rows.1 = (f32[128,3584]{1,0:T(8,128)}, bf16[128,3584]{1,0:T(8,128)(2,1)}) custom-call(s32[1]{0:T(128)} %bitcast.label_ref, bf16[128,3712]{1,0:T(8,128)(2,1)} %copy-done, bf16[128,3712]{1,0:T(8,128)(2,1)} %copy-done.3, bf16[3584,256]{1,0:T(8,128)(2,1)} %bitcast.15, bf16[3584,256]{1,0:T(8,128)(2,1)} %bitcast.16, bf16[256,3584]{1,0:T(8,128)(2,1)} %bitcast.17), custom_call_target="tpu_custom_call" | custom-call | tf_op jit(solution)/shard_map/expert_rows/pallas_call | solution.py:217
  65.9 0.4 collective-permute-start.5
  66.3 0.1 dynamic_slice.3
  66.4 1.6 %reshape.106 = bf16[4,4,64,576]{3,2,1,0:T(8,128)(2,1)S(1)} reshape(bf16[16,36864]{1,0:T(8,128)(2,1)S(1)} %copy-done.2) | data formatting | bytes 2359296 | tf_op jit(solution)/shard_map/reshape | solution.py:382
  68.1 1.0 copy.18
  69.1 0.2 copy.19
  69.2 0.1 pad.4.query_ref
  69.4 0.0 collective-permute-done.5
  69.4 1.3 %copy-done.1 = f32[128,3584]{1,0:T(8,128)S(1)} copy-done((f32[128,3584]{1,0:T(8,128)S(1)}, f32[128,3584]{1,0:T(8,128)}, u32[]{:S(2)}) %copy-start.1) | copy-done | bytes 1835032
  70.7 1.4 %convert_add_fusion = f32[128,3584]{1,0:T(8,128)S(1)} fusion(f32[128,3584]{1,0:T(8,128)S(1)} %copy-done.1, bf16[128,3584]{1,0:T(8,128)(2,1)} %collective-permute-done.5), kind=kLoop, calls=%fused_computation | loop fusion | flops 917504 | bytes 4587520 | tf_op jit(solution)/shard_map/add | solution.py:393
  72.2 0.8 slice.42
  73.0 0.0 collective-permute-start.6
  73.0 0.1 iota_compare_fusion.1
  73.1 0.1 select_reduce_fusion
  73.2 0.1 reshape.103
  73.3 0.2 select_reduce_fusion.1
  73.5 24.4 %collective-permute-done.6 = bf16[64,3584]{1,0:T(8,128)(2,1)} collective-permute-done((bf16[64,3584]{1,0:T(8,128)(2,1)}, bf16[64,3584]{1,0:T(8,128)(2,1)}, u32[]{:S(2)}, u32[]{:S(2)}) %collective-permute-start.6) | collective-permute-done | bytes 458784 | tf_op jit(solution)/shard_map/ppermute | solution.py:183
  97.9 1.1 convert_add_fusion.1
  99.1 7.6 %collective-permute-start.7 = (bf16[32,3584]{1,0:T(8,128)(2,1)S(1)}, bf16[32,3584]{1,0:T(8,128)(2,1)S(1)}, u32[]{:S(2)}, u32[]{:S(2)}) collective-permute-start(bf16[32,3584]{1,0:T(8,128)(2,1)S(1)} %slice.43), channel_id=1, source_target_pairs={{0,4},{1,5},{2,6},{3,7},{4,0},{5,1},{6,2},{7,3},{8,12},{9,13},{10,... | collective-permute-start | bytes 688136 | tf_op jit(solution)/shard_map/ppermute | solution.py:183
  106.7 0.2 convert_reduce_fusion
  106.9 5.6 %collective-permute-done.7 = bf16[32,3584]{1,0:T(8,128)(2,1)S(1)} collective-permute-done((bf16[32,3584]{1,0:T(8,128)(2,1)S(1)}, bf16[32,3584]{1,0:T(8,128)(2,1)S(1)}, u32[]{:S(2)}, u32[]{:S(2)}) %collective-permute-start.7) | collective-permute-done | bytes 229408 | tf_op jit(solution)/shard_map/ppermute | solution.py:183
  112.4 0.1 slice_add_fusion
  112.5 8.9 %collective-permute-start.8 = (bf16[16,3584]{1,0:T(8,128)(2,1)S(1)}, bf16[16,3584]{1,0:T(8,128)(2,1)S(1)}, u32[]{:S(2)}, u32[]{:S(2)}) collective-permute-start(bf16[16,3584]{1,0:T(8,128)(2,1)S(1)} %slice.44), channel_id=1, source_target_pairs={{0,8},{1,9},{2,10},{3,11},{4,12},{5,13},{6,14},{7,15},{8,0},{9,1},... | collective-permute-start | bytes 344072 | tf_op jit(solution)/shard_map/ppermute | solution.py:183
  121.4 0.1 pad_add_fusion.plan_ref
  121.5 3.1 %all-to-all-done = bf16[16,4,32,1152]{3,2,1,0:T(8,128)(2,1)} async-done(((bf16[16,4,32,1152]{3,2,1,0:T(8,128)(2,1)}), bf16[16,4,32,1152]{3,2,1,0:T(8,128)(2,1)}, u32[]{:S(2)}, u32[]{:S(2)}) %all-to-all-start) | async-done | bytes 4718624 | tf_op jit(solution)/shard_map/all_to_all | solution.py:371
  124.6 7.8 %attend_pages.1 = bf16[16,32768]{1,0:T(8,128)(2,1)} custom-call(s32[72]{0:T(128)S(1)} %pad_add_fusion.plan_ref, bf16[4,256,640]{2,1,0:T(8,128)(2,1)S(1)} %pad.4.query_ref, bf16[64,32,1152]{2,1,0:T(8,128)(2,1)} %bitcast.11.pages_ref), custom_call_target="tpu_custom_call" | custom-call | tf_op jit(solution)/shard_map/attend_pages/pallas_call | solution.py:316
  132.4 0.0 collective-permute-done.8
  132.5 0.7 fusion.1
  (23 shorter events, 0.1 us)
Async XLA Ops:
  2.4 15.3 %collective-permute-start = (bf16[16,3712]{1,0:T(8,128)(2,1)}, bf16[16,3712]{1,0:T(8,128)(2,1)S(1)}, u32[]{:S(2)}, u32[]{:S(2)}) collective-permute-start(bf16[16,3712]{1,0:T(8,128)(2,1)} %pack_rows.1.refs_0_), channel_id=1, source_target_pairs={{0,8},{1,9},{2,10},{3,11},{4,12},{5,13},{6,14},{7,15},{8,0},{9,1},... | collective-permute-start | bytes 356360 | tf_op jit(solution)/shard_map/ppermute | solution.py:183
  4.7 5.2 %copy-start.5 = (bf16[16,3712]{1,0:T(8,128)(2,1)S(1)}, bf16[16,3712]{1,0:T(8,128)(2,1)}, u32[]{:S(2)}) copy-start(bf16[16,3712]{1,0:T(8,128)(2,1)} %pack_rows.1.refs_0_) | copy-start | bytes 356356
  9.9 7.8 %collective-permute-start.2 = (bf16[16,3712]{1,0:T(8,128)(2,1)S(1)}, bf16[16,3712]{1,0:T(8,128)(2,1)S(1)}, u32[]{:S(2)}, u32[]{:S(2)}) collective-permute-start(bf16[16,3712]{1,0:T(8,128)(2,1)S(1)} %copy-done.5), channel_id=1, source_target_pairs={{0,12},{1,13},{2,14},{3,15},{4,8},{5,9},{6,10},{7,11},{8,4},{9,5},... | collective-permute-start | bytes 356360 | tf_op jit(solution)/shard_map/ppermute | solution.py:183
  10.0 7.8 %collective-permute-start.1 = (bf16[16,3712]{1,0:T(8,128)(2,1)S(1)}, bf16[16,3712]{1,0:T(8,128)(2,1)S(1)}, u32[]{:S(2)}, u32[]{:S(2)}) collective-permute-start(bf16[16,3712]{1,0:T(8,128)(2,1)S(1)} %copy-done.5), channel_id=1, source_target_pairs={{0,4},{1,5},{2,6},{3,7},{4,0},{5,1},{6,2},{7,3},{8,12},{9,13},{10,... | collective-permute-start | bytes 356360 | tf_op jit(solution)/shard_map/ppermute | solution.py:183
  11.2 113.4 %all-to-all-start = ((bf16[16,4,32,1152]{3,2,1,0:T(8,128)(2,1)}), bf16[16,4,32,1152]{3,2,1,0:T(8,128)(2,1)}, u32[]{:S(2)}, u32[]{:S(2)}) async-start(bf16[16,4,32,1152]{3,2,1,0:T(8,128)(2,1)} %bitcast.14), calls=%async_computation | async-start | bytes 9437184 | tf_op jit(solution)/shard_map/all_to_all | solution.py:371
  17.7 0.7 copy-start.7
  17.7 0.7 copy-start.8
  18.4 0.6 copy-start.9
  20.9 33.5 %collective-permute-start.3 = (bf16[64,3712]{1,0:T(8,128)(2,1)}, bf16[64,3712]{1,0:T(8,128)(2,1)S(1)}, u32[]{:S(2)}, u32[]{:S(2)}) collective-permute-start(bf16[64,3712]{1,0:T(8,128)(2,1)} %join_rows.1), channel_id=1, source_target_pairs={{0,2},{1,3},{2,0},{3,1},{4,6},{5,7},{6,4},{7,5},{8,10},{9,11},{10,... | collective-permute-start | bytes 1425416 | tf_op jit(solution)/shard_map/ppermute | solution.py:183
  55.5 3.1 %copy-start = (bf16[128,3712]{1,0:T(8,128)(2,1)}, bf16[128,3712]{1,0:T(8,128)(2,1)S(1)}, u32[]{:S(2)}) copy-start(bf16[128,3712]{1,0:T(8,128)(2,1)S(1)} %pad_maximum_fusion.kept_ref) | copy-start | bytes 2850820
  55.5 3.1 %collective-permute-start.4 = (bf16[128,3712]{1,0:T(8,128)(2,1)S(1)}, bf16[128,3712]{1,0:T(8,128)(2,1)S(1)}, u32[]{:S(2)}, u32[]{:S(2)}) collective-permute-start(bf16[128,3712]{1,0:T(8,128)(2,1)S(1)} %pad_maximum_fusion.kept_ref), channel_id=1, source_target_pairs={{0,1},{1,0},{2,3},{3,2},{4,5},{5,4},{6,7},{7,6},{8,9},{9,8},{10,11... | collective-permute-start | bytes 2850824 | tf_op jit(solution)/shard_map/ppermute | solution.py:183
  58.6 0.9 copy-start.3
  59.5 6.8 %copy-start.10 = (s32[64]{0:T(128)S(1)}, s32[64]{0:T(128)}, u32[]{:S(2)}) copy-start(s32[64]{0:T(128)} %param.14) | copy-start | bytes 772
  59.5 6.9 %copy-start.2 = (bf16[16,36864]{1,0:T(8,128)(2,1)S(1)}, bf16[16,36864]{1,0:T(8,128)(2,1)}, u32[]{:S(2)}) copy-start(bf16[16,36864]{1,0:T(8,128)(2,1)} %param.11) | copy-start | bytes 3538948
  65.9 3.5 %collective-permute-start.5 = (bf16[128,3584]{1,0:T(8,128)(2,1)}, bf16[128,3584]{1,0:T(8,128)(2,1)}, u32[]{:S(2)}, u32[]{:S(2)}) collective-permute-start(bf16[128,3584]{1,0:T(8,128)(2,1)} %get-tuple-element.15), channel_id=1, source_target_pairs={{0,1},{1,0},{2,3},{3,2},{4,5},{5,4},{6,7},{7,6},{8,9},{9,8},{10,11... | collective-permute-start | bytes 2752520 | tf_op jit(solution)/shard_map/ppermute | solution.py:183
  69.2 1.5 %copy-start.1 = (f32[128,3584]{1,0:T(8,128)S(1)}, f32[128,3584]{1,0:T(8,128)}, u32[]{:S(2)}) copy-start(f32[128,3584]{1,0:T(8,128)} %get-tuple-element.14) | copy-start | bytes 5505028
  70.7 2.3 %copy-start.6 = (s32[64,16]{0,1:T(8,128)S(1)}, s32[64,16]{0,1:T(8,128)}, u32[]{:S(2)}) copy-start(s32[64,16]{0,1:T(8,128)} %param.13) | copy-start | bytes 12292
  70.7 2.6 %copy-start.11 = (s32[64]{0:T(128)S(1)}, s32[64]{0:T(128)}, u32[]{:S(2)}) copy-start(s32[64]{0:T(128)} %param.15) | copy-start | bytes 772
  73.0 24.9 %collective-permute-start.6 = (bf16[64,3584]{1,0:T(8,128)(2,1)}, bf16[64,3584]{1,0:T(8,128)(2,1)}, u32[]{:S(2)}, u32[]{:S(2)}) collective-permute-start(bf16[64,3584]{1,0:T(8,128)(2,1)} %slice.42), channel_id=1, source_target_pairs={{0,2},{1,3},{2,0},{3,1},{4,6},{5,7},{6,4},{7,5},{8,10},{9,11},{10,... | collective-permute-start | bytes 1376264 | tf_op jit(solution)/shard_map/ppermute | solution.py:183
  99.1 13.4 %collective-permute-start.7 = (bf16[32,3584]{1,0:T(8,128)(2,1)S(1)}, bf16[32,3584]{1,0:T(8,128)(2,1)S(1)}, u32[]{:S(2)}, u32[]{:S(2)}) collective-permute-start(bf16[32,3584]{1,0:T(8,128)(2,1)S(1)} %slice.43), channel_id=1, source_target_pairs={{0,4},{1,5},{2,6},{3,7},{4,0},{5,1},{6,2},{7,3},{8,12},{9,13},{10,... | collective-permute-start | bytes 688136 | tf_op jit(solution)/shard_map/ppermute | solution.py:183
  112.5 19.9 %collective-permute-start.8 = (bf16[16,3584]{1,0:T(8,128)(2,1)S(1)}, bf16[16,3584]{1,0:T(8,128)(2,1)S(1)}, u32[]{:S(2)}, u32[]{:S(2)}) collective-permute-start(bf16[16,3584]{1,0:T(8,128)(2,1)S(1)} %slice.44), channel_id=1, source_target_pairs={{0,8},{1,9},{2,10},{3,11},{4,12},{5,13},{6,14},{7,15},{8,0},{9,1},... | collective-permute-start | bytes 344072 | tf_op jit(solution)/shard_map/ppermute | solution.py:183
  124.6 7.8 %copy-start.4 = (bf16[16,3584]{1,0:T(8,128)(2,1)S(1)}, bf16[16,3584]{1,0:T(8,128)(2,1)}, u32[]{:S(2)}) copy-start(bf16[16,3584]{1,0:T(8,128)(2,1)} %rows_ref.1) | copy-start | bytes 344068

commit v7 on v6

--- a/solution.py
+++ b/solution.py
@@ -29,15 +29,46 @@
     return jnp.dot(left, right, preferred_element_type=jnp.float32)
 
 
-def stage_body(
-    peers, group, table_ref, serving_ref, pool_ref, out_ref, pool, pages, order, index, *sems
-):
-    table, serving, pool_sem, order_sem, table_sems, page_sems = sems
+def weigh(routes, scores, experts, lanes):
+    top, rows = routes.shape
+    scaled = scores / jnp.sum(scores, axis=0, keepdims=True) * 2.5
+    labels = lax.broadcasted_iota(jnp.int32, (experts, rows), 0)
+    weights = jnp.zeros((experts, rows), jnp.float32)
+    for k in range(top):
+        weights += jnp.where(labels == routes[k : k + 1, :], scaled[k : k + 1, :], 0.0)
+    side = jnp.zeros((rows, lanes), jnp.float32)
+    line = lax.broadcasted_iota(jnp.int32, (experts, lanes), 1)
+    entry = lax.broadcasted_iota(jnp.int32, (experts, lanes), 0)
+    for part in range(3):
+        piece = weights.astype(jnp.bfloat16)
+        weights = weights - piece.astype(jnp.float32)
+        side += lax.dot_general(
+            piece,
+            ones_where(line == entry + part * experts),
+            (((0,), (0,)), ((), ())),
+            preferred_element_type=jnp.float32,
+        )
+    return side.astype(jnp.bfloat16)
+
+
+def stage_body(peers, group, experts, table_ref, serving_ref, pool_ref, *refs):
+    rows_hbm, routes_hbm, scores_hbm, out_ref, packed_ref, *refs = refs
+    pool, pages, order, index, table, serving, packed, routes, scores, *sems = refs
+    pool_sem, order_sem, table_sems, row_sems, page_sems = sems
+    width = rows_hbm.shape[1]
     fetch = pltpu.make_async_copy(pool_ref, pool, pool_sem)
     fetch_table = pltpu.make_async_copy(table_ref, table, table_sems.at[0])
     fetch_serving = pltpu.make_async_copy(serving_ref, serving, table_sems.at[1])
+    fetch_rows = [
+        pltpu.make_async_copy(routes_hbm, routes, row_sems.at[0]),
+        pltpu.make_async_copy(scores_hbm, scores, row_sems.at[1]),
+        pltpu.make_async_copy(rows_hbm, packed.at[:, :width], row_sems.at[2]),
+    ]
+    send_rows = pltpu.make_async_copy(packed, packed_ref, row_sems.at[3])
     fetch_table.start()
     fetch_serving.start()
+    for fetch_row in fetch_rows:
+        fetch_row.start()
     fetch.start()
     each, slots = table.shape
     span = slots // peers
@@ -76,6 +107,10 @@
         order[k : k + 1, :peers] = column[:1].astype(jnp.int32)
     listing = pltpu.make_async_copy(order, index, order_sem)
     listing.start()
+    for fetch_row in fetch_rows:
+        fetch_row.wait()
+    packed[:, width:] = weigh(routes[...], scores[...], experts, packed.shape[1] - width)
+    send_rows.start()
     fetch.wait()
     pages[...] = pool[...].reshape(pages.shape)
     listing.wait()
@@ -95,18 +130,24 @@
         return carry
 
     lax.fori_loop(0, peers, begin, 0)
+    send_rows.wait()
     lax.fori_loop(0, peers, finish, 0)
 
 
-def stage_pages(group, table, serving, pool, peers, slots):
+def stage_pages(group, table, serving, pool, rows, routes, scores, peers, slots, experts):
+    side = 3 * experts
+    packed = (rows.shape[0], rows.shape[1] + side + -side % 128)
     pairs = pool.shape[1] // (2 * LAT)
     fetched = slots // peers
     listing = (fetched + -fetched % 8, peers + -peers % 128)
     return pl.pallas_call(
-        functools.partial(stage_body, peers, group),
-        out_shape=jax.ShapeDtypeStruct((slots, pairs, 2 * LAT), pool.dtype),
-        in_specs=[pl.BlockSpec(memory_space=pltpu.HBM)] * 3,
-        out_specs=pl.BlockSpec(memory_space=pltpu.HBM),
+        functools.partial(stage_body, peers, group, experts),
+        out_shape=(
+            jax.ShapeDtypeStruct((slots, pairs, 2 * LAT), pool.dtype),
+            jax.ShapeDtypeStruct(packed, rows.dtype),
+        ),
+        in_specs=[pl.BlockSpec(memory_space=pltpu.HBM)] * 6,
+        out_specs=(pl.BlockSpec(memory_space=pltpu.HBM),) * 2,
         scratch_shapes=[
             pltpu.VMEM(pool.shape, pool.dtype),
             pltpu.VMEM((pool.shape[0], pairs, 2 * LAT), pool.dtype),
@@ -114,50 +155,19 @@
             pltpu.SMEM(listing, jnp.int32),
             pltpu.VMEM(table.shape, table.dtype),
             pltpu.VMEM(serving.shape, serving.dtype),
+            pltpu.VMEM(packed, rows.dtype),
+            pltpu.VMEM(routes.shape, routes.dtype),
+            pltpu.VMEM(scores.shape, scores.dtype),
             pltpu.SemaphoreType.DMA,
             pltpu.SemaphoreType.DMA,
             pltpu.SemaphoreType.DMA((2,)),
+            pltpu.SemaphoreType.DMA((4,)),
             pltpu.SemaphoreType.DMA((slots,)),
         ],
         compiler_params=pltpu.CompilerParams(vmem_limit_bytes=56 << 20),
         cost_estimate=pl.CostEstimate(flops=STAGE_FLOPS, bytes_accessed=0, transcendentals=0),
         name="stage_pages",
-    )(table, serving, pool)
-
-
-def pack_body(experts, routes_ref, scores_ref, rows_ref, out_ref):
-    top, rows = routes_ref.shape
-    width = rows_ref.shape[1]
-    scores = scores_ref[...]
-    scaled = scores / jnp.sum(scores, axis=0, keepdims=True) * 2.5
-    labels = lax.broadcasted_iota(jnp.int32, (experts, rows), 0)
-    weights = jnp.zeros((experts, rows), jnp.float32)
-    for k in range(top):
-        weights += jnp.where(labels == routes_ref[k : k + 1, :], scaled[k : k + 1, :], 0.0)
-    out_ref[:, :width] = rows_ref[...]
-    side = jnp.zeros((rows, out_ref.shape[1] - width), jnp.float32)
-    line = lax.broadcasted_iota(jnp.int32, (experts, side.shape[1]), 1)
-    entry = lax.broadcasted_iota(jnp.int32, (experts, side.shape[1]), 0)
-    for part in range(3):
-        piece = weights.astype(jnp.bfloat16)
-        weights = weights - piece.astype(jnp.float32)
-        side += lax.dot_general(
-            piece,
-            ones_where(line == entry + part * experts),
-            (((0,), (0,)), ((), ())),
-            preferred_element_type=jnp.float32,
-        )
-    out_ref[:, width:] = side.astype(out_ref.dtype)
-
-
-def pack_rows(routes, scores, rows, experts):
-    side = 3 * experts
-    width = rows.shape[1] + side + -side % 128
-    return pl.pallas_call(
-        functools.partial(pack_body, experts),
-        out_shape=jax.ShapeDtypeStruct((rows.shape[0], width), rows.dtype),
-        name="pack_rows",
-    )(routes, scores, rows)
+    )(table, serving, pool, rows, routes, scores)
 
 
 def join_body(*refs):
@@ -358,21 +368,27 @@
 
     n_ep = lax.axis_size("ep")
     experts = n_ep // 2
-    packed = pack_rows(routes.T, route_scores.T, residual, experts)
     far, near = peers // 2, peers // 4
-    across = {bit: exchange(packed, group, bit) for bit in (far,)}
-
-    outgoing = stage_pages(
-        group, page_table.T, serving.reshape(1, -1), page_pool, peers, listed
-    )
-    later, outgoing = lax.optimization_barrier((packed, outgoing))
-    across |= {bit: exchange(later, group, bit) for bit in (near, far | near,)}
+
+    outgoing, packed = stage_pages(
+        group,
+        page_table.T,
+        serving.reshape(1, -1),
+        page_pool,
+        residual,
+        routes.T,
+        route_scores.T,
+        peers,
+        listed,
+        experts,
+    )
+    across = [exchange(packed, group, bit) for bit in (far, far | near, near)]
     pairs = outgoing.shape[1]
     arrived = lax.all_to_all(
         outgoing.reshape(peers, fetched, pairs, 2 * LAT), group, split_axis=0, concat_axis=0, tiled=True
     )
 
-    kept = join_rows([packed, across[far], across[near], across[far | near]])
+    kept = join_rows([packed, across[0], across[2], across[1]])
     bit = near // 2
     while bit > 1:
         kept = jnp.concatenate([kept, exchange(kept, group, bit)], axis=0)

time: 134 us -> 133 us (level)
  Pallas kernels: 23 us -> 21.5 us
    pallas_call x2 -> x1, Pallas kernels: 6.95 us -> 5.27 us  [stage_pages(): pl.pallas_call(functools.partial(stage_body, peers, group, experts), out_...]
    unnamed x24 -> x22, local copies, waits for them, and re-layouts: 3.6 us -> 3.62 us
  transfers between devices with their start and end apart: 10 -> 10, of which waited for: 5 -> 5; matrix products, arithmetic and copies ran while one was open for 6% -> 6% of each run, Pallas kernels for 16% -> 12%
where the time goes in v7:
time: 133 us
  waiting for transfers between devices  69.1 us (52%)
  starting transfers between devices  28.6 us (22%)
  Pallas kernels  21.5 us (16%)
  local copies, waits for them, and re-layouts  7.55 us (6%)
  other arithmetic  5.04 us (4%)
    ppermute x9, waiting for transfers between devices, exchange(): return lax.ppermute(block, group, [(d, d ^ bit) for d in range(peers)])  65.9 us
    ppermute x9, starting transfers between devices, exchange(): return lax.ppermute(block, group, [(d, d ^ bit) for d in range(peers)])  21.1 us
    pallas_call x1, Pallas kernels, attend(): pl.pallas_call(attend_body, out_shape=jax.ShapeDtypeStruct(out, jnp.bfloa...  7.98 us
    all_to_all x1, starting transfers between devices, local(): lax.all_to_all(outgoing.reshape(peers, fetched, pairs, 2 * LAT), group, s...  7.45 us
    pallas_call x1, Pallas kernels, expert_rows(): pl.pallas_call(functools.partial(expert_body, experts), out_shape=(jax.Sh...  6.34 us
    pallas_call x1, Pallas kernels, stage_pages(): pl.pallas_call(functools.partial(stage_body, peers, group, experts), out_...  5.27 us
    unnamed x22, local copies, waits for them, and re-layouts  3.62 us
    all_to_all x1, waiting for transfers between devices, local(): lax.all_to_all(outgoing.reshape(peers, fetched, pairs, 2 * LAT), group, s...  3.12 us
  transfers between devices with their start and end apart: 10, of which 5 were waited for; matrix products, arithmetic and copies ran while one was open for 6% of the time, Pallas kernels for 12%

profile of v7, /device:TPU:15, one launch (start us, length us, event | category | flops | bytes accessed | tf_op | source)
XLA Modules:
  0.0 132.5 jit_solution(7343632176754289420)
XLA Ops:
  0.6 5.3 %stage_pages.1 = (bf16[64,32,1152]{2,1,0:T(8,128)(2,1)}, bf16[16,3712]{1,0:T(8,128)(2,1)}) custom-call(s32[16,64]{1,0:T(8,128)} %bitcast.18, s32[1,64]{1,0:T(1,128)} %bitcast.21, bf16[32,36864]{1,0:T(8,128)(2,1)} %pool_ref.1, bf16[16,3584]{1,0:T(8,128)(2,1)} %refs_0_.1, s32[2,16]{1,0:T(2,128)} %bitcast.19, f32[2,16]{1,0:T(2,128)} %bitcast.20), custom_call_target="tpu_custom_call" | custom-call | flops 20000000000 | tf_op jit(solution)/shard_map/stage_pages/pallas_call | solution.py:143
  5.9 1.4 %collective-permute-start.2 = (bf16[16,3712]{1,0:T(8,128)(2,1)}, bf16[16,3712]{1,0:T(8,128)(2,1)S(1)}, u32[]{:S(2)}, u32[]{:S(2)}) collective-permute-start(bf16[16,3712]{1,0:T(8,128)(2,1)} %get-tuple-element.12.refs_0_), channel_id=1, source_target_pairs={{0,12},{1,13},{2,14},{3,15},{4,8},{5,9},{6,10},{7,11},{8,4},{9,5},... | collective-permute-start | bytes 356360 | tf_op jit(solution)/shard_map/ppermute | solution.py:193
  7.3 2.2 %collective-permute-start.1 = (bf16[16,3712]{1,0:T(8,128)(2,1)}, bf16[16,3712]{1,0:T(8,128)(2,1)S(1)}, u32[]{:S(2)}, u32[]{:S(2)}) collective-permute-start(bf16[16,3712]{1,0:T(8,128)(2,1)} %get-tuple-element.12.refs_0_), channel_id=1, source_target_pairs={{0,4},{1,5},{2,6},{3,7},{4,0},{5,1},{6,2},{7,3},{8,12},{9,13},{10,... | collective-permute-start | bytes 356360 | tf_op jit(solution)/shard_map/ppermute | solution.py:193
  9.5 0.0 collective-permute-start
  9.5 7.4 %all-to-all-start = ((bf16[16,4,32,1152]{3,2,1,0:T(8,128)(2,1)}), bf16[16,4,32,1152]{3,2,1,0:T(8,128)(2,1)}, u32[]{:S(2)}, u32[]{:S(2)}) async-start(bf16[16,4,32,1152]{3,2,1,0:T(8,128)(2,1)} %bitcast.14), calls=%async_computation | async-start | bytes 9437184 | tf_op jit(solution)/shard_map/all_to_all | solution.py:387
  16.9 0.0 collective-permute-done.2.refs_3_
  16.9 0.0 copy-start.6
  16.9 0.0 collective-permute-done.1.refs_2_
  16.9 0.0 collective-permute-done.refs_1_
  17.0 0.6 copy-done.6
  17.6 0.1 copy-done.7
  17.6 0.6 copy-done.8
  18.3 1.9 %join_rows.1 = bf16[64,3712]{1,0:T(8,128)(2,1)} custom-call(bf16[16,3712]{1,0:T(8,128)(2,1)} %get-tuple-element.12.refs_0_, bf16[16,3712]{1,0:T(8,128)(2,1)} %copy-done.8, bf16[16,3712]{1,0:T(8,128)(2,1)} %copy-done.7, bf16[16,3712]{1,0:T(8,128)(2,1)} %copy-done.6), custom_call_target="tpu_custom_call" | custom-call | flops 299999985664 | tf_op jit(solution)/shard_map/join_rows/pallas_call | solution.py:183
  20.1 0.3 collective-permute-start.3
  20.4 33.2 %collective-permute-done.3 = bf16[64,3712]{1,0:T(8,128)(2,1)S(1)} collective-permute-done((bf16[64,3712]{1,0:T(8,128)(2,1)}, bf16[64,3712]{1,0:T(8,128)(2,1)S(1)}, u32[]{:S(2)}, u32[]{:S(2)}) %collective-permute-start.3) | collective-permute-done | bytes 475168 | tf_op jit(solution)/shard_map/ppermute | solution.py:193
  53.6 1.1 pad_maximum_fusion.kept_ref
  54.7 0.0 copy-start
  54.7 0.9 collective-permute-start.4
  55.7 2.1 %collective-permute-done.4.other_ref = bf16[128,3712]{1,0:T(8,128)(2,1)S(1)} collective-permute-done((bf16[128,3712]{1,0:T(8,128)(2,1)S(1)}, bf16[128,3712]{1,0:T(8,128)(2,1)S(1)}, u32[]{:S(2)}, u32[]{:S(2)}) %collective-permute-start.4) | collective-permute-done | bytes 950304 | tf_op jit(solution)/shard_map/ppermute | solution.py:193
  57.8 0.9 copy-done.3
  58.8 6.3 %expert_rows.1 = (f32[128,3584]{1,0:T(8,128)}, bf16[128,3584]{1,0:T(8,128)(2,1)}) custom-call(s32[1]{0:T(128)} %bitcast.label_ref, bf16[128,3712]{1,0:T(8,128)(2,1)} %copy-done, bf16[128,3712]{1,0:T(8,128)(2,1)} %copy-done.3, bf16[3584,256]{1,0:T(8,128)(2,1)} %bitcast.15, bf16[3584,256]{1,0:T(8,128)(2,1)} %bitcast.16, bf16[256,3584]{1,0:T(8,128)(2,1)} %bitcast.17), custom_call_target="tpu_custom_call" | custom-call | tf_op jit(solution)/shard_map/expert_rows/pallas_call | solution.py:227
  65.1 0.4 collective-permute-start.5
  65.5 0.1 dynamic_slice.3
  65.6 1.6 %reshape.106 = bf16[4,4,64,576]{3,2,1,0:T(8,128)(2,1)S(1)} reshape(bf16[16,36864]{1,0:T(8,128)(2,1)S(1)} %copy-done.2) | data formatting | bytes 2359296 | tf_op jit(solution)/shard_map/reshape | solution.py:398
  67.2 1.0 copy.18
  68.3 0.2 copy.19
  68.4 0.1 pad.4.query_ref
  68.6 0.0 collective-permute-done.5
  68.6 1.3 %copy-done.1 = f32[128,3584]{1,0:T(8,128)S(1)} copy-done((f32[128,3584]{1,0:T(8,128)S(1)}, f32[128,3584]{1,0:T(8,128)}, u32[]{:S(2)}) %copy-start.1) | copy-done | bytes 1835032
  69.9 1.4 %convert_add_fusion = f32[128,3584]{1,0:T(8,128)S(1)} fusion(f32[128,3584]{1,0:T(8,128)S(1)} %copy-done.1, bf16[128,3584]{1,0:T(8,128)(2,1)} %collective-permute-done.5), kind=kLoop, calls=%fused_computation | loop fusion | flops 917504 | bytes 4587520 | tf_op jit(solution)/shard_map/add | solution.py:409
  71.4 0.8 slice.42
  72.2 0.0 collective-permute-start.6
  72.2 0.1 iota_compare_fusion.1
  72.3 0.1 select_reduce_fusion
  72.4 0.1 reshape.103
  72.5 0.2 select_reduce_fusion.1
  72.7 24.4 %collective-permute-done.6 = bf16[64,3584]{1,0:T(8,128)(2,1)} collective-permute-done((bf16[64,3584]{1,0:T(8,128)(2,1)}, bf16[64,3584]{1,0:T(8,128)(2,1)}, u32[]{:S(2)}, u32[]{:S(2)}) %collective-permute-start.6) | collective-permute-done | bytes 458784 | tf_op jit(solution)/shard_map/ppermute | solution.py:193
  97.1 1.1 convert_add_fusion.1
  98.2 7.2 %collective-permute-start.7 = (bf16[32,3584]{1,0:T(8,128)(2,1)S(1)}, bf16[32,3584]{1,0:T(8,128)(2,1)S(1)}, u32[]{:S(2)}, u32[]{:S(2)}) collective-permute-start(bf16[32,3584]{1,0:T(8,128)(2,1)S(1)} %slice.43), channel_id=1, source_target_pairs={{0,4},{1,5},{2,6},{3,7},{4,0},{5,1},{6,2},{7,3},{8,12},{9,13},{10,... | collective-permute-start | bytes 688136 | tf_op jit(solution)/shard_map/ppermute | solution.py:193
  105.4 0.2 convert_reduce_fusion
  105.6 6.2 %collective-permute-done.7 = bf16[32,3584]{1,0:T(8,128)(2,1)S(1)} collective-permute-done((bf16[32,3584]{1,0:T(8,128)(2,1)S(1)}, bf16[32,3584]{1,0:T(8,128)(2,1)S(1)}, u32[]{:S(2)}, u32[]{:S(2)}) %collective-permute-start.7) | collective-permute-done | bytes 229408 | tf_op jit(solution)/shard_map/ppermute | solution.py:193
  111.8 0.1 slice_add_fusion
  111.8 8.8 %collective-permute-start.8 = (bf16[16,3584]{1,0:T(8,128)(2,1)S(1)}, bf16[16,3584]{1,0:T(8,128)(2,1)S(1)}, u32[]{:S(2)}, u32[]{:S(2)}) collective-permute-start(bf16[16,3584]{1,0:T(8,128)(2,1)S(1)} %slice.44), channel_id=1, source_target_pairs={{0,8},{1,9},{2,10},{3,11},{4,12},{5,13},{6,14},{7,15},{8,0},{9,1},... | collective-permute-start | bytes 344072 | tf_op jit(solution)/shard_map/ppermute | solution.py:193
  120.6 0.1 pad_add_fusion.plan_ref
  120.7 3.1 %all-to-all-done = bf16[16,4,32,1152]{3,2,1,0:T(8,128)(2,1)} async-done(((bf16[16,4,32,1152]{3,2,1,0:T(8,128)(2,1)}), bf16[16,4,32,1152]{3,2,1,0:T(8,128)(2,1)}, u32[]{:S(2)}, u32[]{:S(2)}) %all-to-all-start) | async-done | bytes 4718624 | tf_op jit(solution)/shard_map/all_to_all | solution.py:387
  123.8 8.0 %attend_pages.1 = bf16[16,32768]{1,0:T(8,128)(2,1)} custom-call(s32[72]{0:T(128)S(1)} %pad_add_fusion.plan_ref, bf16[4,256,640]{2,1,0:T(8,128)(2,1)S(1)} %pad.4.query_ref, bf16[64,32,1152]{2,1,0:T(8,128)(2,1)} %bitcast.11.pages_ref), custom_call_target="tpu_custom_call" | custom-call | tf_op jit(solution)/shard_map/attend_pages/pallas_call | solution.py:326
  131.8 0.0 collective-permute-done.8
  131.8 0.7 fusion.1
  (20 shorter events, 0.1 us)
Async XLA Ops:
  5.9 11.0 %collective-permute-start.2 = (bf16[16,3712]{1,0:T(8,128)(2,1)}, bf16[16,3712]{1,0:T(8,128)(2,1)S(1)}, u32[]{:S(2)}, u32[]{:S(2)}) collective-permute-start(bf16[16,3712]{1,0:T(8,128)(2,1)} %get-tuple-element.12.refs_0_), channel_id=1, source_target_pairs={{0,12},{1,13},{2,14},{3,15},{4,8},{5,9},{6,10},{7,11},{8,4},{9,5},... | collective-permute-start | bytes 356360 | tf_op jit(solution)/shard_map/ppermute | solution.py:193
  7.3 9.7 %collective-permute-start.1 = (bf16[16,3712]{1,0:T(8,128)(2,1)}, bf16[16,3712]{1,0:T(8,128)(2,1)S(1)}, u32[]{:S(2)}, u32[]{:S(2)}) collective-permute-start(bf16[16,3712]{1,0:T(8,128)(2,1)} %get-tuple-element.12.refs_0_), channel_id=1, source_target_pairs={{0,4},{1,5},{2,6},{3,7},{4,0},{5,1},{6,2},{7,3},{8,12},{9,13},{10,... | collective-permute-start | bytes 356360 | tf_op jit(solution)/shard_map/ppermute | solution.py:193
  9.5 7.5 %collective-permute-start = (bf16[16,3712]{1,0:T(8,128)(2,1)}, bf16[16,3712]{1,0:T(8,128)(2,1)S(1)}, u32[]{:S(2)}, u32[]{:S(2)}) collective-permute-start(bf16[16,3712]{1,0:T(8,128)(2,1)} %get-tuple-element.12.refs_0_), channel_id=1, source_target_pairs={{0,8},{1,9},{2,10},{3,11},{4,12},{5,13},{6,14},{7,15},{8,0},{9,1},... | collective-permute-start | bytes 356360 | tf_op jit(solution)/shard_map/ppermute | solution.py:193
  9.5 114.4 %all-to-all-start = ((bf16[16,4,32,1152]{3,2,1,0:T(8,128)(2,1)}), bf16[16,4,32,1152]{3,2,1,0:T(8,128)(2,1)}, u32[]{:S(2)}, u32[]{:S(2)}) async-start(bf16[16,4,32,1152]{3,2,1,0:T(8,128)(2,1)} %bitcast.14), calls=%async_computation | async-start | bytes 9437184 | tf_op jit(solution)/shard_map/all_to_all | solution.py:387
  16.9 0.6 copy-start.6
  16.9 0.7 copy-start.7
  17.6 0.7 copy-start.8
  20.1 33.5 %collective-permute-start.3 = (bf16[64,3712]{1,0:T(8,128)(2,1)}, bf16[64,3712]{1,0:T(8,128)(2,1)S(1)}, u32[]{:S(2)}, u32[]{:S(2)}) collective-permute-start(bf16[64,3712]{1,0:T(8,128)(2,1)} %join_rows.1), channel_id=1, source_target_pairs={{0,2},{1,3},{2,0},{3,1},{4,6},{5,7},{6,4},{7,5},{8,10},{9,11},{10,... | collective-permute-start | bytes 1425416 | tf_op jit(solution)/shard_map/ppermute | solution.py:193
  54.7 3.1 %copy-start = (bf16[128,3712]{1,0:T(8,128)(2,1)}, bf16[128,3712]{1,0:T(8,128)(2,1)S(1)}, u32[]{:S(2)}) copy-start(bf16[128,3712]{1,0:T(8,128)(2,1)S(1)} %pad_maximum_fusion.kept_ref) | copy-start | bytes 2850820
  54.7 3.1 %collective-permute-start.4 = (bf16[128,3712]{1,0:T(8,128)(2,1)S(1)}, bf16[128,3712]{1,0:T(8,128)(2,1)S(1)}, u32[]{:S(2)}, u32[]{:S(2)}) collective-permute-start(bf16[128,3712]{1,0:T(8,128)(2,1)S(1)} %pad_maximum_fusion.kept_ref), channel_id=1, source_target_pairs={{0,1},{1,0},{2,3},{3,2},{4,5},{5,4},{6,7},{7,6},{8,9},{9,8},{10,11... | collective-permute-start | bytes 2850824 | tf_op jit(solution)/shard_map/ppermute | solution.py:193
  57.8 0.9 copy-start.3
  58.7 6.8 %copy-start.9 = (s32[64]{0:T(128)S(1)}, s32[64]{0:T(128)}, u32[]{:S(2)}) copy-start(s32[64]{0:T(128)} %param.14) | copy-start | bytes 772
  58.8 6.9 %copy-start.2 = (bf16[16,36864]{1,0:T(8,128)(2,1)S(1)}, bf16[16,36864]{1,0:T(8,128)(2,1)}, u32[]{:S(2)}) copy-start(bf16[16,36864]{1,0:T(8,128)(2,1)} %param.11) | copy-start | bytes 3538948
  65.1 3.5 %collective-permute-start.5 = (bf16[128,3584]{1,0:T(8,128)(2,1)}, bf16[128,3584]{1,0:T(8,128)(2,1)}, u32[]{:S(2)}, u32[]{:S(2)}) collective-permute-start(bf16[128,3584]{1,0:T(8,128)(2,1)} %get-tuple-element.15), channel_id=1, source_target_pairs={{0,1},{1,0},{2,3},{3,2},{4,5},{5,4},{6,7},{7,6},{8,9},{9,8},{10,11... | collective-permute-start | bytes 2752520 | tf_op jit(solution)/shard_map/ppermute | solution.py:193
  68.4 1.5 %copy-start.1 = (f32[128,3584]{1,0:T(8,128)S(1)}, f32[128,3584]{1,0:T(8,128)}, u32[]{:S(2)}) copy-start(f32[128,3584]{1,0:T(8,128)} %get-tuple-element.14) | copy-start | bytes 5505028
  69.9 2.3 %copy-start.5 = (s32[64,16]{0,1:T(8,128)S(1)}, s32[64,16]{0,1:T(8,128)}, u32[]{:S(2)}) copy-start(s32[64,16]{0,1:T(8,128)} %param.13) | copy-start | bytes 12292
  69.9 2.6 %copy-start.10 = (s32[64]{0:T(128)S(1)}, s32[64]{0:T(128)}, u32[]{:S(2)}) copy-start(s32[64]{0:T(128)} %param.15) | copy-start | bytes 772
  72.2 24.9 %collective-permute-start.6 = (bf16[64,3584]{1,0:T(8,128)(2,1)}, bf16[64,3584]{1,0:T(8,128)(2,1)}, u32[]{:S(2)}, u32[]{:S(2)}) collective-permute-start(bf16[64,3584]{1,0:T(8,128)(2,1)} %slice.42), channel_id=1, source_target_pairs={{0,2},{1,3},{2,0},{3,1},{4,6},{5,7},{6,4},{7,5},{8,10},{9,11},{10,... | collective-permute-start | bytes 1376264 | tf_op jit(solution)/shard_map/ppermute | solution.py:193
  98.2 13.5 %collective-permute-start.7 = (bf16[32,3584]{1,0:T(8,128)(2,1)S(1)}, bf16[32,3584]{1,0:T(8,128)(2,1)S(1)}, u32[]{:S(2)}, u32[]{:S(2)}) collective-permute-start(bf16[32,3584]{1,0:T(8,128)(2,1)S(1)} %slice.43), channel_id=1, source_target_pairs={{0,4},{1,5},{2,6},{3,7},{4,0},{5,1},{6,2},{7,3},{8,12},{9,13},{10,... | collective-permute-start | bytes 688136 | tf_op jit(solution)/shard_map/ppermute | solution.py:193
  111.8 20.0 %collective-permute-start.8 = (bf16[16,3584]{1,0:T(8,128)(2,1)S(1)}, bf16[16,3584]{1,0:T(8,128)(2,1)S(1)}, u32[]{:S(2)}, u32[]{:S(2)}) collective-permute-start(bf16[16,3584]{1,0:T(8,128)(2,1)S(1)} %slice.44), channel_id=1, source_target_pairs={{0,8},{1,9},{2,10},{3,11},{4,12},{5,13},{6,14},{7,15},{8,0},{9,1},... | collective-permute-start | bytes 344072 | tf_op jit(solution)/shard_map/ppermute | solution.py:193
  123.8 8.0 %copy-start.4 = (bf16[16,3584]{1,0:T(8,128)(2,1)S(1)}, bf16[16,3584]{1,0:T(8,128)(2,1)}, u32[]{:S(2)}) copy-start(bf16[16,3584]{1,0:T(8,128)(2,1)} %refs_0_.1) | copy-start | bytes 344068

commit v8 on v7

--- a/solution.py
+++ b/solution.py
@@ -54,7 +54,7 @@
 def stage_body(peers, group, experts, table_ref, serving_ref, pool_ref, *refs):
     rows_hbm, routes_hbm, scores_hbm, out_ref, packed_ref, *refs = refs
     pool, pages, order, index, table, serving, packed, routes, scores, *sems = refs
-    pool_sem, order_sem, table_sems, row_sems, page_sems = sems
+    pool_sem, order_sem, table_sems, row_sems, page_sem = sems
     width = rows_hbm.shape[1]
     fetch = pltpu.make_async_copy(pool_ref, pool, pool_sem)
     fetch_table = pltpu.make_async_copy(table_ref, table, table_sems.at[0])
@@ -115,23 +115,16 @@
     pages[...] = pool[...].reshape(pages.shape)
     listing.wait()
 
-    def copy(p, k):
-        slot = p * fetched + k
-        return pltpu.make_async_copy(pages.at[index[k, p]], out_ref.at[slot], page_sems.at[slot])
-
     def begin(p, carry):
         for k in range(fetched):
-            copy(p, k).start()
+            pltpu.make_async_copy(
+                pages.at[index[k, p]], out_ref.at[p * fetched + k], page_sem
+            ).start()
         return carry
 
-    def finish(p, carry):
-        for k in range(fetched):
-            copy(p, k).wait()
-        return carry
-
-    lax.fori_loop(0, peers, begin, 0)
+    lax.fori_loop(0, peers, begin, 0, unroll=4)
     send_rows.wait()
-    lax.fori_loop(0, peers, finish, 0)
+    pltpu.make_async_copy(out_ref, out_ref, page_sem).wait()
 
 
 def stage_pages(group, table, serving, pool, rows, routes, scores, peers, slots, experts):
@@ -162,7 +155,7 @@
             pltpu.SemaphoreType.DMA,
             pltpu.SemaphoreType.DMA((2,)),
             pltpu.SemaphoreType.DMA((4,)),
-            pltpu.SemaphoreType.DMA((slots,)),
+            pltpu.SemaphoreType.DMA,
         ],
         compiler_params=pltpu.CompilerParams(vmem_limit_bytes=56 << 20),
         cost_estimate=pl.CostEstimate(flops=STAGE_FLOPS, bytes_accessed=0, transcendentals=0),
@@ -250,37 +243,22 @@
     rows = query_ref.shape[1]
     contract = (((1,), (1,)), ((), ()))
 
-    def copy(r, i):
-        return pltpu.make_async_copy(
-            pages_ref.at[plan_ref[2 * requests + r * each + i]], context.at[r, i], sems.at[r * each + i]
-        )
-
-    blank = jnp.zeros((pairs, width), context.dtype)
     for r in range(requests):
 
         def begin(i, carry, r=r):
-            copy(r, i).start()
+            pltpu.make_async_copy(
+                pages_ref.at[plan_ref[requests + r * each + i]], context.at[r, i], sems.at[r]
+            ).start()
             return carry
 
-        lax.fori_loop(0, plan_ref[r], begin, 0)
-    for r in range(requests):
-
-        def clear(i, carry, r=r):
-            context[r, i] = blank
-            return carry
-
-        lax.fori_loop(plan_ref[r], each, clear, 0)
+        lax.fori_loop(0, each, begin, 0, unroll=4)
 
     columns = each * pairs
     draft = lax.broadcasted_iota(jnp.int32, (rows, columns), 0) % DRAFT
     early = 2 * lax.broadcasted_iota(jnp.int32, (rows, columns), 1) - draft
 
     def score(r):
-        def finish(i, carry):
-            copy(r, i).wait()
-            return carry
-
-        lax.fori_loop(0, plan_ref[r], finish, 0)
+        pltpu.make_async_copy(context.at[r], context.at[r], sems.at[r]).wait()
         block = context[r].reshape(columns, width)
         low = query_ref[r]
         high = pltpu.roll(low.astype(jnp.float32), SHIFT, 1).astype(low.dtype)
@@ -297,7 +275,7 @@
         even, odd = scored
         if r + 1 < requests:
             scored = score(r + 1)
-        limit = plan_ref[requests + r]
+        limit = plan_ref[r]
         even = jnp.where(early <= limit, even, masked_score)
         odd = jnp.where(early < limit, odd, masked_score)
         highest = jnp.max(jnp.maximum(even, odd), axis=-1, keepdims=True)
@@ -335,7 +313,7 @@
         scratch_shapes=[
             pltpu.VMEM((requests, each, pairs, width), pages.dtype),
             pltpu.VMEM(out, jnp.float32),
-            pltpu.SemaphoreType.DMA((requests * each,)),
+            pltpu.SemaphoreType.DMA((requests,)),
         ],
         compiler_params=pltpu.CompilerParams(vmem_limit_bytes=50 << 20),
         name="attend_pages",
@@ -422,8 +400,7 @@
     same = (own_list[:, None] == own_list[None, :]) & (position[None, :] < position[:, None])
     place = own_list * fetched + jnp.sum(same.astype(jnp.int32), axis=1)
     limits = jnp.sum(jnp.where(chosen, context_len[None, :], 0), axis=1) - DRAFT
-    counts = jnp.minimum((limits + DRAFT - 1) // (2 * pairs) + 1, pages_each)
-    plan = jnp.concatenate([counts, limits, place])
+    plan = jnp.concatenate([limits, place])
     latent_out = attend(plan, query, arrived.reshape(listed, pairs, 2 * LAT), pages_each)
     latent_out, last = lax.optimization_barrier((latent_out, last))
     moe_out = (residual.astype(jnp.float32) + mixed + last.astype(jnp.float32)).astype(jnp.bfloat16)

time: 133 us -> 132 us (level)
  no operation moved by 1% of the time
where the time goes in v8:
time: 132 us; the launch traced here: 131 us
  waiting for transfers between devices  69.1 us (52%)
  starting transfers between devices  28.6 us (22%)
  Pallas kernels  20.2 us (15%)
  local copies, waits for them, and re-layouts  7.55 us (6%)
  other arithmetic  5.03 us (4%)
    ppermute x9, waiting for transfers between devices, exchange(): return lax.ppermute(block, group, [(d, d ^ bit) for d in range(peers)])  66 us
    ppermute x9, starting transfers between devices, exchange(): return lax.ppermute(block, group, [(d, d ^ bit) for d in range(peers)])  21.1 us
    all_to_all x1, starting transfers between devices, local(): lax.all_to_all(outgoing.reshape(peers, fetched, pairs, 2 * LAT), group, s...  7.45 us
    pallas_call x1, Pallas kernels, attend(): pl.pallas_call(attend_body, out_shape=jax.ShapeDtypeStruct(out, jnp.bfloa...  7.26 us
    pallas_call x1, Pallas kernels, expert_rows(): pl.pallas_call(functools.partial(expert_body, experts), out_shape=(jax.Sh...  6.32 us
    pallas_call x1, Pallas kernels, stage_pages(): pl.pallas_call(functools.partial(stage_body, peers, group, experts), out_...  4.71 us
    unnamed x22, local copies, waits for them, and re-layouts  3.61 us
    all_to_all x1, waiting for transfers between devices, local(): lax.all_to_all(outgoing.reshape(peers, fetched, pairs, 2 * LAT), group, s...  3.13 us
  transfers between devices with their start and end apart: 10, of which 5 were waited for; matrix products, arithmetic and copies ran while one was open for 6% of the time, Pallas kernels for 12%

profile of v8, /device:TPU:15, one launch (start us, length us, event | category | flops | bytes accessed | tf_op | source)
XLA Modules:
  0.0 131.2 jit_solution(17912428142196283920)
XLA Ops:
  0.6 4.7 %stage_pages.1 = (bf16[64,32,1152]{2,1,0:T(8,128)(2,1)}, bf16[16,3712]{1,0:T(8,128)(2,1)}) custom-call(s32[16,64]{1,0:T(8,128)} %bitcast.18, s32[1,64]{1,0:T(1,128)} %bitcast.21, bf16[32,36864]{1,0:T(8,128)(2,1)} %pool_ref.1, bf16[16,3584]{1,0:T(8,128)(2,1)} %refs_0_.1, s32[2,16]{1,0:T(2,128)} %bitcast.19, f32[2,16]{1,0:T(2,128)} %bitcast.20), custom_call_target="tpu_custom_call" | custom-call | flops 20000000000 | tf_op jit(solution)/shard_map/stage_pages/pallas_call | solution.py:136
  5.3 1.4 %collective-permute-start.2 = (bf16[16,3712]{1,0:T(8,128)(2,1)}, bf16[16,3712]{1,0:T(8,128)(2,1)S(1)}, u32[]{:S(2)}, u32[]{:S(2)}) collective-permute-start(bf16[16,3712]{1,0:T(8,128)(2,1)} %get-tuple-element.12.refs_0_), channel_id=1, source_target_pairs={{0,12},{1,13},{2,14},{3,15},{4,8},{5,9},{6,10},{7,11},{8,4},{9,5},... | collective-permute-start | bytes 356360 | tf_op jit(solution)/shard_map/ppermute | solution.py:186
  6.7 2.2 %collective-permute-start.1 = (bf16[16,3712]{1,0:T(8,128)(2,1)}, bf16[16,3712]{1,0:T(8,128)(2,1)S(1)}, u32[]{:S(2)}, u32[]{:S(2)}) collective-permute-start(bf16[16,3712]{1,0:T(8,128)(2,1)} %get-tuple-element.12.refs_0_), channel_id=1, source_target_pairs={{0,4},{1,5},{2,6},{3,7},{4,0},{5,1},{6,2},{7,3},{8,12},{9,13},{10,... | collective-permute-start | bytes 356360 | tf_op jit(solution)/shard_map/ppermute | solution.py:186
  8.9 0.0 collective-permute-start
  8.9 7.4 %all-to-all-start = ((bf16[16,4,32,1152]{3,2,1,0:T(8,128)(2,1)}), bf16[16,4,32,1152]{3,2,1,0:T(8,128)(2,1)}, u32[]{:S(2)}, u32[]{:S(2)}) async-start(bf16[16,4,32,1152]{3,2,1,0:T(8,128)(2,1)} %bitcast.14), calls=%async_computation | async-start | bytes 9437184 | tf_op jit(solution)/shard_map/all_to_all | solution.py:365
  16.4 0.0 collective-permute-done.2.refs_3_
  16.4 0.0 copy-start.6
  16.4 0.0 collective-permute-done.1.refs_2_
  16.4 0.0 collective-permute-done.refs_1_
  16.4 0.6 copy-done.6
  17.0 0.1 copy-done.7
  17.1 0.6 copy-done.8
  17.7 1.9 %join_rows.1 = bf16[64,3712]{1,0:T(8,128)(2,1)} custom-call(bf16[16,3712]{1,0:T(8,128)(2,1)} %get-tuple-element.12.refs_0_, bf16[16,3712]{1,0:T(8,128)(2,1)} %copy-done.8, bf16[16,3712]{1,0:T(8,128)(2,1)} %copy-done.7, bf16[16,3712]{1,0:T(8,128)(2,1)} %copy-done.6), custom_call_target="tpu_custom_call" | custom-call | flops 299999985664 | tf_op jit(solution)/shard_map/join_rows/pallas_call | solution.py:176
  19.6 0.3 collective-permute-start.3
  19.9 33.2 %collective-permute-done.3 = bf16[64,3712]{1,0:T(8,128)(2,1)S(1)} collective-permute-done((bf16[64,3712]{1,0:T(8,128)(2,1)}, bf16[64,3712]{1,0:T(8,128)(2,1)S(1)}, u32[]{:S(2)}, u32[]{:S(2)}) %collective-permute-start.3) | collective-permute-done | bytes 475168 | tf_op jit(solution)/shard_map/ppermute | solution.py:186
  53.1 1.1 pad_maximum_fusion.kept_ref
  54.2 0.0 copy-start
  54.2 0.9 collective-permute-start.4
  55.1 2.1 %collective-permute-done.4.other_ref = bf16[128,3712]{1,0:T(8,128)(2,1)S(1)} collective-permute-done((bf16[128,3712]{1,0:T(8,128)(2,1)S(1)}, bf16[128,3712]{1,0:T(8,128)(2,1)S(1)}, u32[]{:S(2)}, u32[]{:S(2)}) %collective-permute-start.4) | collective-permute-done | bytes 950304 | tf_op jit(solution)/shard_map/ppermute | solution.py:186
  57.3 0.9 copy-done.3
  58.2 6.3 %expert_rows.1 = (f32[128,3584]{1,0:T(8,128)}, bf16[128,3584]{1,0:T(8,128)(2,1)}) custom-call(s32[1]{0:T(128)} %bitcast.label_ref, bf16[128,3712]{1,0:T(8,128)(2,1)} %copy-done, bf16[128,3712]{1,0:T(8,128)(2,1)} %copy-done.3, bf16[3584,256]{1,0:T(8,128)(2,1)} %bitcast.15, bf16[3584,256]{1,0:T(8,128)(2,1)} %bitcast.16, bf16[256,3584]{1,0:T(8,128)(2,1)} %bitcast.17), custom_call_target="tpu_custom_call" | custom-call | tf_op jit(solution)/shard_map/expert_rows/pallas_call | solution.py:220
  64.5 0.4 collective-permute-start.5
  65.0 0.1 dynamic_slice.3
  65.1 1.6 %reshape.106 = bf16[4,4,64,576]{3,2,1,0:T(8,128)(2,1)S(1)} reshape(bf16[16,36864]{1,0:T(8,128)(2,1)S(1)} %copy-done.2) | data formatting | bytes 2359296 | tf_op jit(solution)/shard_map/reshape | solution.py:376
  66.7 1.0 copy.18
  67.7 0.2 copy.19
  67.9 0.1 pad.4.query_ref
  68.0 0.0 collective-permute-done.5
  68.0 1.3 %copy-done.1 = f32[128,3584]{1,0:T(8,128)S(1)} copy-done((f32[128,3584]{1,0:T(8,128)S(1)}, f32[128,3584]{1,0:T(8,128)}, u32[]{:S(2)}) %copy-start.1) | copy-done | bytes 1835032
  69.4 1.4 %convert_add_fusion = f32[128,3584]{1,0:T(8,128)S(1)} fusion(f32[128,3584]{1,0:T(8,128)S(1)} %copy-done.1, bf16[128,3584]{1,0:T(8,128)(2,1)} %collective-permute-done.5), kind=kLoop, calls=%fused_computation | loop fusion | flops 917504 | bytes 4587520 | tf_op jit(solution)/shard_map/add | solution.py:387
  70.8 0.8 slice.42
  71.6 0.0 collective-permute-start.6
  71.6 0.1 iota_compare_fusion.1
  71.7 0.1 select_reduce_fusion
  71.9 0.1 reshape.103
  71.9 0.2 select_reduce_fusion.1
  72.1 24.4 %collective-permute-done.6 = bf16[64,3584]{1,0:T(8,128)(2,1)} collective-permute-done((bf16[64,3584]{1,0:T(8,128)(2,1)}, bf16[64,3584]{1,0:T(8,128)(2,1)}, u32[]{:S(2)}, u32[]{:S(2)}) %collective-permute-start.6) | collective-permute-done | bytes 458784 | tf_op jit(solution)/shard_map/ppermute | solution.py:186
  96.6 1.1 convert_add_fusion.1
  97.7 7.1 %collective-permute-start.7 = (bf16[32,3584]{1,0:T(8,128)(2,1)S(1)}, bf16[32,3584]{1,0:T(8,128)(2,1)S(1)}, u32[]{:S(2)}, u32[]{:S(2)}) collective-permute-start(bf16[32,3584]{1,0:T(8,128)(2,1)S(1)} %slice.43), channel_id=1, source_target_pairs={{0,4},{1,5},{2,6},{3,7},{4,0},{5,1},{6,2},{7,3},{8,12},{9,13},{10,... | collective-permute-start | bytes 688136 | tf_op jit(solution)/shard_map/ppermute | solution.py:186
  104.8 0.2 convert_reduce_fusion
  105.0 6.2 %collective-permute-done.7 = bf16[32,3584]{1,0:T(8,128)(2,1)S(1)} collective-permute-done((bf16[32,3584]{1,0:T(8,128)(2,1)S(1)}, bf16[32,3584]{1,0:T(8,128)(2,1)S(1)}, u32[]{:S(2)}, u32[]{:S(2)}) %collective-permute-start.7) | collective-permute-done | bytes 229408 | tf_op jit(solution)/shard_map/ppermute | solution.py:186
  111.2 0.1 slice_add_fusion
  111.3 8.8 %collective-permute-start.8 = (bf16[16,3584]{1,0:T(8,128)(2,1)S(1)}, bf16[16,3584]{1,0:T(8,128)(2,1)S(1)}, u32[]{:S(2)}, u32[]{:S(2)}) collective-permute-start(bf16[16,3584]{1,0:T(8,128)(2,1)S(1)} %slice.44), channel_id=1, source_target_pairs={{0,8},{1,9},{2,10},{3,11},{4,12},{5,13},{6,14},{7,15},{8,0},{9,1},... | collective-permute-start | bytes 344072 | tf_op jit(solution)/shard_map/ppermute | solution.py:186
  120.1 0.1 pad_add_fusion.plan_ref
  120.1 3.1 %all-to-all-done = bf16[16,4,32,1152]{3,2,1,0:T(8,128)(2,1)} async-done(((bf16[16,4,32,1152]{3,2,1,0:T(8,128)(2,1)}), bf16[16,4,32,1152]{3,2,1,0:T(8,128)(2,1)}, u32[]{:S(2)}, u32[]{:S(2)}) %all-to-all-start) | async-done | bytes 4718624 | tf_op jit(solution)/shard_map/all_to_all | solution.py:365
  123.3 7.3 %attend_pages.1 = bf16[16,32768]{1,0:T(8,128)(2,1)} custom-call(s32[68]{0:T(128)S(1)} %pad_add_fusion.plan_ref, bf16[4,256,640]{2,1,0:T(8,128)(2,1)S(1)} %pad.4.query_ref, bf16[64,32,1152]{2,1,0:T(8,128)(2,1)} %bitcast.11.pages_ref), custom_call_target="tpu_custom_call" | custom-call | tf_op jit(solution)/shard_map/attend_pages/pallas_call | solution.py:304
  130.5 0.0 collective-permute-done.8
  130.6 0.7 fusion.1
  (20 shorter events, 0.1 us)
Async XLA Ops:
  5.3 11.0 %collective-permute-start.2 = (bf16[16,3712]{1,0:T(8,128)(2,1)}, bf16[16,3712]{1,0:T(8,128)(2,1)S(1)}, u32[]{:S(2)}, u32[]{:S(2)}) collective-permute-start(bf16[16,3712]{1,0:T(8,128)(2,1)} %get-tuple-element.12.refs_0_), channel_id=1, source_target_pairs={{0,12},{1,13},{2,14},{3,15},{4,8},{5,9},{6,10},{7,11},{8,4},{9,5},... | collective-permute-start | bytes 356360 | tf_op jit(solution)/shard_map/ppermute | solution.py:186
  6.7 9.7 %collective-permute-start.1 = (bf16[16,3712]{1,0:T(8,128)(2,1)}, bf16[16,3712]{1,0:T(8,128)(2,1)S(1)}, u32[]{:S(2)}, u32[]{:S(2)}) collective-permute-start(bf16[16,3712]{1,0:T(8,128)(2,1)} %get-tuple-element.12.refs_0_), channel_id=1, source_target_pairs={{0,4},{1,5},{2,6},{3,7},{4,0},{5,1},{6,2},{7,3},{8,12},{9,13},{10,... | collective-permute-start | bytes 356360 | tf_op jit(solution)/shard_map/ppermute | solution.py:186
  8.9 7.5 %collective-permute-start = (bf16[16,3712]{1,0:T(8,128)(2,1)}, bf16[16,3712]{1,0:T(8,128)(2,1)S(1)}, u32[]{:S(2)}, u32[]{:S(2)}) collective-permute-start(bf16[16,3712]{1,0:T(8,128)(2,1)} %get-tuple-element.12.refs_0_), channel_id=1, source_target_pairs={{0,8},{1,9},{2,10},{3,11},{4,12},{5,13},{6,14},{7,15},{8,0},{9,1},... | collective-permute-start | bytes 356360 | tf_op jit(solution)/shard_map/ppermute | solution.py:186
  8.9 114.4 %all-to-all-start = ((bf16[16,4,32,1152]{3,2,1,0:T(8,128)(2,1)}), bf16[16,4,32,1152]{3,2,1,0:T(8,128)(2,1)}, u32[]{:S(2)}, u32[]{:S(2)}) async-start(bf16[16,4,32,1152]{3,2,1,0:T(8,128)(2,1)} %bitcast.14), calls=%async_computation | async-start | bytes 9437184 | tf_op jit(solution)/shard_map/all_to_all | solution.py:365
  16.4 0.6 copy-start.6
  16.4 0.7 copy-start.7
  17.1 0.7 copy-start.8
  19.6 33.5 %collective-permute-start.3 = (bf16[64,3712]{1,0:T(8,128)(2,1)}, bf16[64,3712]{1,0:T(8,128)(2,1)S(1)}, u32[]{:S(2)}, u32[]{:S(2)}) collective-permute-start(bf16[64,3712]{1,0:T(8,128)(2,1)} %join_rows.1), channel_id=1, source_target_pairs={{0,2},{1,3},{2,0},{3,1},{4,6},{5,7},{6,4},{7,5},{8,10},{9,11},{10,... | collective-permute-start | bytes 1425416 | tf_op jit(solution)/shard_map/ppermute | solution.py:186
  54.2 3.1 %copy-start = (bf16[128,3712]{1,0:T(8,128)(2,1)}, bf16[128,3712]{1,0:T(8,128)(2,1)S(1)}, u32[]{:S(2)}) copy-start(bf16[128,3712]{1,0:T(8,128)(2,1)S(1)} %pad_maximum_fusion.kept_ref) | copy-start | bytes 2850820
  54.2 3.1 %collective-permute-start.4 = (bf16[128,3712]{1,0:T(8,128)(2,1)S(1)}, bf16[128,3712]{1,0:T(8,128)(2,1)S(1)}, u32[]{:S(2)}, u32[]{:S(2)}) collective-permute-start(bf16[128,3712]{1,0:T(8,128)(2,1)S(1)} %pad_maximum_fusion.kept_ref), channel_id=1, source_target_pairs={{0,1},{1,0},{2,3},{3,2},{4,5},{5,4},{6,7},{7,6},{8,9},{9,8},{10,11... | collective-permute-start | bytes 2850824 | tf_op jit(solution)/shard_map/ppermute | solution.py:186
  57.3 0.9 copy-start.3
  58.2 6.8 %copy-start.9 = (s32[64]{0:T(128)S(1)}, s32[64]{0:T(128)}, u32[]{:S(2)}) copy-start(s32[64]{0:T(128)} %param.14) | copy-start | bytes 772
  58.2 6.9 %copy-start.2 = (bf16[16,36864]{1,0:T(8,128)(2,1)S(1)}, bf16[16,36864]{1,0:T(8,128)(2,1)}, u32[]{:S(2)}) copy-start(bf16[16,36864]{1,0:T(8,128)(2,1)} %param.11) | copy-start | bytes 3538948
  64.5 3.5 %collective-permute-start.5 = (bf16[128,3584]{1,0:T(8,128)(2,1)}, bf16[128,3584]{1,0:T(8,128)(2,1)}, u32[]{:S(2)}, u32[]{:S(2)}) collective-permute-start(bf16[128,3584]{1,0:T(8,128)(2,1)} %get-tuple-element.15), channel_id=1, source_target_pairs={{0,1},{1,0},{2,3},{3,2},{4,5},{5,4},{6,7},{7,6},{8,9},{9,8},{10,11... | collective-permute-start | bytes 2752520 | tf_op jit(solution)/shard_map/ppermute | solution.py:186
  67.9 1.5 %copy-start.1 = (f32[128,3584]{1,0:T(8,128)S(1)}, f32[128,3584]{1,0:T(8,128)}, u32[]{:S(2)}) copy-start(f32[128,3584]{1,0:T(8,128)} %get-tuple-element.14) | copy-start | bytes 5505028
  69.4 2.3 %copy-start.5 = (s32[64,16]{0,1:T(8,128)S(1)}, s32[64,16]{0,1:T(8,128)}, u32[]{:S(2)}) copy-start(s32[64,16]{0,1:T(8,128)} %param.13) | copy-start | bytes 12292
  69.4 2.6 %copy-start.10 = (s32[64]{0:T(128)S(1)}, s32[64]{0:T(128)}, u32[]{:S(2)}) copy-start(s32[64]{0:T(128)} %param.15) | copy-start | bytes 772
  71.6 24.9 %collective-permute-start.6 = (bf16[64,3584]{1,0:T(8,128)(2,1)}, bf16[64,3584]{1,0:T(8,128)(2,1)}, u32[]{:S(2)}, u32[]{:S(2)}) collective-permute-start(bf16[64,3584]{1,0:T(8,128)(2,1)} %slice.42), channel_id=1, source_target_pairs={{0,2},{1,3},{2,0},{3,1},{4,6},{5,7},{6,4},{7,5},{8,10},{9,11},{10,... | collective-permute-start | bytes 1376264 | tf_op jit(solution)/shard_map/ppermute | solution.py:186
  97.7 13.5 %collective-permute-start.7 = (bf16[32,3584]{1,0:T(8,128)(2,1)S(1)}, bf16[32,3584]{1,0:T(8,128)(2,1)S(1)}, u32[]{:S(2)}, u32[]{:S(2)}) collective-permute-start(bf16[32,3584]{1,0:T(8,128)(2,1)S(1)} %slice.43), channel_id=1, source_target_pairs={{0,4},{1,5},{2,6},{3,7},{4,0},{5,1},{6,2},{7,3},{8,12},{9,13},{10,... | collective-permute-start | bytes 688136 | tf_op jit(solution)/shard_map/ppermute | solution.py:186
  111.3 19.3 %collective-permute-start.8 = (bf16[16,3584]{1,0:T(8,128)(2,1)S(1)}, bf16[16,3584]{1,0:T(8,128)(2,1)S(1)}, u32[]{:S(2)}, u32[]{:S(2)}) collective-permute-start(bf16[16,3584]{1,0:T(8,128)(2,1)S(1)} %slice.44), channel_id=1, source_target_pairs={{0,8},{1,9},{2,10},{3,11},{4,12},{5,13},{6,14},{7,15},{8,0},{9,1},... | collective-permute-start | bytes 344072 | tf_op jit(solution)/shard_map/ppermute | solution.py:186
  123.3 7.3 %copy-start.4 = (bf16[16,3584]{1,0:T(8,128)(2,1)S(1)}, bf16[16,3584]{1,0:T(8,128)(2,1)}, u32[]{:S(2)}) copy-start(bf16[16,3584]{1,0:T(8,128)(2,1)} %refs_0_.1) | copy-start | bytes 344068

commit v9 on v8

--- a/solution.py
+++ b/solution.py
@@ -17,6 +17,7 @@
 
 exponent_scale = 192.0 ** (-0.5) * math.log2(math.e)
 masked_score = -1e30
+PIECES = 4
 JOIN_FLOPS = 300_000_000_000
 STAGE_FLOPS = 20_000_000_000
 
@@ -238,7 +239,7 @@
     )(label, kept, other, gate, up, down)
 
 
-def attend_body(plan_ref, query_ref, pages_ref, out_ref, context, held, sems):
+def attend_body(plan_ref, query_ref, pages_ref, out_ref, context, held, packed, sems, out_sem):
     requests, each, pairs, width = context.shape
     rows = query_ref.shape[1]
     contract = (((1,), (1,)), ((), ()))
@@ -294,7 +295,12 @@
             held[r * DRAFT : (r + 1) * DRAFT, h * KV : (h + 1) * KV] = latent[
                 h * DRAFT : (h + 1) * DRAFT, :
             ]
-    out_ref[...] = held[...].astype(out_ref.dtype)
+    span = held.shape[1] // PIECES
+    for piece in range(PIECES):
+        lanes = slice(piece * span, (piece + 1) * span)
+        packed[:, lanes] = held[:, lanes].astype(packed.dtype)
+        pltpu.make_async_copy(packed.at[:, lanes], out_ref.at[:, lanes], out_sem).start()
+    pltpu.make_async_copy(packed, out_ref, out_sem).wait()
 
 
 def attend(plan, query, pages, each):
@@ -309,11 +315,13 @@
             pl.BlockSpec(memory_space=pltpu.VMEM),
             pl.BlockSpec(memory_space=pltpu.HBM),
         ],
-        out_specs=pl.BlockSpec(memory_space=pltpu.VMEM),
+        out_specs=pl.BlockSpec(memory_space=pltpu.HBM),
         scratch_shapes=[
             pltpu.VMEM((requests, each, pairs, width), pages.dtype),
             pltpu.VMEM(out, jnp.float32),
+            pltpu.VMEM(out, jnp.bfloat16),
             pltpu.SemaphoreType.DMA((requests,)),
+            pltpu.SemaphoreType.DMA,
         ],
         compiler_params=pltpu.CompilerParams(vmem_limit_bytes=50 << 20),
         name="attend_pages",

time: 132 us -> 132 us (level)
  no operation moved by 1% of the time
where the time goes in v9:
time: 132 us; the launch traced here: 131 us
  waiting for transfers between devices  69.1 us (52%)
  starting transfers between devices  28.6 us (22%)
  Pallas kernels  20.1 us (15%)
  local copies, waits for them, and re-layouts  7.55 us (6%)
  other arithmetic  5.03 us (4%)
    ppermute x9, waiting for transfers between devices, exchange(): return lax.ppermute(block, group, [(d, d ^ bit) for d in range(peers)])  66 us
    ppermute x9, starting transfers between devices, exchange(): return lax.ppermute(block, group, [(d, d ^ bit) for d in range(peers)])  21.1 us
    all_to_all x1, starting transfers between devices, local(): lax.all_to_all(outgoing.reshape(peers, fetched, pairs, 2 * LAT), group, s...  7.45 us
    pallas_call x1, Pallas kernels, attend(): pl.pallas_call(attend_body, out_shape=jax.ShapeDtypeStruct(out, jnp.bfloa...  7.15 us
    pallas_call x1, Pallas kernels, expert_rows(): pl.pallas_call(functools.partial(expert_body, experts), out_shape=(jax.Sh...  6.32 us
    pallas_call x1, Pallas kernels, stage_pages(): pl.pallas_call(functools.partial(stage_body, peers, group, experts), out_...  4.71 us
    unnamed x22, local copies, waits for them, and re-layouts  3.61 us
    all_to_all x1, waiting for transfers between devices, local(): lax.all_to_all(outgoing.reshape(peers, fetched, pairs, 2 * LAT), group, s...  3.13 us
  transfers between devices with their start and end apart: 10, of which 5 were waited for; matrix products, arithmetic and copies ran while one was open for 6% of the time, Pallas kernels for 12%

profile of v9, /device:TPU:15, one launch (start us, length us, event | category | flops | bytes accessed | tf_op | source)
XLA Modules:
  0.0 131.1 jit_solution(15470122450266695193)
XLA Ops:
  0.6 4.7 %stage_pages.1 = (bf16[64,32,1152]{2,1,0:T(8,128)(2,1)}, bf16[16,3712]{1,0:T(8,128)(2,1)}) custom-call(s32[16,64]{1,0:T(8,128)} %bitcast.18, s32[1,64]{1,0:T(1,128)} %bitcast.21, bf16[32,36864]{1,0:T(8,128)(2,1)} %pool_ref.1, bf16[16,3584]{1,0:T(8,128)(2,1)} %refs_0_.1, s32[2,16]{1,0:T(2,128)} %bitcast.19, f32[2,16]{1,0:T(2,128)} %bitcast.20), custom_call_target="tpu_custom_call" | custom-call | flops 20000000000 | tf_op jit(solution)/shard_map/stage_pages/pallas_call | solution.py:137
  5.3 1.4 %collective-permute-start.2 = (bf16[16,3712]{1,0:T(8,128)(2,1)}, bf16[16,3712]{1,0:T(8,128)(2,1)S(1)}, u32[]{:S(2)}, u32[]{:S(2)}) collective-permute-start(bf16[16,3712]{1,0:T(8,128)(2,1)} %get-tuple-element.12.refs_0_), channel_id=1, source_target_pairs={{0,12},{1,13},{2,14},{3,15},{4,8},{5,9},{6,10},{7,11},{8,4},{9,5},... | collective-permute-start | bytes 356360 | tf_op jit(solution)/shard_map/ppermute | solution.py:187
  6.7 2.2 %collective-permute-start.1 = (bf16[16,3712]{1,0:T(8,128)(2,1)}, bf16[16,3712]{1,0:T(8,128)(2,1)S(1)}, u32[]{:S(2)}, u32[]{:S(2)}) collective-permute-start(bf16[16,3712]{1,0:T(8,128)(2,1)} %get-tuple-element.12.refs_0_), channel_id=1, source_target_pairs={{0,4},{1,5},{2,6},{3,7},{4,0},{5,1},{6,2},{7,3},{8,12},{9,13},{10,... | collective-permute-start | bytes 356360 | tf_op jit(solution)/shard_map/ppermute | solution.py:187
  8.9 0.0 collective-permute-start
  8.9 7.4 %all-to-all-start = ((bf16[16,4,32,1152]{3,2,1,0:T(8,128)(2,1)}), bf16[16,4,32,1152]{3,2,1,0:T(8,128)(2,1)}, u32[]{:S(2)}, u32[]{:S(2)}) async-start(bf16[16,4,32,1152]{3,2,1,0:T(8,128)(2,1)} %bitcast.14), calls=%async_computation | async-start | bytes 9437184 | tf_op jit(solution)/shard_map/all_to_all | solution.py:373
  16.4 0.0 collective-permute-done.2.refs_3_
  16.4 0.0 collective-permute-done.1.refs_2_
  16.4 0.0 collective-permute-done.refs_1_
  16.4 0.6 copy-done.6
  17.0 0.1 copy-done.7
  17.1 0.6 copy-done.8
  17.7 1.9 %join_rows.1 = bf16[64,3712]{1,0:T(8,128)(2,1)} custom-call(bf16[16,3712]{1,0:T(8,128)(2,1)} %get-tuple-element.12.refs_0_, bf16[16,3712]{1,0:T(8,128)(2,1)} %copy-done.8, bf16[16,3712]{1,0:T(8,128)(2,1)} %copy-done.7, bf16[16,3712]{1,0:T(8,128)(2,1)} %copy-done.6), custom_call_target="tpu_custom_call" | custom-call | flops 299999985664 | tf_op jit(solution)/shard_map/join_rows/pallas_call | solution.py:177
  19.6 0.3 collective-permute-start.3
  19.9 33.2 %collective-permute-done.3 = bf16[64,3712]{1,0:T(8,128)(2,1)S(1)} collective-permute-done((bf16[64,3712]{1,0:T(8,128)(2,1)}, bf16[64,3712]{1,0:T(8,128)(2,1)S(1)}, u32[]{:S(2)}, u32[]{:S(2)}) %collective-permute-start.3) | collective-permute-done | bytes 475168 | tf_op jit(solution)/shard_map/ppermute | solution.py:187
  53.1 1.1 pad_maximum_fusion.kept_ref
  54.2 0.0 copy-start
  54.2 0.9 collective-permute-start.4
  55.1 2.1 %collective-permute-done.4.other_ref = bf16[128,3712]{1,0:T(8,128)(2,1)S(1)} collective-permute-done((bf16[128,3712]{1,0:T(8,128)(2,1)S(1)}, bf16[128,3712]{1,0:T(8,128)(2,1)S(1)}, u32[]{:S(2)}, u32[]{:S(2)}) %collective-permute-start.4) | collective-permute-done | bytes 950304 | tf_op jit(solution)/shard_map/ppermute | solution.py:187
  57.3 0.9 copy-done.3
  58.2 6.3 %expert_rows.1 = (f32[128,3584]{1,0:T(8,128)}, bf16[128,3584]{1,0:T(8,128)(2,1)}) custom-call(s32[1]{0:T(128)} %bitcast.label_ref, bf16[128,3712]{1,0:T(8,128)(2,1)} %copy-done, bf16[128,3712]{1,0:T(8,128)(2,1)} %copy-done.3, bf16[3584,256]{1,0:T(8,128)(2,1)} %bitcast.15, bf16[3584,256]{1,0:T(8,128)(2,1)} %bitcast.16, bf16[256,3584]{1,0:T(8,128)(2,1)} %bitcast.17), custom_call_target="tpu_custom_call" | custom-call | tf_op jit(solution)/shard_map/expert_rows/pallas_call | solution.py:221
  64.5 0.4 collective-permute-start.5
  65.0 0.1 dynamic_slice.3
  65.1 1.6 %reshape.106 = bf16[4,4,64,576]{3,2,1,0:T(8,128)(2,1)S(1)} reshape(bf16[16,36864]{1,0:T(8,128)(2,1)S(1)} %copy-done.2) | data formatting | bytes 2359296 | tf_op jit(solution)/shard_map/reshape | solution.py:384
  66.7 1.0 copy.18
  67.7 0.2 copy.19
  67.9 0.0 copy-start.1
  67.9 0.1 pad.4.query_ref
  68.0 0.0 collective-permute-done.5
  68.0 1.3 %copy-done.1 = f32[128,3584]{1,0:T(8,128)S(1)} copy-done((f32[128,3584]{1,0:T(8,128)S(1)}, f32[128,3584]{1,0:T(8,128)}, u32[]{:S(2)}) %copy-start.1) | copy-done | bytes 1835032
  69.4 1.4 %convert_add_fusion = f32[128,3584]{1,0:T(8,128)S(1)} fusion(f32[128,3584]{1,0:T(8,128)S(1)} %copy-done.1, bf16[128,3584]{1,0:T(8,128)(2,1)} %collective-permute-done.5), kind=kLoop, calls=%fused_computation | loop fusion | flops 917504 | bytes 4587520 | tf_op jit(solution)/shard_map/add | solution.py:395
  70.8 0.8 slice.42
  71.6 0.0 collective-permute-start.6
  71.6 0.1 iota_compare_fusion.1
  71.7 0.1 select_reduce_fusion
  71.9 0.1 reshape.103
  71.9 0.2 select_reduce_fusion.1
  72.1 24.4 %collective-permute-done.6 = bf16[64,3584]{1,0:T(8,128)(2,1)} collective-permute-done((bf16[64,3584]{1,0:T(8,128)(2,1)}, bf16[64,3584]{1,0:T(8,128)(2,1)}, u32[]{:S(2)}, u32[]{:S(2)}) %collective-permute-start.6) | collective-permute-done | bytes 458784 | tf_op jit(solution)/shard_map/ppermute | solution.py:187
  96.6 1.1 convert_add_fusion.1
  97.7 7.1 %collective-permute-start.7 = (bf16[32,3584]{1,0:T(8,128)(2,1)S(1)}, bf16[32,3584]{1,0:T(8,128)(2,1)S(1)}, u32[]{:S(2)}, u32[]{:S(2)}) collective-permute-start(bf16[32,3584]{1,0:T(8,128)(2,1)S(1)} %slice.43), channel_id=1, source_target_pairs={{0,4},{1,5},{2,6},{3,7},{4,0},{5,1},{6,2},{7,3},{8,12},{9,13},{10,... | collective-permute-start | bytes 688136 | tf_op jit(solution)/shard_map/ppermute | solution.py:187
  104.8 0.2 convert_reduce_fusion
  105.0 6.2 %collective-permute-done.7 = bf16[32,3584]{1,0:T(8,128)(2,1)S(1)} collective-permute-done((bf16[32,3584]{1,0:T(8,128)(2,1)S(1)}, bf16[32,3584]{1,0:T(8,128)(2,1)S(1)}, u32[]{:S(2)}, u32[]{:S(2)}) %collective-permute-start.7) | collective-permute-done | bytes 229408 | tf_op jit(solution)/shard_map/ppermute | solution.py:187
  111.2 0.1 slice_add_fusion
  111.3 8.8 %collective-permute-start.8 = (bf16[16,3584]{1,0:T(8,128)(2,1)S(1)}, bf16[16,3584]{1,0:T(8,128)(2,1)S(1)}, u32[]{:S(2)}, u32[]{:S(2)}) collective-permute-start(bf16[16,3584]{1,0:T(8,128)(2,1)S(1)} %slice.44), channel_id=1, source_target_pairs={{0,8},{1,9},{2,10},{3,11},{4,12},{5,13},{6,14},{7,15},{8,0},{9,1},... | collective-permute-start | bytes 344072 | tf_op jit(solution)/shard_map/ppermute | solution.py:187
  120.1 0.1 pad_add_fusion.plan_ref
  120.1 3.1 %all-to-all-done = bf16[16,4,32,1152]{3,2,1,0:T(8,128)(2,1)} async-done(((bf16[16,4,32,1152]{3,2,1,0:T(8,128)(2,1)}), bf16[16,4,32,1152]{3,2,1,0:T(8,128)(2,1)}, u32[]{:S(2)}, u32[]{:S(2)}) %all-to-all-start) | async-done | bytes 4718624 | tf_op jit(solution)/shard_map/all_to_all | solution.py:373
  123.3 7.2 %attend_pages.1 = bf16[16,32768]{1,0:T(8,128)(2,1)} custom-call(s32[68]{0:T(128)S(1)} %pad_add_fusion.plan_ref, bf16[4,256,640]{2,1,0:T(8,128)(2,1)S(1)} %pad.4.query_ref, bf16[64,32,1152]{2,1,0:T(8,128)(2,1)} %bitcast.11.pages_ref), custom_call_target="tpu_custom_call" | custom-call | tf_op jit(solution)/shard_map/attend_pages/pallas_call | solution.py:310
  130.4 0.0 collective-permute-done.8
  130.4 0.7 fusion.1
  (20 shorter events, 0.1 us)
Async XLA Ops:
  5.3 11.0 %collective-permute-start.2 = (bf16[16,3712]{1,0:T(8,128)(2,1)}, bf16[16,3712]{1,0:T(8,128)(2,1)S(1)}, u32[]{:S(2)}, u32[]{:S(2)}) collective-permute-start(bf16[16,3712]{1,0:T(8,128)(2,1)} %get-tuple-element.12.refs_0_), channel_id=1, source_target_pairs={{0,12},{1,13},{2,14},{3,15},{4,8},{5,9},{6,10},{7,11},{8,4},{9,5},... | collective-permute-start | bytes 356360 | tf_op jit(solution)/shard_map/ppermute | solution.py:187
  6.7 9.7 %collective-permute-start.1 = (bf16[16,3712]{1,0:T(8,128)(2,1)}, bf16[16,3712]{1,0:T(8,128)(2,1)S(1)}, u32[]{:S(2)}, u32[]{:S(2)}) collective-permute-start(bf16[16,3712]{1,0:T(8,128)(2,1)} %get-tuple-element.12.refs_0_), channel_id=1, source_target_pairs={{0,4},{1,5},{2,6},{3,7},{4,0},{5,1},{6,2},{7,3},{8,12},{9,13},{10,... | collective-permute-start | bytes 356360 | tf_op jit(solution)/shard_map/ppermute | solution.py:187
  8.9 7.5 %collective-permute-start = (bf16[16,3712]{1,0:T(8,128)(2,1)}, bf16[16,3712]{1,0:T(8,128)(2,1)S(1)}, u32[]{:S(2)}, u32[]{:S(2)}) collective-permute-start(bf16[16,3712]{1,0:T(8,128)(2,1)} %get-tuple-element.12.refs_0_), channel_id=1, source_target_pairs={{0,8},{1,9},{2,10},{3,11},{4,12},{5,13},{6,14},{7,15},{8,0},{9,1},... | collective-permute-start | bytes 356360 | tf_op jit(solution)/shard_map/ppermute | solution.py:187
  8.9 114.4 %all-to-all-start = ((bf16[16,4,32,1152]{3,2,1,0:T(8,128)(2,1)}), bf16[16,4,32,1152]{3,2,1,0:T(8,128)(2,1)}, u32[]{:S(2)}, u32[]{:S(2)}) async-start(bf16[16,4,32,1152]{3,2,1,0:T(8,128)(2,1)} %bitcast.14), calls=%async_computation | async-start | bytes 9437184 | tf_op jit(solution)/shard_map/all_to_all | solution.py:373
  16.4 0.6 copy-start.6
  16.4 0.7 copy-start.7
  17.1 0.7 copy-start.8
  19.6 33.5 %collective-permute-start.3 = (bf16[64,3712]{1,0:T(8,128)(2,1)}, bf16[64,3712]{1,0:T(8,128)(2,1)S(1)}, u32[]{:S(2)}, u32[]{:S(2)}) collective-permute-start(bf16[64,3712]{1,0:T(8,128)(2,1)} %join_rows.1), channel_id=1, source_target_pairs={{0,2},{1,3},{2,0},{3,1},{4,6},{5,7},{6,4},{7,5},{8,10},{9,11},{10,... | collective-permute-start | bytes 1425416 | tf_op jit(solution)/shard_map/ppermute | solution.py:187
  54.2 3.1 %copy-start = (bf16[128,3712]{1,0:T(8,128)(2,1)}, bf16[128,3712]{1,0:T(8,128)(2,1)S(1)}, u32[]{:S(2)}) copy-start(bf16[128,3712]{1,0:T(8,128)(2,1)S(1)} %pad_maximum_fusion.kept_ref) | copy-start | bytes 2850820
  54.2 3.1 %collective-permute-start.4 = (bf16[128,3712]{1,0:T(8,128)(2,1)S(1)}, bf16[128,3712]{1,0:T(8,128)(2,1)S(1)}, u32[]{:S(2)}, u32[]{:S(2)}) collective-permute-start(bf16[128,3712]{1,0:T(8,128)(2,1)S(1)} %pad_maximum_fusion.kept_ref), channel_id=1, source_target_pairs={{0,1},{1,0},{2,3},{3,2},{4,5},{5,4},{6,7},{7,6},{8,9},{9,8},{10,11... | collective-permute-start | bytes 2850824 | tf_op jit(solution)/shard_map/ppermute | solution.py:187
  57.3 0.9 copy-start.3
  58.2 6.8 %copy-start.9 = (s32[64]{0:T(128)S(1)}, s32[64]{0:T(128)}, u32[]{:S(2)}) copy-start(s32[64]{0:T(128)} %param.14) | copy-start | bytes 772
  58.2 6.9 %copy-start.2 = (bf16[16,36864]{1,0:T(8,128)(2,1)S(1)}, bf16[16,36864]{1,0:T(8,128)(2,1)}, u32[]{:S(2)}) copy-start(bf16[16,36864]{1,0:T(8,128)(2,1)} %param.11) | copy-start | bytes 3538948
  64.5 3.5 %collective-permute-start.5 = (bf16[128,3584]{1,0:T(8,128)(2,1)}, bf16[128,3584]{1,0:T(8,128)(2,1)}, u32[]{:S(2)}, u32[]{:S(2)}) collective-permute-start(bf16[128,3584]{1,0:T(8,128)(2,1)} %get-tuple-element.15), channel_id=1, source_target_pairs={{0,1},{1,0},{2,3},{3,2},{4,5},{5,4},{6,7},{7,6},{8,9},{9,8},{10,11... | collective-permute-start | bytes 2752520 | tf_op jit(solution)/shard_map/ppermute | solution.py:187
  67.9 1.5 %copy-start.1 = (f32[128,3584]{1,0:T(8,128)S(1)}, f32[128,3584]{1,0:T(8,128)}, u32[]{:S(2)}) copy-start(f32[128,3584]{1,0:T(8,128)} %get-tuple-element.14) | copy-start | bytes 5505028
  69.4 2.3 %copy-start.5 = (s32[64,16]{0,1:T(8,128)S(1)}, s32[64,16]{0,1:T(8,128)}, u32[]{:S(2)}) copy-start(s32[64,16]{0,1:T(8,128)} %param.13) | copy-start | bytes 12292
  69.4 2.6 %copy-start.10 = (s32[64]{0:T(128)S(1)}, s32[64]{0:T(128)}, u32[]{:S(2)}) copy-start(s32[64]{0:T(128)} %param.15) | copy-start | bytes 772
  71.6 24.9 %collective-permute-start.6 = (bf16[64,3584]{1,0:T(8,128)(2,1)}, bf16[64,3584]{1,0:T(8,128)(2,1)}, u32[]{:S(2)}, u32[]{:S(2)}) collective-permute-start(bf16[64,3584]{1,0:T(8,128)(2,1)} %slice.42), channel_id=1, source_target_pairs={{0,2},{1,3},{2,0},{3,1},{4,6},{5,7},{6,4},{7,5},{8,10},{9,11},{10,... | collective-permute-start | bytes 1376264 | tf_op jit(solution)/shard_map/ppermute | solution.py:187
  97.7 13.5 %collective-permute-start.7 = (bf16[32,3584]{1,0:T(8,128)(2,1)S(1)}, bf16[32,3584]{1,0:T(8,128)(2,1)S(1)}, u32[]{:S(2)}, u32[]{:S(2)}) collective-permute-start(bf16[32,3584]{1,0:T(8,128)(2,1)S(1)} %slice.43), channel_id=1, source_target_pairs={{0,4},{1,5},{2,6},{3,7},{4,0},{5,1},{6,2},{7,3},{8,12},{9,13},{10,... | collective-permute-start | bytes 688136 | tf_op jit(solution)/shard_map/ppermute | solution.py:187
  111.3 19.2 %collective-permute-start.8 = (bf16[16,3584]{1,0:T(8,128)(2,1)S(1)}, bf16[16,3584]{1,0:T(8,128)(2,1)S(1)}, u32[]{:S(2)}, u32[]{:S(2)}) collective-permute-start(bf16[16,3584]{1,0:T(8,128)(2,1)S(1)} %slice.44), channel_id=1, source_target_pairs={{0,8},{1,9},{2,10},{3,11},{4,12},{5,13},{6,14},{7,15},{8,0},{9,1},... | collective-permute-start | bytes 344072 | tf_op jit(solution)/shard_map/ppermute | solution.py:187
  123.3 7.2 %copy-start.4 = (bf16[16,3584]{1,0:T(8,128)(2,1)S(1)}, bf16[16,3584]{1,0:T(8,128)(2,1)}, u32[]{:S(2)}) copy-start(bf16[16,3584]{1,0:T(8,128)(2,1)} %refs_0_.1) | copy-start | bytes 344068

commit v10 on v9

--- a/solution.py
+++ b/solution.py
@@ -68,9 +68,9 @@
     send_rows = pltpu.make_async_copy(packed, packed_ref, row_sems.at[3])
     fetch_table.start()
     fetch_serving.start()
+    fetch.start()
     for fetch_row in fetch_rows:
         fetch_row.start()
-    fetch.start()
     each, slots = table.shape
     span = slots // peers
     fetched = out_ref.shape[0] // peers
@@ -239,7 +239,7 @@
     )(label, kept, other, gate, up, down)
 
 
-def attend_body(plan_ref, query_ref, pages_ref, out_ref, context, held, packed, sems, out_sem):
+def attend_body(plan_ref, query_ref, high_ref, pages_ref, out_ref, context, held, packed, sems, out_sem):
     requests, each, pairs, width = context.shape
     rows = query_ref.shape[1]
     contract = (((1,), (1,)), ((), ()))
@@ -262,7 +262,7 @@
         pltpu.make_async_copy(context.at[r], context.at[r], sems.at[r]).wait()
         block = context[r].reshape(columns, width)
         low = query_ref[r]
-        high = pltpu.roll(low.astype(jnp.float32), SHIFT, 1).astype(low.dtype)
+        high = high_ref[r]
         even = lax.dot_general(
             low, block[:, :HALF], contract, preferred_element_type=jnp.float32
         )
@@ -303,7 +303,7 @@
     pltpu.make_async_copy(packed, out_ref, out_sem).wait()
 
 
-def attend(plan, query, pages, each):
+def attend(plan, query, high, pages, each):
     requests, rows, _ = query.shape
     _, pairs, width = pages.shape
     out = (requests * DRAFT, (rows // DRAFT) * KV)
@@ -312,6 +312,7 @@
         out_shape=jax.ShapeDtypeStruct(out, jnp.bfloat16),
         in_specs=[
             pl.BlockSpec(memory_space=pltpu.SMEM),
+            pl.BlockSpec(memory_space=pltpu.VMEM),
             pl.BlockSpec(memory_space=pltpu.VMEM),
             pl.BlockSpec(memory_space=pltpu.HBM),
         ],
@@ -325,7 +326,7 @@
         ],
         compiler_params=pltpu.CompilerParams(vmem_limit_bytes=50 << 20),
         name="attend_pages",
-    )(plan, query, pages)
+    )(plan, query, high, pages)
 
 
 def local(
@@ -383,7 +384,7 @@
     other = exchange(kept, group, 1)
     heads = queries.reshape(requests_dev, DRAFT, HEADS, LAT).transpose(0, 2, 1, 3)
     heads = heads.reshape(requests_dev, HEADS * DRAFT, LAT)
-    query = jnp.pad(heads, ((0, 0), (0, 0), (0, SHIFT)))
+    query = [jnp.pad(heads, ((0, 0), (0, 0), sides)) for sides in ((0, SHIFT), (SHIFT, 0))]
     label = (lax.axis_index("ep") // 2).reshape(1)
     mixed, leaving = expert_rows(label, kept, other, w_gate[0], w_up[0], w_down[0], experts)
     bit = 1
@@ -409,7 +410,7 @@
     place = own_list * fetched + jnp.sum(same.astype(jnp.int32), axis=1)
     limits = jnp.sum(jnp.where(chosen, context_len[None, :], 0), axis=1) - DRAFT
     plan = jnp.concatenate([limits, place])
-    latent_out = attend(plan, query, arrived.reshape(listed, pairs, 2 * LAT), pages_each)
+    latent_out = attend(plan, *query, arrived.reshape(listed, pairs, 2 * LAT), pages_each)
     latent_out, last = lax.optimization_barrier((latent_out, last))
     moe_out = (residual.astype(jnp.float32) + mixed + last.astype(jnp.float32)).astype(jnp.bfloat16)
     return (latent_out, moe_out)

time: 132 us -> 132 us (level)
    unnamed x22 -> x24, local copies, waits for them, and re-layouts: 3.61 us -> 4.18 us
  transfers between devices with their start and end apart: 10 -> 10, of which waited for: 5 -> 5; matrix products, arithmetic and copies ran while one was open for 6% -> 5% of each run, Pallas kernels for 12% -> 12%
where the time goes in v10:
time: 132 us; the launch traced here: 131 us
  waiting for transfers between devices  70.1 us (53%)
  starting transfers between devices  28.1 us (21%)
  Pallas kernels  20 us (15%)
  local copies, waits for them, and re-layouts  8.04 us (6%)
  other arithmetic  3.97 us (3%)
    ppermute x9, waiting for transfers between devices, exchange(): return lax.ppermute(block, group, [(d, d ^ bit) for d in range(peers)])  66.9 us
    ppermute x9, starting transfers between devices, exchange(): return lax.ppermute(block, group, [(d, d ^ bit) for d in range(peers)])  20.7 us
    all_to_all x1, starting transfers between devices, local(): lax.all_to_all(outgoing.reshape(peers, fetched, pairs, 2 * LAT), group, s...  7.45 us
    pallas_call x1, Pallas kernels, attend(): pl.pallas_call(attend_body, out_shape=jax.ShapeDtypeStruct(out, jnp.bfloa...  7.05 us
    pallas_call x1, Pallas kernels, expert_rows(): pl.pallas_call(functools.partial(expert_body, experts), out_shape=(jax.Sh...  6.34 us
    pallas_call x1, Pallas kernels, stage_pages(): pl.pallas_call(functools.partial(stage_body, peers, group, experts), out_...  4.78 us
    unnamed x24, local copies, waits for them, and re-layouts  4.18 us
    all_to_all x1, waiting for transfers between devices, local(): lax.all_to_all(outgoing.reshape(peers, fetched, pairs, 2 * LAT), group, s...  3.24 us
  transfers between devices with their start and end apart: 10, of which 5 were waited for; matrix products, arithmetic and copies ran while one was open for 5% of the time, Pallas kernels for 12%

profile of v10, /device:TPU:15, one launch (start us, length us, event | category | flops | bytes accessed | tf_op | source)
XLA Modules:
  0.0 131.1 jit_solution(8348785604939884814)
XLA Ops:
  0.6 4.8 %stage_pages.1 = (bf16[64,32,1152]{2,1,0:T(8,128)(2,1)}, bf16[16,3712]{1,0:T(8,128)(2,1)}) custom-call(s32[16,64]{1,0:T(8,128)} %bitcast.18, s32[1,64]{1,0:T(1,128)} %bitcast.21, bf16[32,36864]{1,0:T(8,128)(2,1)} %pool_ref.1, bf16[16,3584]{1,0:T(8,128)(2,1)} %refs_0_.1, s32[2,16]{1,0:T(2,128)} %bitcast.19, f32[2,16]{1,0:T(2,128)} %bitcast.20), custom_call_target="tpu_custom_call" | custom-call | flops 20000000000 | tf_op jit(solution)/shard_map/stage_pages/pallas_call | solution.py:137
  5.4 1.4 %collective-permute-start.2 = (bf16[16,3712]{1,0:T(8,128)(2,1)}, bf16[16,3712]{1,0:T(8,128)(2,1)S(1)}, u32[]{:S(2)}, u32[]{:S(2)}) collective-permute-start(bf16[16,3712]{1,0:T(8,128)(2,1)} %get-tuple-element.13.refs_0_), channel_id=1, source_target_pairs={{0,12},{1,13},{2,14},{3,15},{4,8},{5,9},{6,10},{7,11},{8,4},{9,5},... | collective-permute-start | bytes 356360 | tf_op jit(solution)/shard_map/ppermute | solution.py:187
  6.8 2.2 %collective-permute-start.1 = (bf16[16,3712]{1,0:T(8,128)(2,1)}, bf16[16,3712]{1,0:T(8,128)(2,1)S(1)}, u32[]{:S(2)}, u32[]{:S(2)}) collective-permute-start(bf16[16,3712]{1,0:T(8,128)(2,1)} %get-tuple-element.13.refs_0_), channel_id=1, source_target_pairs={{0,4},{1,5},{2,6},{3,7},{4,0},{5,1},{6,2},{7,3},{8,12},{9,13},{10,... | collective-permute-start | bytes 356360 | tf_op jit(solution)/shard_map/ppermute | solution.py:187
  9.0 0.0 collective-permute-start
  9.0 7.4 %all-to-all-start = ((bf16[16,4,32,1152]{3,2,1,0:T(8,128)(2,1)}), bf16[16,4,32,1152]{3,2,1,0:T(8,128)(2,1)}, u32[]{:S(2)}, u32[]{:S(2)}) async-start(bf16[16,4,32,1152]{3,2,1,0:T(8,128)(2,1)} %bitcast.14), calls=%async_computation | async-start | bytes 9437184 | tf_op jit(solution)/shard_map/all_to_all | solution.py:374
  16.4 0.0 collective-permute-done.2.refs_3_
  16.4 0.0 collective-permute-done.1.refs_2_
  16.5 0.0 collective-permute-done.refs_1_
  16.5 0.6 copy-done.7
  17.1 0.1 copy-done.8
  17.1 0.7 copy-done.9
  17.8 1.9 %join_rows.1 = bf16[64,3712]{1,0:T(8,128)(2,1)} custom-call(bf16[16,3712]{1,0:T(8,128)(2,1)} %get-tuple-element.13.refs_0_, bf16[16,3712]{1,0:T(8,128)(2,1)} %copy-done.9, bf16[16,3712]{1,0:T(8,128)(2,1)} %copy-done.8, bf16[16,3712]{1,0:T(8,128)(2,1)} %copy-done.7), custom_call_target="tpu_custom_call" | custom-call | flops 299999985664 | tf_op jit(solution)/shard_map/join_rows/pallas_call | solution.py:177
  19.7 0.3 collective-permute-start.3
  20.0 33.2 %collective-permute-done.3 = bf16[64,3712]{1,0:T(8,128)(2,1)S(1)} collective-permute-done((bf16[64,3712]{1,0:T(8,128)(2,1)}, bf16[64,3712]{1,0:T(8,128)(2,1)S(1)}, u32[]{:S(2)}, u32[]{:S(2)}) %collective-permute-start.3) | collective-permute-done | bytes 475168 | tf_op jit(solution)/shard_map/ppermute | solution.py:187
  53.1 1.1 pad_maximum_fusion.kept_ref
  54.2 0.0 copy-start.1
  54.2 0.9 collective-permute-start.4
  55.2 2.1 %collective-permute-done.4.other_ref = bf16[128,3712]{1,0:T(8,128)(2,1)S(1)} collective-permute-done((bf16[128,3712]{1,0:T(8,128)(2,1)S(1)}, bf16[128,3712]{1,0:T(8,128)(2,1)S(1)}, u32[]{:S(2)}, u32[]{:S(2)}) %collective-permute-start.4) | collective-permute-done | bytes 950304 | tf_op jit(solution)/shard_map/ppermute | solution.py:187
  57.3 0.0 copy-done.1
  57.3 0.9 copy-done.4
  58.3 6.3 %expert_rows.1 = (f32[128,3584]{1,0:T(8,128)}, bf16[128,3584]{1,0:T(8,128)(2,1)}) custom-call(s32[1]{0:T(128)} %bitcast.label_ref, bf16[128,3712]{1,0:T(8,128)(2,1)} %copy-done.1, bf16[128,3712]{1,0:T(8,128)(2,1)} %copy-done.4, bf16[3584,256]{1,0:T(8,128)(2,1)} %bitcast.15, bf16[3584,256]{1,0:T(8,128)(2,1)} %bitcast.16, bf16[256,3584]{1,0:T(8,128)(2,1)} %bitcast.17), custom_call_target="tpu_custom_call" | custom-call | tf_op jit(solution)/shard_map/expert_rows/pallas_call | solution.py:221
  64.6 0.4 collective-permute-start.5
  65.1 0.1 dynamic_slice.3
  65.1 1.6 %reshape.106 = bf16[4,4,64,576]{3,2,1,0:T(8,128)(2,1)S(1)} reshape(bf16[16,36864]{1,0:T(8,128)(2,1)S(1)} %copy-done.3) | data formatting | bytes 2359296 | tf_op jit(solution)/shard_map/reshape | solution.py:385
  66.8 1.0 copy.19
  67.8 0.2 copy.20
  68.0 0.8 fusion.3
  68.8 0.0 collective-permute-done.5
  68.8 0.7 copy-done.2
  69.5 0.2 convert_add_fusion
  69.7 1.2 copy-done
  71.0 0.1 collective-permute-start.6
  71.0 0.1 iota_compare_fusion.1
  71.1 0.1 select_reduce_fusion
  71.3 0.1 reshape.103
  71.4 0.2 select_reduce_fusion.1
  71.6 24.1 %collective-permute-done.6 = bf16[64,3584]{1,0:T(8,128)(2,1)S(1)} collective-permute-done((bf16[64,3584]{1,0:T(8,128)(2,1)S(1)}, bf16[64,3584]{1,0:T(8,128)(2,1)S(1)}, u32[]{:S(2)}, u32[]{:S(2)}) %collective-permute-start.6) | collective-permute-done | bytes 458784 | tf_op jit(solution)/shard_map/ppermute | solution.py:187
  95.7 1.3 convert_add_fusion.1
  97.0 6.9 %collective-permute-start.7 = (bf16[32,3584]{1,0:T(8,128)(2,1)S(1)}, bf16[32,3584]{1,0:T(8,128)(2,1)S(1)}, u32[]{:S(2)}, u32[]{:S(2)}) collective-permute-start(bf16[32,3584]{1,0:T(8,128)(2,1)S(1)} %slice.43), channel_id=1, source_target_pairs={{0,4},{1,5},{2,6},{3,7},{4,0},{5,1},{6,2},{7,3},{8,12},{9,13},{10,... | collective-permute-start | bytes 688136 | tf_op jit(solution)/shard_map/ppermute | solution.py:187
  103.9 0.2 convert_reduce_fusion
  104.1 7.4 %collective-permute-done.7 = bf16[32,3584]{1,0:T(8,128)(2,1)S(1)} collective-permute-done((bf16[32,3584]{1,0:T(8,128)(2,1)S(1)}, bf16[32,3584]{1,0:T(8,128)(2,1)S(1)}, u32[]{:S(2)}, u32[]{:S(2)}) %collective-permute-start.7) | collective-permute-done | bytes 229408 | tf_op jit(solution)/shard_map/ppermute | solution.py:187
  111.5 0.1 slice_add_fusion
  111.6 8.5 %collective-permute-start.8 = (bf16[16,3584]{1,0:T(8,128)(2,1)S(1)}, bf16[16,3584]{1,0:T(8,128)(2,1)S(1)}, u32[]{:S(2)}, u32[]{:S(2)}) collective-permute-start(bf16[16,3584]{1,0:T(8,128)(2,1)S(1)} %slice.44), channel_id=1, source_target_pairs={{0,8},{1,9},{2,10},{3,11},{4,12},{5,13},{6,14},{7,15},{8,0},{9,1},... | collective-permute-start | bytes 344072 | tf_op jit(solution)/shard_map/ppermute | solution.py:187
  120.0 0.1 pad_add_fusion.plan_ref
  120.1 3.2 %all-to-all-done = bf16[16,4,32,1152]{3,2,1,0:T(8,128)(2,1)} async-done(((bf16[16,4,32,1152]{3,2,1,0:T(8,128)(2,1)}), bf16[16,4,32,1152]{3,2,1,0:T(8,128)(2,1)}, u32[]{:S(2)}, u32[]{:S(2)}) %all-to-all-start) | async-done | bytes 4718624 | tf_op jit(solution)/shard_map/all_to_all | solution.py:374
  123.3 7.0 %attend_pages.1 = bf16[16,32768]{1,0:T(8,128)(2,1)} custom-call(s32[68]{0:T(128)S(1)} %pad_add_fusion.plan_ref, bf16[4,256,640]{2,1,0:T(8,128)(2,1)S(1)} %get-tuple-element.18.query_ref, bf16[4,256,640]{2,1,0:T(8,128)(2,1)S(1)} %get-tuple-element.19.high_ref, bf16[64,32,1152]{2,1,0:T(8,128)(2,1)} %bitcast.11.pages_ref), custom_call_target="tpu_custom_call" | custom-call | tf_op jit(solution)/shard_map/attend_pages/pallas_call | solution.py:310
  130.4 0.0 collective-permute-done.8
  130.4 0.7 fusion.1
  (22 shorter events, 0.1 us)
Async XLA Ops:
  5.4 11.0 %collective-permute-start.2 = (bf16[16,3712]{1,0:T(8,128)(2,1)}, bf16[16,3712]{1,0:T(8,128)(2,1)S(1)}, u32[]{:S(2)}, u32[]{:S(2)}) collective-permute-start(bf16[16,3712]{1,0:T(8,128)(2,1)} %get-tuple-element.13.refs_0_), channel_id=1, source_target_pairs={{0,12},{1,13},{2,14},{3,15},{4,8},{5,9},{6,10},{7,11},{8,4},{9,5},... | collective-permute-start | bytes 356360 | tf_op jit(solution)/shard_map/ppermute | solution.py:187
  6.8 9.7 %collective-permute-start.1 = (bf16[16,3712]{1,0:T(8,128)(2,1)}, bf16[16,3712]{1,0:T(8,128)(2,1)S(1)}, u32[]{:S(2)}, u32[]{:S(2)}) collective-permute-start(bf16[16,3712]{1,0:T(8,128)(2,1)} %get-tuple-element.13.refs_0_), channel_id=1, source_target_pairs={{0,4},{1,5},{2,6},{3,7},{4,0},{5,1},{6,2},{7,3},{8,12},{9,13},{10,... | collective-permute-start | bytes 356360 | tf_op jit(solution)/shard_map/ppermute | solution.py:187
  9.0 7.5 %collective-permute-start = (bf16[16,3712]{1,0:T(8,128)(2,1)}, bf16[16,3712]{1,0:T(8,128)(2,1)S(1)}, u32[]{:S(2)}, u32[]{:S(2)}) collective-permute-start(bf16[16,3712]{1,0:T(8,128)(2,1)} %get-tuple-element.13.refs_0_), channel_id=1, source_target_pairs={{0,8},{1,9},{2,10},{3,11},{4,12},{5,13},{6,14},{7,15},{8,0},{9,1},... | collective-permute-start | bytes 356360 | tf_op jit(solution)/shard_map/ppermute | solution.py:187
  9.0 114.4 %all-to-all-start = ((bf16[16,4,32,1152]{3,2,1,0:T(8,128)(2,1)}), bf16[16,4,32,1152]{3,2,1,0:T(8,128)(2,1)}, u32[]{:S(2)}, u32[]{:S(2)}) async-start(bf16[16,4,32,1152]{3,2,1,0:T(8,128)(2,1)} %bitcast.14), calls=%async_computation | async-start | bytes 9437184 | tf_op jit(solution)/shard_map/all_to_all | solution.py:374
  16.4 0.6 copy-start.7
  16.5 0.7 copy-start.8
  17.1 0.7 copy-start.9
  19.7 33.5 %collective-permute-start.3 = (bf16[64,3712]{1,0:T(8,128)(2,1)}, bf16[64,3712]{1,0:T(8,128)(2,1)S(1)}, u32[]{:S(2)}, u32[]{:S(2)}) collective-permute-start(bf16[64,3712]{1,0:T(8,128)(2,1)} %join_rows.1), channel_id=1, source_target_pairs={{0,2},{1,3},{2,0},{3,1},{4,6},{5,7},{6,4},{7,5},{8,10},{9,11},{10,... | collective-permute-start | bytes 1425416 | tf_op jit(solution)/shard_map/ppermute | solution.py:187
  54.2 3.1 %copy-start.1 = (bf16[128,3712]{1,0:T(8,128)(2,1)}, bf16[128,3712]{1,0:T(8,128)(2,1)S(1)}, u32[]{:S(2)}) copy-start(bf16[128,3712]{1,0:T(8,128)(2,1)S(1)} %pad_maximum_fusion.kept_ref) | copy-start | bytes 2850820
  54.2 3.1 %collective-permute-start.4 = (bf16[128,3712]{1,0:T(8,128)(2,1)S(1)}, bf16[128,3712]{1,0:T(8,128)(2,1)S(1)}, u32[]{:S(2)}, u32[]{:S(2)}) collective-permute-start(bf16[128,3712]{1,0:T(8,128)(2,1)S(1)} %pad_maximum_fusion.kept_ref), channel_id=1, source_target_pairs={{0,1},{1,0},{2,3},{3,2},{4,5},{5,4},{6,7},{7,6},{8,9},{9,8},{10,11... | collective-permute-start | bytes 2850824 | tf_op jit(solution)/shard_map/ppermute | solution.py:187
  57.3 0.9 copy-start.4
  58.3 6.8 %copy-start.10 = (s32[64]{0:T(128)S(1)}, s32[64]{0:T(128)}, u32[]{:S(2)}) copy-start(s32[64]{0:T(128)} %param.14) | copy-start | bytes 772
  58.3 6.9 %copy-start.3 = (bf16[16,36864]{1,0:T(8,128)(2,1)S(1)}, bf16[16,36864]{1,0:T(8,128)(2,1)}, u32[]{:S(2)}) copy-start(bf16[16,36864]{1,0:T(8,128)(2,1)} %param.11) | copy-start | bytes 3538948
  64.6 4.2 %collective-permute-start.5 = (bf16[128,3584]{1,0:T(8,128)(2,1)}, bf16[128,3584]{1,0:T(8,128)(2,1)S(1)}, u32[]{:S(2)}, u32[]{:S(2)}) collective-permute-start(bf16[128,3584]{1,0:T(8,128)(2,1)} %get-tuple-element.16), channel_id=1, source_target_pairs={{0,1},{1,0},{2,3},{3,2},{4,5},{5,4},{6,7},{7,6},{8,9},{9,8},{10,11... | collective-permute-start | bytes 2752520 | tf_op jit(solution)/shard_map/ppermute | solution.py:187
  68.0 1.5 %copy-start.2 = (f32[128,3584]{1,0:T(8,128)S(1)}, f32[128,3584]{1,0:T(8,128)}, u32[]{:S(2)}) copy-start(f32[128,3584]{1,0:T(8,128)} %get-tuple-element.15) | copy-start | bytes 5505028
  69.5 1.7 %copy-start.6 = (s32[64,16]{0,1:T(8,128)S(1)}, s32[64,16]{0,1:T(8,128)}, u32[]{:S(2)}) copy-start(s32[64,16]{0,1:T(8,128)} %param.13) | copy-start | bytes 12292
  69.5 1.9 %copy-start.11 = (s32[64]{0:T(128)S(1)}, s32[64]{0:T(128)}, u32[]{:S(2)}) copy-start(s32[64]{0:T(128)} %param.15) | copy-start | bytes 772
  69.7 1.2 copy-start
  71.0 24.7 %collective-permute-start.6 = (bf16[64,3584]{1,0:T(8,128)(2,1)S(1)}, bf16[64,3584]{1,0:T(8,128)(2,1)S(1)}, u32[]{:S(2)}, u32[]{:S(2)}) collective-permute-start(bf16[64,3584]{1,0:T(8,128)(2,1)S(1)} %slice.42), channel_id=1, source_target_pairs={{0,2},{1,3},{2,0},{3,1},{4,6},{5,7},{6,4},{7,5},{8,10},{9,11},{10,... | collective-permute-start | bytes 1376264 | tf_op jit(solution)/shard_map/ppermute | solution.py:187
  97.0 14.5 %collective-permute-start.7 = (bf16[32,3584]{1,0:T(8,128)(2,1)S(1)}, bf16[32,3584]{1,0:T(8,128)(2,1)S(1)}, u32[]{:S(2)}, u32[]{:S(2)}) collective-permute-start(bf16[32,3584]{1,0:T(8,128)(2,1)S(1)} %slice.43), channel_id=1, source_target_pairs={{0,4},{1,5},{2,6},{3,7},{4,0},{5,1},{6,2},{7,3},{8,12},{9,13},{10,... | collective-permute-start | bytes 688136 | tf_op jit(solution)/shard_map/ppermute | solution.py:187
  111.6 18.8 %collective-permute-start.8 = (bf16[16,3584]{1,0:T(8,128)(2,1)S(1)}, bf16[16,3584]{1,0:T(8,128)(2,1)S(1)}, u32[]{:S(2)}, u32[]{:S(2)}) collective-permute-start(bf16[16,3584]{1,0:T(8,128)(2,1)S(1)} %slice.44), channel_id=1, source_target_pairs={{0,8},{1,9},{2,10},{3,11},{4,12},{5,13},{6,14},{7,15},{8,0},{9,1},... | collective-permute-start | bytes 344072 | tf_op jit(solution)/shard_map/ppermute | solution.py:187
  123.3 7.1 %copy-start.5 = (bf16[16,3584]{1,0:T(8,128)(2,1)S(1)}, bf16[16,3584]{1,0:T(8,128)(2,1)}, u32[]{:S(2)}) copy-start(bf16[16,3584]{1,0:T(8,128)(2,1)} %refs_0_.1) | copy-start | bytes 344068

commit v11 on v10

--- a/solution.py
+++ b/solution.py
@@ -410,9 +410,10 @@
     place = own_list * fetched + jnp.sum(same.astype(jnp.int32), axis=1)
     limits = jnp.sum(jnp.where(chosen, context_len[None, :], 0), axis=1) - DRAFT
     plan = jnp.concatenate([limits, place])
+    mixed = residual.astype(jnp.float32) + mixed
     latent_out = attend(plan, *query, arrived.reshape(listed, pairs, 2 * LAT), pages_each)
-    latent_out, last = lax.optimization_barrier((latent_out, last))
-    moe_out = (residual.astype(jnp.float32) + mixed + last.astype(jnp.float32)).astype(jnp.bfloat16)
+    latent_out, last, mixed = lax.optimization_barrier((latent_out, last, mixed))
+    moe_out = (mixed + last.astype(jnp.float32)).astype(jnp.bfloat16)
     return (latent_out, moe_out)
 
 

time: 132 us -> 132 us (level)
  waiting for transfers between devices: 70.1 us -> 75.8 us
  starting transfers between devices: 28.1 us -> 24.3 us
    ppermute x9, waiting for transfers between devices: 66.9 us -> 71.6 us  [exchange(): return lax.ppermute(block, group, [(d, d ^ bit) for d in range(peers)])]
    ppermute x9, starting transfers between devices: 20.7 us -> 16.9 us  [exchange(): return lax.ppermute(block, group, [(d, d ^ bit) for d in range(peers)])]
    unnamed x24 -> x22, local copies, waits for them, and re-layouts: 4.18 us -> 3.22 us
where the time goes in v11:
time: 132 us; the launch traced here: 131 us
  waiting for transfers between devices  75.8 us (57%)
  starting transfers between devices  24.3 us (18%)
  Pallas kernels  20 us (15%)
  local copies, waits for them, and re-layouts  7.09 us (5%)
  other arithmetic  2.83 us (2%)
    ppermute x9, waiting for transfers between devices, exchange(): return lax.ppermute(block, group, [(d, d ^ bit) for d in range(peers)])  71.6 us
    ppermute x9, starting transfers between devices, exchange(): return lax.ppermute(block, group, [(d, d ^ bit) for d in range(peers)])  16.9 us
    all_to_all x1, starting transfers between devices, local(): lax.all_to_all(outgoing.reshape(peers, fetched, pairs, 2 * LAT), group, s...  7.45 us
    pallas_call x1, Pallas kernels, attend(): pl.pallas_call(attend_body, out_shape=jax.ShapeDtypeStruct(out, jnp.bfloa...  7.05 us
    pallas_call x1, Pallas kernels, expert_rows(): pl.pallas_call(functools.partial(expert_body, experts), out_shape=(jax.Sh...  6.34 us
    pallas_call x1, Pallas kernels, stage_pages(): pl.pallas_call(functools.partial(stage_body, peers, group, experts), out_...  4.78 us
    all_to_all x1, waiting for transfers between devices, local(): lax.all_to_all(outgoing.reshape(peers, fetched, pairs, 2 * LAT), group, s...  4.22 us
    unnamed x22, local copies, waits for them, and re-layouts  3.22 us
  transfers between devices with their start and end apart: 10, of which 5 were waited for; matrix products, arithmetic and copies ran while one was open for 5% of the time, Pallas kernels for 12%

profile of v11, /device:TPU:15, one launch (start us, length us, event | category | flops | bytes accessed | tf_op | source)
XLA Modules:
  0.0 130.9 jit_solution(10462802908767344342)
XLA Ops:
  0.6 4.8 %stage_pages.1 = (bf16[64,32,1152]{2,1,0:T(8,128)(2,1)}, bf16[16,3712]{1,0:T(8,128)(2,1)}) custom-call(s32[16,64]{1,0:T(8,128)} %bitcast.18, s32[1,64]{1,0:T(1,128)} %bitcast.21, bf16[32,36864]{1,0:T(8,128)(2,1)} %pool_ref.1, bf16[16,3584]{1,0:T(8,128)(2,1)} %refs_0_.1, s32[2,16]{1,0:T(2,128)} %bitcast.19, f32[2,16]{1,0:T(2,128)} %bitcast.20), custom_call_target="tpu_custom_call" | custom-call | flops 20000000000 | tf_op jit(solution)/shard_map/stage_pages/pallas_call | solution.py:137
  5.4 1.4 %collective-permute-start.2 = (bf16[16,3712]{1,0:T(8,128)(2,1)}, bf16[16,3712]{1,0:T(8,128)(2,1)S(1)}, u32[]{:S(2)}, u32[]{:S(2)}) collective-permute-start(bf16[16,3712]{1,0:T(8,128)(2,1)} %get-tuple-element.14.refs_0_), channel_id=1, source_target_pairs={{0,12},{1,13},{2,14},{3,15},{4,8},{5,9},{6,10},{7,11},{8,4},{9,5},... | collective-permute-start | bytes 356360 | tf_op jit(solution)/shard_map/ppermute | solution.py:187
  6.8 2.2 %collective-permute-start.1 = (bf16[16,3712]{1,0:T(8,128)(2,1)}, bf16[16,3712]{1,0:T(8,128)(2,1)S(1)}, u32[]{:S(2)}, u32[]{:S(2)}) collective-permute-start(bf16[16,3712]{1,0:T(8,128)(2,1)} %get-tuple-element.14.refs_0_), channel_id=1, source_target_pairs={{0,4},{1,5},{2,6},{3,7},{4,0},{5,1},{6,2},{7,3},{8,12},{9,13},{10,... | collective-permute-start | bytes 356360 | tf_op jit(solution)/shard_map/ppermute | solution.py:187
  9.0 0.0 collective-permute-start
  9.0 7.4 %all-to-all-start = ((bf16[16,4,32,1152]{3,2,1,0:T(8,128)(2,1)}), bf16[16,4,32,1152]{3,2,1,0:T(8,128)(2,1)}, u32[]{:S(2)}, u32[]{:S(2)}) async-start(bf16[16,4,32,1152]{3,2,1,0:T(8,128)(2,1)} %bitcast.14), calls=%async_computation | async-start | bytes 9437184 | tf_op jit(solution)/shard_map/all_to_all | solution.py:374
  16.4 0.0 collective-permute-done.2.refs_3_
  16.4 0.0 collective-permute-done.1.refs_2_
  16.5 0.0 collective-permute-done.refs_1_
  16.5 0.6 copy-done.6
  17.1 0.1 copy-done.7
  17.1 0.6 copy-done.8
  17.8 1.9 %join_rows.1 = bf16[64,3712]{1,0:T(8,128)(2,1)} custom-call(bf16[16,3712]{1,0:T(8,128)(2,1)} %get-tuple-element.14.refs_0_, bf16[16,3712]{1,0:T(8,128)(2,1)} %copy-done.8, bf16[16,3712]{1,0:T(8,128)(2,1)} %copy-done.7, bf16[16,3712]{1,0:T(8,128)(2,1)} %copy-done.6), custom_call_target="tpu_custom_call" | custom-call | flops 299999985664 | tf_op jit(solution)/shard_map/join_rows/pallas_call | solution.py:177
  19.7 0.3 collective-permute-start.3
  19.9 33.2 %collective-permute-done.3 = bf16[64,3712]{1,0:T(8,128)(2,1)S(1)} collective-permute-done((bf16[64,3712]{1,0:T(8,128)(2,1)}, bf16[64,3712]{1,0:T(8,128)(2,1)S(1)}, u32[]{:S(2)}, u32[]{:S(2)}) %collective-permute-start.3) | collective-permute-done | bytes 475168 | tf_op jit(solution)/shard_map/ppermute | solution.py:187
  53.1 1.1 pad_maximum_fusion.kept_ref
  54.2 0.0 copy-start
  54.3 0.9 collective-permute-start.4
  55.2 2.1 %collective-permute-done.4.other_ref = bf16[128,3712]{1,0:T(8,128)(2,1)S(1)} collective-permute-done((bf16[128,3712]{1,0:T(8,128)(2,1)S(1)}, bf16[128,3712]{1,0:T(8,128)(2,1)S(1)}, u32[]{:S(2)}, u32[]{:S(2)}) %collective-permute-start.4) | collective-permute-done | bytes 950304 | tf_op jit(solution)/shard_map/ppermute | solution.py:187
  57.3 0.9 copy-done.3
  58.3 6.3 %expert_rows.1 = (f32[128,3584]{1,0:T(8,128)}, bf16[128,3584]{1,0:T(8,128)(2,1)}) custom-call(s32[1]{0:T(128)} %bitcast.label_ref, bf16[128,3712]{1,0:T(8,128)(2,1)} %copy-done, bf16[128,3712]{1,0:T(8,128)(2,1)} %copy-done.3, bf16[3584,256]{1,0:T(8,128)(2,1)} %bitcast.15, bf16[3584,256]{1,0:T(8,128)(2,1)} %bitcast.16, bf16[256,3584]{1,0:T(8,128)(2,1)} %bitcast.17), custom_call_target="tpu_custom_call" | custom-call | tf_op jit(solution)/shard_map/expert_rows/pallas_call | solution.py:221
  64.6 0.4 collective-permute-start.5
  65.1 0.1 dynamic_slice.3
  65.1 0.1 iota_compare_fusion.1
  65.2 0.1 select_reduce_fusion
  65.4 0.1 reshape.103
  65.4 1.6 %reshape.106 = bf16[4,4,64,576]{3,2,1,0:T(8,128)(2,1)S(1)} reshape(bf16[16,36864]{1,0:T(8,128)(2,1)S(1)} %copy-done.2) | data formatting | bytes 2359296 | tf_op jit(solution)/shard_map/reshape | solution.py:385
  67.1 1.0 copy.19
  68.1 0.2 copy.20
  68.3 0.8 fusion.1
  69.1 0.0 collective-permute-done.5
  69.1 0.7 copy-done.1
  69.8 0.2 convert_add_fusion
  70.0 0.1 collective-permute-start.6
  70.1 0.3 copy-done.10
  70.4 0.2 select_reduce_fusion.1
  70.6 0.2 convert_reduce_fusion
  70.8 0.0 copy-start.4
  70.8 17.8 %collective-permute-done.6 = bf16[64,3584]{1,0:T(8,128)(2,1)S(1)} collective-permute-done((bf16[64,3584]{1,0:T(8,128)(2,1)S(1)}, bf16[64,3584]{1,0:T(8,128)(2,1)S(1)}, u32[]{:S(2)}, u32[]{:S(2)}) %collective-permute-start.6) | collective-permute-done | bytes 458784 | tf_op jit(solution)/shard_map/ppermute | solution.py:187
  88.6 0.1 convert_add_fusion.1
  88.8 4.2 %collective-permute-start.7 = (bf16[32,3584]{1,0:T(8,128)(2,1)S(1)}, bf16[32,3584]{1,0:T(8,128)(2,1)S(1)}, u32[]{:S(2)}, u32[]{:S(2)}) collective-permute-start(bf16[32,3584]{1,0:T(8,128)(2,1)S(1)} %slice.39), channel_id=1, source_target_pairs={{0,4},{1,5},{2,6},{3,7},{4,0},{5,1},{6,2},{7,3},{8,12},{9,13},{10,... | collective-permute-start | bytes 688136 | tf_op jit(solution)/shard_map/ppermute | solution.py:187
  93.0 0.1 pad_add_fusion.plan_ref
  93.1 18.4 %collective-permute-done.7 = bf16[32,3584]{1,0:T(8,128)(2,1)S(1)} collective-permute-done((bf16[32,3584]{1,0:T(8,128)(2,1)S(1)}, bf16[32,3584]{1,0:T(8,128)(2,1)S(1)}, u32[]{:S(2)}, u32[]{:S(2)}) %collective-permute-start.7) | collective-permute-done | bytes 229408 | tf_op jit(solution)/shard_map/ppermute | solution.py:187
  111.5 0.1 slice_add_fusion
  111.6 7.4 %collective-permute-start.8 = (bf16[16,3584]{1,0:T(8,128)(2,1)S(1)}, bf16[16,3584]{1,0:T(8,128)(2,1)S(1)}, u32[]{:S(2)}, u32[]{:S(2)}) collective-permute-start(bf16[16,3584]{1,0:T(8,128)(2,1)S(1)} %slice.40), channel_id=1, source_target_pairs={{0,8},{1,9},{2,10},{3,11},{4,12},{5,13},{6,14},{7,15},{8,0},{9,1},... | collective-permute-start | bytes 344072 | tf_op jit(solution)/shard_map/ppermute | solution.py:187
  119.0 4.2 %all-to-all-done = bf16[16,4,32,1152]{3,2,1,0:T(8,128)(2,1)} async-done(((bf16[16,4,32,1152]{3,2,1,0:T(8,128)(2,1)}), bf16[16,4,32,1152]{3,2,1,0:T(8,128)(2,1)}, u32[]{:S(2)}, u32[]{:S(2)}) %all-to-all-start) | async-done | bytes 4718624 | tf_op jit(solution)/shard_map/all_to_all | solution.py:374
  123.2 7.0 %attend_pages.1 = bf16[16,32768]{1,0:T(8,128)(2,1)} custom-call(s32[68]{0:T(128)S(1)} %pad_add_fusion.plan_ref, bf16[4,256,640]{2,1,0:T(8,128)(2,1)S(1)} %get-tuple-element.19.query_ref, bf16[4,256,640]{2,1,0:T(8,128)(2,1)S(1)} %get-tuple-element.20.high_ref, bf16[64,32,1152]{2,1,0:T(8,128)(2,1)} %bitcast.11.pages_ref), custom_call_target="tpu_custom_call" | custom-call | tf_op jit(solution)/shard_map/attend_pages/pallas_call | solution.py:310
  130.3 0.0 collective-permute-done.8
  130.3 0.7 add_convert_fusion
  (21 shorter events, 0.2 us)
Async XLA Ops:
  5.4 11.0 %collective-permute-start.2 = (bf16[16,3712]{1,0:T(8,128)(2,1)}, bf16[16,3712]{1,0:T(8,128)(2,1)S(1)}, u32[]{:S(2)}, u32[]{:S(2)}) collective-permute-start(bf16[16,3712]{1,0:T(8,128)(2,1)} %get-tuple-element.14.refs_0_), channel_id=1, source_target_pairs={{0,12},{1,13},{2,14},{3,15},{4,8},{5,9},{6,10},{7,11},{8,4},{9,5},... | collective-permute-start | bytes 356360 | tf_op jit(solution)/shard_map/ppermute | solution.py:187
  6.8 9.7 %collective-permute-start.1 = (bf16[16,3712]{1,0:T(8,128)(2,1)}, bf16[16,3712]{1,0:T(8,128)(2,1)S(1)}, u32[]{:S(2)}, u32[]{:S(2)}) collective-permute-start(bf16[16,3712]{1,0:T(8,128)(2,1)} %get-tuple-element.14.refs_0_), channel_id=1, source_target_pairs={{0,4},{1,5},{2,6},{3,7},{4,0},{5,1},{6,2},{7,3},{8,12},{9,13},{10,... | collective-permute-start | bytes 356360 | tf_op jit(solution)/shard_map/ppermute | solution.py:187
  9.0 7.5 %collective-permute-start = (bf16[16,3712]{1,0:T(8,128)(2,1)}, bf16[16,3712]{1,0:T(8,128)(2,1)S(1)}, u32[]{:S(2)}, u32[]{:S(2)}) collective-permute-start(bf16[16,3712]{1,0:T(8,128)(2,1)} %get-tuple-element.14.refs_0_), channel_id=1, source_target_pairs={{0,8},{1,9},{2,10},{3,11},{4,12},{5,13},{6,14},{7,15},{8,0},{9,1},... | collective-permute-start | bytes 356360 | tf_op jit(solution)/shard_map/ppermute | solution.py:187
  9.0 114.2 %all-to-all-start = ((bf16[16,4,32,1152]{3,2,1,0:T(8,128)(2,1)}), bf16[16,4,32,1152]{3,2,1,0:T(8,128)(2,1)}, u32[]{:S(2)}, u32[]{:S(2)}) async-start(bf16[16,4,32,1152]{3,2,1,0:T(8,128)(2,1)} %bitcast.14), calls=%async_computation | async-start | bytes 9437184 | tf_op jit(solution)/shard_map/all_to_all | solution.py:374
  16.4 0.6 copy-start.6
  16.5 0.7 copy-start.7
  17.1 0.7 copy-start.8
  19.7 33.5 %collective-permute-start.3 = (bf16[64,3712]{1,0:T(8,128)(2,1)}, bf16[64,3712]{1,0:T(8,128)(2,1)S(1)}, u32[]{:S(2)}, u32[]{:S(2)}) collective-permute-start(bf16[64,3712]{1,0:T(8,128)(2,1)} %join_rows.1), channel_id=1, source_target_pairs={{0,2},{1,3},{2,0},{3,1},{4,6},{5,7},{6,4},{7,5},{8,10},{9,11},{10,... | collective-permute-start | bytes 1425416 | tf_op jit(solution)/shard_map/ppermute | solution.py:187
  54.2 3.1 %copy-start = (bf16[128,3712]{1,0:T(8,128)(2,1)}, bf16[128,3712]{1,0:T(8,128)(2,1)S(1)}, u32[]{:S(2)}) copy-start(bf16[128,3712]{1,0:T(8,128)(2,1)S(1)} %pad_maximum_fusion.kept_ref) | copy-start | bytes 2850820
  54.3 3.1 %collective-permute-start.4 = (bf16[128,3712]{1,0:T(8,128)(2,1)S(1)}, bf16[128,3712]{1,0:T(8,128)(2,1)S(1)}, u32[]{:S(2)}, u32[]{:S(2)}) collective-permute-start(bf16[128,3712]{1,0:T(8,128)(2,1)S(1)} %pad_maximum_fusion.kept_ref), channel_id=1, source_target_pairs={{0,1},{1,0},{2,3},{3,2},{4,5},{5,4},{6,7},{7,6},{8,9},{9,8},{10,11... | collective-permute-start | bytes 2850824 | tf_op jit(solution)/shard_map/ppermute | solution.py:187
  57.3 0.9 copy-start.3
  58.3 6.8 %copy-start.9 = (s32[64]{0:T(128)S(1)}, s32[64]{0:T(128)}, u32[]{:S(2)}) copy-start(s32[64]{0:T(128)} %param.14) | copy-start | bytes 772
  58.3 6.9 %copy-start.5 = (s32[64,16]{0,1:T(8,128)S(1)}, s32[64,16]{0,1:T(8,128)}, u32[]{:S(2)}) copy-start(s32[64,16]{0,1:T(8,128)} %param.13) | copy-start | bytes 12292
  58.3 7.2 %copy-start.2 = (bf16[16,36864]{1,0:T(8,128)(2,1)S(1)}, bf16[16,36864]{1,0:T(8,128)(2,1)}, u32[]{:S(2)}) copy-start(bf16[16,36864]{1,0:T(8,128)(2,1)} %param.11) | copy-start | bytes 3538948
  64.6 4.5 %collective-permute-start.5 = (bf16[128,3584]{1,0:T(8,128)(2,1)}, bf16[128,3584]{1,0:T(8,128)(2,1)S(1)}, u32[]{:S(2)}, u32[]{:S(2)}) collective-permute-start(bf16[128,3584]{1,0:T(8,128)(2,1)} %get-tuple-element.17), channel_id=1, source_target_pairs={{0,1},{1,0},{2,3},{3,2},{4,5},{5,4},{6,7},{7,6},{8,9},{9,8},{10,11... | collective-permute-start | bytes 2752520 | tf_op jit(solution)/shard_map/ppermute | solution.py:187
  68.3 1.5 %copy-start.1 = (f32[128,3584]{1,0:T(8,128)S(1)}, f32[128,3584]{1,0:T(8,128)}, u32[]{:S(2)}) copy-start(f32[128,3584]{1,0:T(8,128)} %get-tuple-element.16) | copy-start | bytes 5505028
  69.8 0.7 copy-start.10
  70.0 18.6 %collective-permute-start.6 = (bf16[64,3584]{1,0:T(8,128)(2,1)S(1)}, bf16[64,3584]{1,0:T(8,128)(2,1)S(1)}, u32[]{:S(2)}, u32[]{:S(2)}) collective-permute-start(bf16[64,3584]{1,0:T(8,128)(2,1)S(1)} %slice.38), channel_id=1, source_target_pairs={{0,2},{1,3},{2,0},{3,1},{4,6},{5,7},{6,4},{7,5},{8,10},{9,11},{10,... | collective-permute-start | bytes 1376264 | tf_op jit(solution)/shard_map/ppermute | solution.py:187
  70.8 48.1 %copy-start.4 = (bf16[16,3584]{1,0:T(8,128)(2,1)S(1)}, bf16[16,3584]{1,0:T(8,128)(2,1)}, u32[]{:S(2)}) copy-start(bf16[16,3584]{1,0:T(8,128)(2,1)} %refs_0_.1) | copy-start | bytes 344068
  88.8 22.7 %collective-permute-start.7 = (bf16[32,3584]{1,0:T(8,128)(2,1)S(1)}, bf16[32,3584]{1,0:T(8,128)(2,1)S(1)}, u32[]{:S(2)}, u32[]{:S(2)}) collective-permute-start(bf16[32,3584]{1,0:T(8,128)(2,1)S(1)} %slice.39), channel_id=1, source_target_pairs={{0,4},{1,5},{2,6},{3,7},{4,0},{5,1},{6,2},{7,3},{8,12},{9,13},{10,... | collective-permute-start | bytes 688136 | tf_op jit(solution)/shard_map/ppermute | solution.py:187
  111.6 18.7 %collective-permute-start.8 = (bf16[16,3584]{1,0:T(8,128)(2,1)S(1)}, bf16[16,3584]{1,0:T(8,128)(2,1)S(1)}, u32[]{:S(2)}, u32[]{:S(2)}) collective-permute-start(bf16[16,3584]{1,0:T(8,128)(2,1)S(1)} %slice.40), channel_id=1, source_target_pairs={{0,8},{1,9},{2,10},{3,11},{4,12},{5,13},{6,14},{7,15},{8,0},{9,1},... | collective-permute-start | bytes 344072 | tf_op jit(solution)/shard_map/ppermute | solution.py:187
